TPU v7x, 128 devices: a whole 4x4x4 slice. The times are simulated.
128 devices in a mesh: gx: 32 (over y_lo, x, z), gy: 4 (over y_hi, core).
Axes of the slice: x: 4, y: 4 (y_hi: 2, y_lo: 2; y = y_hi * 2 + y_lo), z: 4, core: 2. Of those that a mesh axis runs over, the one named last changes fastest.
Arguments:
- state: float32 [32, 4, 96, 8, 128], P('gx', 'gy'), may hold values from -4 to 4, as said below
- leaving: int32 [32, 4, 24], P('gx', 'gy'), may hold values from 0 to 95, as said below
- pairs: int32 [32, 4, 2, 576], P('gx', 'gy'), may hold values from 0 to 863, as said below
- counts: int32 [32, 4, 2], P('gx', 'gy'), may hold values from 0 to 576, as said below
- wall_flags: int32 [32, 4, 96, 128], P('gx', 'gy'), may hold values 0 or 1
- cell_index: int32 [32, 4, 96, 128], P('gx', 'gy'), may hold values from 0 to 255
- fluid_temp: float32 [32, 4, 256], P('gx', 'gy'), may hold values from -5 to 5
Outputs:
- moved_state: float32 [32, 4, 96, 8, 128], P('gx', 'gy')
- rates: float32 [32, 4, 96, 4, 128], P('gx', 'gy')
- fluid_terms: float32 [32, 4, 2, 256], P('gx', 'gy')
Inputs may be any that keep to these rules, and one draw needn't show every extreme that they name: `leaving`: the 24 slots of one column are distinct. pairs[a, b, 0, k] names an own block; pairs[a, b, 1, k] names a neighbourhood block other than the own block itself. The first counts[a, b, 0] pairs have their partner in the own column (384 to 479), the other listed ones outside it. Slots at or beyond counts[a, b, 1] hold valid indices and are ignored. counts[a, b, 0] <= counts[a, b, 1]; some column lists all 576 pairs. `state`: radii lie in 0.3 to 0.7.
All inputs are finite; a program needn't handle non-finite values. No bound on the sum of `wall_flags` on one device may be relied on, other than what follows from the above.
Results may differ from a plain program's by a relative error of at most 0.0003.
Values sent between devices are 32-bit elements; how exact they have to be, the bound alone decides.
A program may use at most 64 MiB of HBM per device.

v0:
```python
import math

import jax
import jax.numpy as jnp
from jax import lax
from jax.sharding import PartitionSpec as P

pair_group = 16
cell_group = 32
soften = 0.01
stiffness = 0.2
damping = 0.05
conductance = 0.05
film_gain = 0.5
wall_gain = 2.0
wall_temp = 1.0
gravity = 1.0
cell_volume = 32.0


def with_halo(block, sides, width):
    for axis, dim in sides:
        count = lax.axis_size(axis)
        forward = [(i, i + 1) for i in range(count - 1)]
        forward.append((count - 1, 0))
        backward = [(target, source) for source, target in forward]
        low = lax.ppermute(
            lax.slice_in_dim(block, block.shape[dim] - width, None, axis=dim), axis, forward
        )
        high = lax.ppermute(lax.slice_in_dim(block, 0, width, axis=dim), axis, backward)
        block = jnp.concatenate([low, block, high], axis=dim)
    return block


def from_behind(value, axis, steps):
    count = lax.axis_size(axis)
    pairs = [(source, (source + steps) % count) for source in range(count)]
    return lax.ppermute(value, axis, pairs)


def pair_terms(blk_first, blk_second):
    pos_a = blk_first[:, 0:3]
    pos_b = blk_second[:, 0:3]
    delta = pos_a[:, :, :, None] - pos_b[:, :, None, :]
    dist = jnp.sqrt(jnp.sum(delta * delta, axis=1) + soften)
    vrel = blk_first[:, 3:6][:, :, :, None] - blk_second[:, 3:6][:, :, None, :]
    normal_speed = jnp.sum(vrel * delta, axis=1) / dist
    rad_a = blk_first[:, 7][:, :, None]
    rad_b = blk_second[:, 7][:, None, :]
    intersection = jnp.maximum(rad_a + rad_b - dist, 0.0)
    root = jnp.sqrt(intersection)
    weight = (stiffness * intersection * root - damping * root * normal_speed) / dist
    pushed = weight[:, None] * delta
    conduct = (
        conductance
        * jnp.sqrt(rad_a * rad_b / (rad_a + rad_b) * intersection)
        * (blk_second[:, 6][:, None, :] - blk_first[:, 6][:, :, None])
    )
    side_first = jnp.concatenate(
        [jnp.sum(pushed, axis=3), jnp.sum(conduct, axis=2)[:, None]], axis=1
    )
    side_second = -jnp.concatenate(
        [jnp.sum(pushed, axis=2), jnp.sum(conduct, axis=1)[:, None]], axis=1
    )
    return (side_first, side_second)


def select_rows(source, index):
    return jnp.take(source, index, axis=0)


def deposit_rows(totals, index, values):
    return totals.at[index].add(values)


def finish(mine, own, flags, cells, fluid_table):
    radius = mine[:, 7]
    temper = mine[:, 6]
    volume = 4.0 / 3.0 * math.pi * radius * radius * radius
    ncells = fluid_table.shape[0]
    blocks = cells.shape[0]
    cell_ids = jnp.arange(ncells)
    step_size = min(cell_group, blocks)

    def cell_pass(group):
        low = group * step_size
        cell_part = lax.dynamic_slice_in_dim(cells, low, step_size)
        radius_part = lax.dynamic_slice_in_dim(radius, low, step_size)
        temper_part = lax.dynamic_slice_in_dim(temper, low, step_size)
        volume_part = lax.dynamic_slice_in_dim(volume, low, step_size)
        matches = (cell_part[:, :, None] == cell_ids[None, None, :]).astype(jnp.float32)
        fluid_part = jnp.sum(matches * fluid_table[None, None, :], axis=2)
        flow_part = film_gain * radius_part * radius_part * (temper_part - fluid_part)
        solid_part = jnp.sum(matches * volume_part[:, :, None], axis=(0, 1))
        heat_part = jnp.sum(matches * flow_part[:, :, None], axis=(0, 1))
        return (flow_part, solid_part, heat_part)

    flows, solids, heats = lax.map(cell_pass, jnp.arange(blocks // step_size))
    to_fluid = flows.reshape(radius.shape)
    to_wall = wall_gain * flags.astype(jnp.float32) * (wall_temp - temper) * radius
    accel = own[:, 0:3] / volume[:, None]
    accel = accel.at[:, 2].add(-gravity)
    heating = (own[:, 3] + to_wall - to_fluid) / volume
    rates = jnp.concatenate([accel, heating[:, None]], axis=1)
    solid = jnp.sum(solids, axis=0) / cell_volume
    heat = jnp.sum(heats, axis=0)
    return (rates, jnp.stack([solid, heat]))


def padded(values):
    return jnp.concatenate([values, jnp.zeros((pair_group,), values.dtype)])


def sweep(
    acc, source, src_first, src_second, acc_first, acc_second, keep_first, keep_second, low, high
):
    turns = (high - low + pair_group - 1) // pair_group
    last_src = source.shape[0] - 1
    last_acc = acc.shape[0] - 1

    def turn(step, totals):
        start = (low + step * pair_group).astype(jnp.int32)
        live = (start + jnp.arange(pair_group) < high).astype(jnp.float32)

        def cut(values):
            return lax.dynamic_slice_in_dim(values, start, pair_group)

        take_first = jnp.clip(cut(src_first), 0, last_src)
        take_second = jnp.clip(cut(src_second), 0, last_src)
        side_first, side_second = pair_terms(
            select_rows(source, take_first), select_rows(source, take_second)
        )
        put_first = jnp.clip(cut(acc_first), 0, last_acc)
        put_second = jnp.clip(cut(acc_second), 0, last_acc)
        totals = deposit_rows(
            totals, put_first, side_first * (live * cut(keep_first))[:, None, None]
        )
        totals = deposit_rows(
            totals, put_second, side_second * (live * cut(keep_second))[:, None, None]
        )
        return totals

    return lax.fori_loop(0, turns, turn, acc)


def fetch_ghosts(mine):
    blocks = mine.shape[0]
    haloed = with_halo(mine[None, None], (("gx", 0), ("gy", 1)), 1)
    return haloed.reshape(9 * blocks, 8, mine.shape[2])


def shards(state, leaving, pairs, counts, wall_flags, cell_index, fluid_temp):
    blocks = state.shape[2]
    width = state.shape[4]
    center = 4 * blocks
    mine = state[0, 0]
    slots = leaving[0, 0]
    departing = select_rows(mine, slots)
    arrived = from_behind(departing, "gx", 1)
    mine = mine.at[slots].set(arrived)
    first = pairs[0, 0, 0]
    second = pairs[0, 0, 1]
    total = counts[0, 0, 1]
    first_pad = padded(first)
    second_pad = padded(second)
    ones = jnp.ones(first_pad.shape, jnp.float32)
    acc = jnp.zeros((9 * blocks, 4, width), jnp.float32)
    haloed = fetch_ghosts(mine)
    acc = sweep(
        acc,
        haloed,
        first_pad + center,
        second_pad,
        first_pad + center,
        second_pad,
        ones,
        ones,
        0,
        total,
    )
    grid = acc.reshape(3, 3, blocks, 4, width)
    rows = grid[:, 1]
    for offset in (1, -1):
        rows = rows + from_behind(grid[:, 1 + offset], "gy", offset)
    own = rows[1]
    for offset in (1, -1):
        own = own + from_behind(rows[1 + offset], "gx", offset)
    rates, fluid = finish(mine, own, wall_flags[0, 0], cell_index[0, 0], fluid_temp[0, 0])
    return (mine[None, None], rates[None, None], fluid[None, None])


def solution(mesh):
    in_specs = (
        P("gx", "gy", None, None, None),
        P("gx", "gy", None),
        P("gx", "gy", None, None),
        P("gx", "gy", None),
        P("gx", "gy", None, None),
        P("gx", "gy", None, None),
        P("gx", "gy", None),
    )
    out_specs = (
        P("gx", "gy", None, None, None),
        P("gx", "gy", None, None, None),
        P("gx", "gy", None, None),
    )
    return jax.shard_map(shards, mesh=mesh, in_specs=in_specs, out_specs=out_specs, check_vma=False)
```

profile of v0, /device:TPU:114, one launch (start us, length us, event | category | flops | bytes accessed | tf_op | source)
XLA Modules:
  0.0 619.2 jit_solution(39575184855771)
XLA Ops:
  3.9 4.5 collective-permute-done
  9.9 2.4 collective-permute-start.1
  12.3 7.7 %collective-permute-done.1 = f32[1,1,96,8,128]{4,3,2,1,0:T(8,128)S(1)} collective-permute-done((f32[1,1,96,8,128]{4,3,2,1,0:T(8,128)S(1)}, f32[1,1,96,8,128]{4,3,2,1,0:T(8,128)S(1)}, u32[]{:S(2)}, u32[]{:S(2)}) %collective-permute-start.1) | collective-permute-done | bytes 393248 | tf_op jit(solution)/shard_map/ppermute | solution.py:27
  20.0 4.3 collective-permute-done.2
  25.4 3.2 collective-permute-start.4
  32.8 21.9 %collective-permute-done.3 = f32[3,1,96,8,128]{4,3,2,1,0:T(8,128)S(1)} collective-permute-done((f32[3,1,96,8,128]{4,3,2,1,0:T(8,128)}, f32[3,1,96,8,128]{4,3,2,1,0:T(8,128)S(1)}, u32[]{:S(2)}, u32[]{:S(2)}) %collective-permute-start.3) | collective-permute-done | bytes 1179680 | tf_op jit(solution)/shard_map/ppermute | solution.py:27
  57.1 189.6 %while.27 = (s32[]{:T(128)}, f32[864,4,128]{2,1,0:T(4,128)S(1)}, s32[]{:T(128)}, s32[592]{0:T(1024)S(1)}, f32[864,8,128]{2,1,0:T(8,128)}, /*index=5*/s32[592]{0:...) while((s32[]{:T(128)}, f32[864,4,128]{2,1,0:T(4,128)S(1)}, s32[]{:T(128)}, ...), condition=%wide.region_10.12_spmd, body=%wide.region_1.11_spmd.sunk | while | flops 12396822 | bytes 9757671 | solution.py:143
  57.2 2.6 gather_fusion.1
  59.9 2.6 gather_fusion
  62.6 2.1 fusion.45
  66.2 2.1 fusion.49
  71.8 2.6 gather_fusion.1
  74.5 2.6 gather_fusion
  77.1 2.1 fusion.45
  80.8 2.1 fusion.49
  86.4 2.6 gather_fusion.1
  89.0 2.6 gather_fusion
  91.7 2.1 fusion.45
  95.4 2.1 fusion.49
  100.9 2.6 gather_fusion.1
  103.6 2.6 gather_fusion
  106.3 2.1 fusion.45
  110.0 2.1 fusion.49
  115.5 2.6 gather_fusion.1
  118.2 2.6 gather_fusion
  120.9 2.1 fusion.45
  124.6 2.1 fusion.49
  130.1 2.6 gather_fusion.1
  132.8 2.6 gather_fusion
  135.5 2.1 fusion.45
  139.2 2.1 fusion.49
  144.7 2.6 gather_fusion.1
  147.4 2.6 gather_fusion
  150.1 2.1 fusion.45
  153.8 2.1 fusion.49
  159.3 2.6 gather_fusion.1
  162.0 2.6 gather_fusion
  164.6 2.1 fusion.45
  168.3 2.1 fusion.49
  173.9 2.6 gather_fusion.1
  176.5 2.6 gather_fusion
  179.2 2.1 fusion.45
  182.9 2.1 fusion.49
  188.4 2.6 gather_fusion.1
  191.1 2.6 gather_fusion
  193.8 2.1 fusion.45
  197.5 2.1 fusion.49
  203.0 2.6 gather_fusion.1
  205.7 2.6 gather_fusion
  208.4 2.1 fusion.45
  212.1 2.1 fusion.49
  217.6 2.6 gather_fusion.1
  220.3 2.6 gather_fusion
  223.0 2.1 fusion.45
  226.7 2.1 fusion.49
  232.2 2.6 gather_fusion.1
  234.9 2.6 gather_fusion
  237.6 2.1 fusion.45
  247.6 131.7 %collective-permute-start.5 = (f32[3,96,4,128]{3,2,1,0:T(4,128)}, f32[3,96,4,128]{3,2,1,0:T(4,128)S(1)}, u32[]{:S(2)}, u32[]{:S(2)}) collective-permute-start(f32[3,96,4,128]{3,2,1,0:T(4,128)} %get-tuple-element.227), channel_id=1, source_target_pairs={{0,1},{1,2},{2,3},{3,0},{4,5},{5,6},{6,7},{7,4},{8,9},{9,10},{10,1... | collective-permute-start | bytes 1769480 | tf_op jit(solution)/shard_map/ppermute | solution.py:38
  379.2 72.9 %collective-permute-start.6 = (f32[3,96,4,128]{3,2,1,0:T(4,128)S(1)}, f32[3,96,4,128]{3,2,1,0:T(4,128)}, u32[]{:S(2)}, u32[]{:S(2)}) collective-permute-start(f32[3,96,4,128]{3,2,1,0:T(4,128)S(1)} %get-tuple-element.228), channel_id=1, source_target_pairs={{0,3},{1,0},{2,1},{3,2},{4,7},{5,4},{6,5},{7,6},{8,11},{9,8},{10,9... | collective-permute-start | bytes 1769480 | tf_op jit(solution)/shard_map/ppermute | solution.py:38
  452.1 20.3 %while.28 = (s32[]{:T(128)}, f32[3,32,128]{2,1,0:T(8,128)S(1)}, f32[3,256]{1,0:T(4,128)S(1)}, f32[3,256]{1,0:T(4,128)S(1)}, s32[3]{0:T(128)S(1)}, /*index=5*/f32...) while((s32[]{:T(128)}, f32[3,32,128]{2,1,0:T(8,128)S(1)}, ...), condition=%wide.region_15.17_spmd.clone, body=%wide.region_11.16_spmd.clone.sunk | while | flops 8400390 | bytes 236759 | solution.py:98
  473.7 134.5 %collective-permute-start.7 = (f32[96,4,128]{2,1,0:T(4,128)S(1)}, f32[96,4,128]{2,1,0:T(4,128)S(1)}, u32[]{:S(2)}, u32[]{:S(2)}) collective-permute-start(f32[96,4,128]{2,1,0:T(4,128)S(1)} %get-tuple-element.229), channel_id=1, source_target_pairs={{0,4},{4,8},{8,12},{12,16},{16,20},{20,24},{24,28},{28,32},{32,36}... | collective-permute-start | bytes 589832 | tf_op jit(solution)/shard_map/ppermute | solution.py:38
  608.9 2.6 collective-permute-done.7
  611.4 4.6 collective-permute-done.8
  (277 shorter events, 105.1 us)
Async XLA Ops:
  0.6 29.4 %copy-start.5 = (s32[1,1,2,576]{3,2,1,0:T(2,128)S(1)}, s32[1,1,2,576]{3,2,1,0:T(2,128)}, u32[]{:S(2)}) copy-start(s32[1,1,2,576]{3,2,1,0:T(2,128)} %param.17) | copy-start | bytes 13828
  0.6 28.0 %copy-start.7 = (s32[1,1,2]{2,1,0:T(1,128)S(1)}, s32[1,1,2]{2,1,0:T(1,128)}, u32[]{:S(2)}) copy-start(s32[1,1,2]{2,1,0:T(1,128)} %param.18) | copy-start | bytes 28
  3.7 4.7 collective-permute-start
  9.9 606.2 %copy-start = (f32[96,8,128]{2,1,0:T(8,128)}, f32[96,8,128]{2,1,0:T(8,128)S(1)}, u32[]{:S(2)}) copy-start(f32[96,8,128]{2,1,0:T(8,128)S(1)} %scatter_fusion.2) | copy-start | bytes 1179652
  9.9 10.1 %collective-permute-start.1 = (f32[1,1,96,8,128]{4,3,2,1,0:T(8,128)S(1)}, f32[1,1,96,8,128]{4,3,2,1,0:T(8,128)S(1)}, u32[]{:S(2)}, u32[]{:S(2)}) collective-permute-start(f32[1,1,96,8,128]{4,3,2,1,0:T(8,128)S(1)} %bitcast.87), channel_id=1, source_target_pairs={{0,4},{4,8},{8,12},{12,16},{16,20},{20,24},{24,28},{28,32},{32,36}... | collective-permute-start | bytes 1179656 | tf_op jit(solution)/shard_map/ppermute | solution.py:27
  12.3 12.0 %collective-permute-start.2 = (f32[1,1,96,8,128]{4,3,2,1,0:T(8,128)S(1)}, f32[1,1,96,8,128]{4,3,2,1,0:T(8,128)S(1)}, u32[]{:S(2)}, u32[]{:S(2)}) collective-permute-start(f32[1,1,96,8,128]{4,3,2,1,0:T(8,128)S(1)} %bitcast.88), channel_id=1, source_target_pairs={{4,0},{8,4},{12,8},{16,12},{20,16},{24,20},{28,24},{32,28},{36,32}... | collective-permute-start | bytes 1179656 | tf_op jit(solution)/shard_map/ppermute | solution.py:30
  25.4 29.4 %collective-permute-start.3 = (f32[3,1,96,8,128]{4,3,2,1,0:T(8,128)}, f32[3,1,96,8,128]{4,3,2,1,0:T(8,128)S(1)}, u32[]{:S(2)}, u32[]{:S(2)}) collective-permute-start(f32[3,1,96,8,128]{4,3,2,1,0:T(8,128)} %pad_maximum_fusion.1), channel_id=1, source_target_pairs={{0,1},{1,2},{2,3},{3,0},{4,5},{5,6},{6,7},{7,4},{8,9},{9,10},{10,1... | collective-permute-start | bytes 3538952 | tf_op jit(solution)/shard_map/ppermute | solution.py:27
  25.4 29.4 %collective-permute-start.4 = (f32[3,1,96,8,128]{4,3,2,1,0:T(8,128)}, f32[3,1,96,8,128]{4,3,2,1,0:T(8,128)S(1)}, u32[]{:S(2)}, u32[]{:S(2)}) collective-permute-start(f32[3,1,96,8,128]{4,3,2,1,0:T(8,128)} %pad_maximum_fusion.1), channel_id=1, source_target_pairs={{1,0},{2,1},{3,2},{0,3},{5,4},{6,5},{7,6},{4,7},{9,8},{10,9},{11,1... | collective-permute-start | bytes 3538952 | tf_op jit(solution)/shard_map/ppermute | solution.py:30
  32.2 22.6 %copy-start.1 = (f32[96,1,128]{2,1,0:T(1,128)}, f32[96,1,128]{2,1,0:T(1,128)S(1)}, u32[]{:S(2)}) copy-start(f32[96,1,128]{2,1,0:T(1,128)S(1)} %get-tuple-element.234) | copy-start | bytes 147460
  57.0 395.0 %copy-start.3 = (f32[3,32,128]{2,1,0:T(8,128)S(1)}, f32[3,32,128]{2,1,0:T(8,128)}, u32[]{:S(2)}) copy-start(f32[3,32,128]{2,1,0:T(8,128)} %custom-call.6) | copy-start | bytes 147460
  57.0 395.0 %copy-start.4 = (f32[1,1,256]{2,1,0:T(1,128)S(1)}, f32[1,1,256]{2,1,0:T(1,128)}, u32[]{:S(2)}) copy-start(f32[1,1,256]{2,1,0:T(1,128)} %param.21) | copy-start | bytes 3076
  57.1 395.0 %copy-start.6 = (f32[3,256]{1,0:T(4,128)S(1)}, f32[3,256]{1,0:T(4,128)}, u32[]{:S(2)}) copy-start(f32[3,256]{1,0:T(4,128)} %custom-call.8) | copy-start | bytes 9220
  247.6 368.6 %copy-start.2 = (f32[1,1,96,128]{3,2,1,0:T(8,128)S(1)}, f32[1,1,96,128]{3,2,1,0:T(8,128)}, u32[]{:S(2)}) copy-start(f32[1,1,96,128]{3,2,1,0:T(8,128)} %convert_multiply_fusion) | copy-start | bytes 147460
  247.6 224.8 %collective-permute-start.5 = (f32[3,96,4,128]{3,2,1,0:T(4,128)}, f32[3,96,4,128]{3,2,1,0:T(4,128)S(1)}, u32[]{:S(2)}, u32[]{:S(2)}) collective-permute-start(f32[3,96,4,128]{3,2,1,0:T(4,128)} %get-tuple-element.227), channel_id=1, source_target_pairs={{0,1},{1,2},{2,3},{3,0},{4,5},{5,6},{6,7},{7,4},{8,9},{9,10},{10,1... | collective-permute-start | bytes 1769480 | tf_op jit(solution)/shard_map/ppermute | solution.py:38
  379.2 93.2 %collective-permute-start.6 = (f32[3,96,4,128]{3,2,1,0:T(4,128)S(1)}, f32[3,96,4,128]{3,2,1,0:T(4,128)}, u32[]{:S(2)}, u32[]{:S(2)}) collective-permute-start(f32[3,96,4,128]{3,2,1,0:T(4,128)S(1)} %get-tuple-element.228), channel_id=1, source_target_pairs={{0,3},{1,0},{2,1},{3,2},{4,7},{5,4},{6,5},{7,6},{8,11},{9,8},{10,9... | collective-permute-start | bytes 1769480 | tf_op jit(solution)/shard_map/ppermute | solution.py:38
  473.7 137.7 %collective-permute-start.7 = (f32[96,4,128]{2,1,0:T(4,128)S(1)}, f32[96,4,128]{2,1,0:T(4,128)S(1)}, u32[]{:S(2)}, u32[]{:S(2)}) collective-permute-start(f32[96,4,128]{2,1,0:T(4,128)S(1)} %get-tuple-element.229), channel_id=1, source_target_pairs={{0,4},{4,8},{8,12},{12,16},{16,20},{20,24},{24,28},{28,32},{32,36}... | collective-permute-start | bytes 589832 | tf_op jit(solution)/shard_map/ppermute | solution.py:38
  608.3 7.8 %collective-permute-start.8 = (f32[96,4,128]{2,1,0:T(4,128)S(1)}, f32[96,4,128]{2,1,0:T(4,128)S(1)}, u32[]{:S(2)}, u32[]{:S(2)}) collective-permute-start(f32[96,4,128]{2,1,0:T(4,128)S(1)} %get-tuple-element.230), channel_id=1, source_target_pairs={{0,124},{4,0},{8,4},{12,8},{16,12},{20,16},{24,20},{28,24},{32,28}... | collective-permute-start | bytes 589832 | tf_op jit(solution)/shard_map/ppermute | solution.py:38
where the time goes:
time: 623 us; the launch traced here: 619 us
  starting transfers between devices  345 us (55%)
  other arithmetic  142 us (23%)
  local copies, waits for them, and re-layouts  81.2 us (13%)
  waiting for transfers between devices  45.6 us (7%)
    ppermute x5, starting transfers between devices, from_behind(): return lax.ppermute(value, axis, pairs)  339 us
    gather x27, local copies, waits for them, and re-layouts, select_rows(): return jnp.take(source, index, axis=0)  67.1 us
    ppermute x2, waiting for transfers between devices, with_halo(): lax.ppermute(lax.slice_in_dim(block, block.shape[dim] - width, None, axis...  29.6 us
    scatter-add x26, other arithmetic, deposit_rows(): return totals.at[index].add(values)  28.4 us
    reduce_sum x13, other arithmetic, pair_terms(): normal_speed = jnp.sum(vrel * delta, axis=1) / dist  27 us
    reduce_sum x13, other arithmetic, pair_terms(): jnp.sum(pushed, axis=2)  26.7 us
    div x13, other arithmetic, pair_terms(): (stiffness * intersection * root - damping * root * normal_speed) / dist  20.2 us
  transfers between devices with their start and end apart: 9, of which 6 were waited for; matrix products, arithmetic and copies ran while one was open for 4% of the time, Pallas kernels for 0%

commit v1 on v0

v1 whole, which is shorter than its diff:
```python
import functools
import math

import jax
import jax.numpy as jnp
from jax import lax
from jax.experimental import pallas as pl
from jax.experimental.pallas import tpu as pltpu
from jax.sharding import PartitionSpec as P

soften = 0.01
stiffness = 0.2
damping = 0.05
conductance = 0.05
film_gain = 0.5
wall_gain = 2.0
wall_temp = 1.0
gravity = 1.0
cell_volume = 32.0

f32 = jnp.float32
bf16 = jnp.bfloat16
i32 = jnp.int32

tiny = 1e-30
group = 12
lag_a = 2
lag_b = 2
ring = lag_a + lag_b
MESH = pl.DeviceIdType.MESH


def iota(shape, dim):
    return lax.broadcasted_iota(i32, shape, dim)


def split2(value):
    hi = value.astype(bf16).astype(f32)
    return hi, (value - hi).astype(bf16).astype(f32)


def split3(value):
    hi = value.astype(bf16).astype(f32)
    rest = value - hi
    mid = rest.astype(bf16).astype(f32)
    return hi, mid, rest - mid


def dot_tt(left, right):
    return lax.dot_general(left, right, (((1,), (1,)), ((), ())), preferred_element_type=f32)


def neighbours():
    a = lax.axis_index("gx")
    b = lax.axis_index("gy")
    na = lax.axis_size("gx")
    nb = lax.axis_size("gy")
    return (
        {"gx": lax.rem(a + 1, na)},
        {"gx": lax.rem(a + na - 1, na)},
        {"gy": lax.rem(b + 1, nb)},
        {"gy": lax.rem(b + nb - 1, nb)},
    )


def greet(everyone):
    barrier = pltpu.get_barrier_semaphore()
    for device in everyone:
        pl.semaphore_signal(barrier, inc=1, device_id=device, device_id_type=MESH)
    pl.semaphore_wait(barrier, len(everyone))


def sort_pairs(lanes, pad, total):
    own = pad[0:1, :]
    code = pad[1:2, :]
    region = jnp.zeros_like(code)
    for step in range(1, 9):
        region = region + (code >= 96 * step).astype(i32)
    far = code - 96 * region
    live = iota((1, lanes), 1) < total

    def among(*names):
        hit = region == names[0]
        for name in names[1:]:
            hit = hit | (region == name)
        return hit

    kind = jnp.where(among(1, 4, 5), 0, jnp.where(among(0, 3), 1, jnp.where(among(2), 2, 3)))
    kind = jnp.where(live, kind, 4)
    u_far = among(0, 1, 2, 3)
    u = jnp.where(u_far, far, own) + jnp.where(among(4, 5, 3), 0, 96)
    v_slot = jnp.where(u_far, own, far)
    v_side = jnp.where(among(4, 1, 7), 0, jnp.where(among(5, 3, 0, 8), 1, 2))
    ranks = iota((8, lanes), 0)
    marks = (ranks == kind).astype(f32)
    before = (iota((lanes, lanes), 0) < iota((lanes, lanes), 1)).astype(bf16)
    seen = jnp.dot(marks.astype(bf16), before, preferred_element_type=f32)
    starts = jnp.sum((kind < ranks).astype(f32), axis=1, keepdims=True)
    place = jnp.sum(marks * (seen + starts), axis=0, keepdims=True)
    target = (iota((lanes, lanes), 0).astype(f32) == place).astype(bf16)
    rows = iota((8, lanes), 0)
    values = jnp.where(
        rows == 0, u, jnp.where(rows == 1, v_slot, jnp.where(rows == 2, v_side, 0))
    )
    moved = dot_tt(values.astype(bf16), target)
    packed = moved[0:1] + 256.0 * (moved[1:2] + 96.0 * moved[2:3])
    diag = iota((8, 128), 0) == iota((8, 128), 1)
    begin = jnp.sum(jnp.where(diag, starts, 0.0), axis=0, keepdims=True)
    return packed.astype(i32), begin.astype(i32)


def halo_kernel(
    leaving_ref,
    counts_ref,
    pairs_ref,
    state_ref,
    cols_ref,
    lists_ref,
    cat,
    dep,
    moved,
    pad,
    slot_vec,
    slot_smem,
    dep_send,
    dep_recv,
    list_send,
    list_recv,
    col_send,
    col_recv,
    local_sem,
):
    blocks = state_ref.shape[0]
    count = leaving_ref.shape[0]
    ahead, behind, up, down = neighbours()
    for m in range(count):
        dep[m] = state_ref[leaving_ref[m]]
    greet((ahead, behind, up, down))
    depart = pltpu.make_async_remote_copy(
        src_ref=dep,
        dst_ref=cat.at[0:count],
        send_sem=dep_send,
        recv_sem=dep_recv,
        device_id=ahead,
        device_id_type=MESH,
    )
    depart.start()
    place = iota((8, 128), 1)
    slot = place + count
    for m in range(count):
        slot = jnp.where(place == leaving_ref[m], m, slot)
    slot_vec[...] = slot
    to_smem = pltpu.make_async_copy(slot_vec, slot_smem, local_sem)
    to_smem.start()
    cat[count : count + blocks] = state_ref[...]
    lanes = pad.shape[1]
    pad[...] = jnp.zeros_like(pad)
    pad[0:2, 0 : pairs_ref.shape[1]] = pairs_ref[...]
    packed, begin = sort_pairs(lanes, pad, counts_ref[1])
    lists_ref[0] = jnp.zeros((8, 128), i32)
    for row in range(lanes // 128):
        lists_ref[0, row : row + 1, :] = packed[:, 128 * row : 128 * row + 128]
    lists_ref[0, 6:7, :] = begin
    copies = []
    for at, device in ((1, down), (2, up), (3, ahead)):
        copy = pltpu.make_async_remote_copy(
            src_ref=lists_ref.at[0],
            dst_ref=lists_ref.at[at],
            send_sem=list_send.at[at - 1],
            recv_sem=list_recv.at[at - 1],
            device_id=device,
            device_id_type=MESH,
        )
        copy.start()
        copies.append(copy)
    to_smem.wait()
    depart.wait()

    def place_block(j, carry):
        moved[j] = cat[slot_smem[0, j]]
        return carry

    lax.fori_loop(0, blocks, place_block, 0)
    keep = pltpu.make_async_copy(moved, cols_ref.at[0], local_sem)
    keep.start()
    for at, device in ((1, ahead), (2, down), (3, up)):
        copy = pltpu.make_async_remote_copy(
            src_ref=moved,
            dst_ref=cols_ref.at[at],
            send_sem=col_send.at[at - 1],
            recv_sem=col_recv.at[at - 1],
            device_id=device,
            device_id_type=MESH,
        )
        copy.start()
        copies.append(copy)
    keep.wait()
    for copy in copies:
        copy.wait()


def build_tables(cols_ref, U, V, L, RB, extra):
    rows = iota((8, 128), 0)
    eye = (iota((128, 128), 0) == iota((128, 128), 1)).astype(bf16)
    c6 = jnp.where(rows == 6, 1.0, 0.0)
    c7 = jnp.where(rows == 7, 0.25, 0.0)
    ca = jnp.where(rows < 3, -2.0, 0.0)
    cb = jnp.where(rows < 6, -0.25, 0.0)
    ones = jnp.where(rows >= 6, 1.0, 0.0)

    def dense(g, carry):
        at = pl.ds(g * 8, 8)
        x = [cols_ref[at, c, :] for c in range(3)]
        v = [cols_ref[at, c, :] for c in range(3, 6)]
        root = jnp.sqrt(cols_ref[at, 7, :])
        extra[at, 3, :] = jnp.ones((8, 128), f32)
        extra[at, 4, :] = root * cols_ref[at, 6, :]
        extra[at, 5, :] = root
        extra[at, 6, :] = x[0] * x[0] + x[1] * x[1] + x[2] * x[2] + 0.5 * soften
        extra[at, 7, :] = x[0] * v[0] + x[1] * v[1] + x[2] * v[2]
        return carry

    lax.fori_loop(0, cols_ref.shape[0] // 8, dense, 0, unroll=2)

    def one(i, want_u, v_at):
        S = cols_ref[i]
        E = extra[i]
        hi, mid = split2(jnp.where(rows < 3, S, jnp.where(rows < 6, E, 0.0)))
        L[i] = jnp.concatenate([hi, mid], axis=0).astype(bf16)
        full = jnp.where(rows < 6, S, E)
        hi, mid, lo = split3(full)
        if want_u:
            natural = jnp.concatenate(
                [hi, jnp.where(rows < 6, hi, lo), mid, ones, ones, ones], axis=0
            ).astype(bf16)
            U[i] = dot_tt(eye, natural).astype(bf16)
        if v_at is not None:
            def swap(value):
                return jnp.where(
                    rows < 3, pltpu.roll(value, 5, 0), pltpu.roll(value, 3, 0)
                )

            a0 = hi * ca + c6
            a1 = mid * ca + c6
            b0 = swap(hi) * cb + c7
            b1 = swap(mid) * cb + c7
            A = jnp.concatenate([a0, a1, a0, hi * c6, mid * c6, lo * c6], axis=0)
            B = jnp.concatenate([b0, b1, b0, hi * c7, mid * c7, lo * c7], axis=0)
            V[v_at, :, 0:128] = A.astype(bf16)
            V[v_at, :, 128:256] = B.astype(bf16)

    def sweep(low, high, want_u, shift):
        step = 4

        def body(t, carry):
            for q in range(step):
                i = low + t * step + q
                one(i, want_u, None if shift is None else i + shift)
            return carry

        lax.fori_loop(0, (high - low) // step, body, 0)

    sweep(0, 96, True, 0)
    sweep(96, 192, True, None)
    sweep(192, 384, False, -96)

    for col in range(2):
        radius = cols_ref[96 * col : 96 * col + 96, 7, :]
        turned = jnp.concatenate([radius, jnp.zeros((32, 128), f32)], axis=0).T

        def spread(g, carry, turned=turned, col=col):
            here = pltpu.roll(turned, lax.rem(128 - 8 * g, 128), 1)
            for c in range(8):
                RB[96 * col + 8 * g + c] = jnp.broadcast_to(here[:, c : c + 1], (128, 128))
            return carry

        lax.fori_loop(0, 12, spread, 0)


def pair_kernel(lists_ref, cols_ref, moved_ref, own_ref, sides_ref, U, V, L, RB, extra, acc, *rings):
    AB = rings[0:ring]
    M = rings[ring : 2 * ring]
    moved_ref[...] = cols_ref[0:96]
    build_tables(cols_ref, U, V, L, RB, extra)
    trash = acc.shape[0] - 1
    acc[...] = jnp.zeros_like(acc)

    ends = []
    shifts = []
    so_far = 0
    for at in range(4):
        low = lists_ref[at * 1024 + 6 * 128 + at]
        high = lists_ref[at * 1024 + 6 * 128 + at + 1]
        shifts.append(at * 1024 + low - so_far)
        so_far = so_far + (high - low)
        ends.append(so_far)
    n = ends[3]
    last = jnp.maximum(n - 1, 0)

    def entry(k):
        k = jnp.minimum(k, last)
        shift = jnp.where(
            k < ends[0],
            shifts[0],
            jnp.where(k < ends[1], shifts[1], jnp.where(k < ends[2], shifts[2], shifts[3])),
        )
        code = lists_ref[k + shift]
        return code & 255, lax.shift_right_logical(code, 8)

    def spot(v):
        return jnp.where(v < 96, v, v + 96)

    def distances(k, at):
        u, v = entry(k)
        AB[at][...] = jnp.dot(U[u], V[v], preferred_element_type=f32)

    def weights(k, at):
        u, v = entry(k)
        rt = cols_ref[spot(v), 7:8, :]
        for r in range(0, 128, 16):
            A = AB[at][r : r + 16, 0:128]
            B = AB[at][r : r + 16, 128:256]
            R = RB[u, r : r + 16, :] + rt
            inv = lax.rsqrt(A)
            gap = R - A * inv
            inter = jnp.maximum(gap, 0.0)
            root = inter * lax.rsqrt(jnp.maximum(gap, tiny))
            W = (root * inv) * (inter - B * inv)
            G = root * lax.rsqrt(R)
            wh = W.astype(bf16)
            gh = G.astype(bf16)
            M[at][r : r + 16, 0:128] = wh
            M[at][r : r + 16, 128:256] = gh
            M[at][128 + r : 144 + r, 0:128] = (W - wh.astype(f32)).astype(bf16)
            M[at][128 + r : 144 + r, 128:256] = (G - gh.astype(f32)).astype(bf16)

    rows = iota((8, 128), 0)

    def folded(out):
        both = out[0:8] + out[8:16]
        return jnp.where(rows < 4, both[:, 0:128], both[:, 128:256])

    def sums(k, at):
        u, v = entry(k)
        w = spot(v)
        first = jnp.concatenate([L[u], L[u]], axis=1)
        second = jnp.concatenate([L[w], L[w]], axis=1)
        m = M[at]
        crossed = jnp.concatenate(
            [
                jnp.concatenate([m[0:128, 0:128], m[128:256, 0:128]], axis=1),
                jnp.concatenate([m[0:128, 128:256], m[128:256, 128:256]], axis=1),
            ],
            axis=0,
        )
        to_second = folded(jnp.dot(first, m[...], preferred_element_type=f32))
        to_first = folded(dot_tt(second, crossed))
        live = k < n
        u = jnp.where(live, u, trash)
        w = jnp.where(live, w, trash)
        acc[u] += to_first
        acc[w] += to_second

    for q in range(ring):
        distances(q, q)
    for q in range(lag_b):
        weights(q, q)

    def turn(t, carry):
        for q in range(group):
            k = t * group + q
            sums(k, q % ring)
            weights(k + lag_b, (q + lag_b) % ring)
            distances(k + ring, q % ring)
        return carry

    lax.fori_loop(0, lax.div(n + group - 1, group), turn, 0)

    def result(i):
        S = cols_ref[i]
        got = acc[i]
        hi, mid = split2(S)
        force = stiffness * ((hi + mid) * got[3:4] - got)
        heat = conductance * jnp.sqrt(S[7:8]) * (got[4:5] - S[6:7] * got[5:6])
        return jnp.where(rows < 3, force, jnp.where(rows == 3, heat, 0.0))

    def close(t, carry):
        for q in range(4):
            i = t * 4 + q
            own_ref[i] = result(i)
        return carry

    lax.fori_loop(0, 24, close, 0)

    def close_far(t, carry):
        for q in range(4):
            i = t * 4 + q
            lower = result(96 + 2 * i)
            upper = result(97 + 2 * i)
            sides_ref[i] = jnp.where(rows < 4, lower, pltpu.roll(upper, 4, 0))
        return carry

    lax.fori_loop(0, 36, close_far, 0)


def finish_kernel(
    moved_ref,
    own_ref,
    sides_ref,
    flags_ref,
    cells_ref,
    table_ref,
    rates_ref,
    fluid_ref,
    got,
    heat_in,
    to_fluid,
    sums,
    send,
    recv,
):
    ahead, behind, up, down = neighbours()
    greet((ahead, behind, up, down))
    copies = []
    for at, device in ((0, behind), (1, up), (2, down)):
        copy = pltpu.make_async_remote_copy(
            src_ref=sides_ref.at[at],
            dst_ref=got.at[at],
            send_sem=send.at[at],
            recv_sem=recv.at[at],
            device_id=device,
            device_id_type=MESH,
        )
        copy.start()
        copies.append(copy)

    table = jnp.concatenate(split3(table_ref[...]), axis=0).astype(bf16)
    sums[...] = jnp.zeros_like(sums)
    sub = iota((16, 128), 0)

    def cells_of(g, carry):
        at = pl.ds(g * 8, 8)
        temper = moved_ref[at, 6, :]
        radius = moved_ref[at, 7, :]
        volume = 4.0 / 3.0 * math.pi * radius * radius * radius
        cell = cells_ref[at, :]
        high = lax.shift_right_logical(cell, 4)
        low = cell & 15
        fluid = []
        hots = []
        for c in range(8):
            hot_high = (sub == high[c : c + 1]).astype(f32)
            hot_low = (sub == low[c : c + 1]).astype(f32)
            parts = jnp.dot(table, hot_low.astype(bf16), preferred_element_type=f32)
            value = parts[0:16] + parts[16:32] + parts[32:48]
            fluid.append(jnp.sum(value * hot_high, axis=0, keepdims=True))
            hots.append((hot_high, hot_low))
        flow = film_gain * radius * radius * (temper - jnp.concatenate(fluid, axis=0))
        to_fluid[at, :] = flow
        pieces = split3(volume) + split3(flow)
        total = sums[...]
        for c in range(8):
            hot_high, hot_low = hots[c]
            spread = jnp.concatenate([hot_low * piece[c : c + 1] for piece in pieces], axis=0)
            total = total + dot_tt(hot_high.astype(bf16), spread.astype(bf16))
        sums[...] = total
        wall = wall_gain * flags_ref[at, :].astype(f32) * (wall_temp - temper) * radius
        heat_in[at, :] = wall - flow
        return carry

    lax.fori_loop(0, 12, cells_of, 0)
    total = sums[...]
    fluid_ref[0] = (total[:, 0:16] + total[:, 16:32] + total[:, 32:48]) / cell_volume
    fluid_ref[1] = total[:, 48:64] + total[:, 64:80] + total[:, 80:96]
    for copy in copies:
        copy.wait()

    def combine(g, carry):
        at = pl.ds(g * 8, 8)
        radius = moved_ref[at, 7, :]
        volume = 4.0 / 3.0 * math.pi * radius * radius * radius
        inverse = 1.0 / volume
        half = pl.ds(g * 4, 4)
        for c in range(4):
            near = own_ref[at, c, :]
            even = got[0, half, c, :] + got[1, half, c, :] + got[2, half, c, :]
            odd = got[0, half, c + 4, :] + got[1, half, c + 4, :] + got[2, half, c + 4, :]
            far = jnp.stack([even, odd], axis=1).reshape(8, 128)
            value = near + far
            if c == 3:
                value = value + heat_in[at, :]
            value = value * inverse
            if c == 2:
                value = value - gravity
            rates_ref[at, c, :] = value
        return carry

    lax.fori_loop(0, 12, combine, 0)


def vmem():
    return pl.BlockSpec(memory_space=pltpu.VMEM)


def smem():
    return pl.BlockSpec(memory_space=pltpu.SMEM)


def shards(state, leaving, pairs, counts, wall_flags, cell_index, fluid_temp):
    mine = state[0, 0]
    blocks = mine.shape[0]
    count = leaving.shape[2]
    lanes = -(-pairs.shape[3] // 128) * 128
    cols, lists = pl.pallas_call(
        halo_kernel,
        out_shape=(
            jax.ShapeDtypeStruct((4, blocks, 8, 128), f32),
            jax.ShapeDtypeStruct((4, 8, 128), i32),
        ),
        in_specs=[smem(), smem(), vmem(), vmem()],
        out_specs=(pl.BlockSpec(memory_space=pl.ANY), vmem()),
        scratch_shapes=[
            pltpu.VMEM((count + blocks, 8, 128), f32),
            pltpu.VMEM((count, 8, 128), f32),
            pltpu.VMEM((blocks, 8, 128), f32),
            pltpu.VMEM((8, lanes), i32),
            pltpu.VMEM((8, 128), i32),
            pltpu.SMEM((8, 128), i32),
            pltpu.SemaphoreType.DMA,
            pltpu.SemaphoreType.DMA,
            pltpu.SemaphoreType.DMA((3,)),
            pltpu.SemaphoreType.DMA((3,)),
            pltpu.SemaphoreType.DMA((3,)),
            pltpu.SemaphoreType.DMA((3,)),
            pltpu.SemaphoreType.DMA,
        ],
        compiler_params=pltpu.CompilerParams(
            collective_id=0, has_side_effects=True, vmem_limit_bytes=16 * 2**20
        ),
        name="halo",
    )(leaving[0, 0], counts[0, 0], pairs[0, 0], mine)

    moved, own, sides = pl.pallas_call(
        pair_kernel,
        out_shape=(
            jax.ShapeDtypeStruct((blocks, 8, 128), f32),
            jax.ShapeDtypeStruct((blocks, 8, 128), f32),
            jax.ShapeDtypeStruct((3 * blocks // 2, 8, 128), f32),
        ),
        in_specs=[smem(), vmem()],
        out_specs=(vmem(), vmem(), vmem()),
        scratch_shapes=[
            pltpu.VMEM((2 * blocks, 128, 48), bf16),
            pltpu.VMEM((3 * blocks, 48, 256), bf16),
            pltpu.VMEM((4 * blocks, 16, 128), bf16),
            pltpu.VMEM((2 * blocks, 128, 128), f32),
            pltpu.VMEM((4 * blocks, 8, 128), f32),
            pltpu.VMEM((4 * blocks + 1, 8, 128), f32),
        ]
        + [pltpu.VMEM((128, 256), f32)] * ring
        + [pltpu.VMEM((256, 256), bf16)] * ring,
        compiler_params=pltpu.CompilerParams(vmem_limit_bytes=52 * 2**20),
        name="contact",
    )(lists.reshape(4096), cols.reshape(4 * blocks, 8, 128))

    rates, fluid = pl.pallas_call(
        finish_kernel,
        out_shape=(
            jax.ShapeDtypeStruct((blocks, 4, 128), f32),
            jax.ShapeDtypeStruct((2, 16, 16), f32),
        ),
        in_specs=[vmem()] * 6,
        out_specs=(vmem(), vmem()),
        scratch_shapes=[
            pltpu.VMEM((3, blocks // 2, 8, 128), f32),
            pltpu.VMEM((blocks, 128), f32),
            pltpu.VMEM((blocks, 128), f32),
            pltpu.VMEM((16, 96), f32),
            pltpu.SemaphoreType.DMA((3,)),
            pltpu.SemaphoreType.DMA((3,)),
        ],
        compiler_params=pltpu.CompilerParams(
            collective_id=1, has_side_effects=True, vmem_limit_bytes=16 * 2**20
        ),
        name="finish",
    )(
        moved,
        own,
        sides.reshape(3, blocks // 2, 8, 128),
        wall_flags[0, 0],
        cell_index[0, 0],
        fluid_temp.reshape(16, 16),
    )
    return moved[None, None], rates[None, None], fluid.reshape(1, 1, 2, 256)


def solution(mesh):
    in_specs = (
        P("gx", "gy", None, None, None),
        P("gx", "gy", None),
        P("gx", "gy", None, None),
        P("gx", "gy", None),
        P("gx", "gy", None, None),
        P("gx", "gy", None, None),
        P("gx", "gy", None),
    )
    out_specs = (
        P("gx", "gy", None, None, None),
        P("gx", "gy", None, None, None),
        P("gx", "gy", None, None),
    )
    return jax.shard_map(shards, mesh=mesh, in_specs=in_specs, out_specs=out_specs, check_vma=False)
```

time: 623 us -> 106 us (0.17)
  the two profiles are of different devices: /device:TPU:114 before, /device:TPU:3 now
where the time goes in v1:
time: 106 us
  Pallas kernels  97.4 us (92%)
  local copies, waits for them, and re-layouts  7.06 us (7%)
    pallas_call x1, Pallas kernels, shards(): pl.pallas_call(pair_kernel, out_shape=(jax.ShapeDtypeStruct((blocks, 8, 1...  44.6 us
    pallas_call x1, Pallas kernels, shards(): pl.pallas_call(finish_kernel, out_shape=(jax.ShapeDtypeStruct((blocks, 4,...  31.5 us
    pallas_call x1, Pallas kernels, shards(): pl.pallas_call(halo_kernel, out_shape=(jax.ShapeDtypeStruct((4, blocks, 8...  21.4 us
    unnamed x20, local copies, waits for them, and re-layouts  6.32 us

profile of v1, /device:TPU:3, one launch (start us, length us, event | category | flops | bytes accessed | tf_op | source)
XLA Modules:
  0.0 105.9 jit_solution(7628113369740339367)
XLA Ops:
  0.6 0.0 copy-start.8
  0.6 0.0 copy-start.1
  0.7 1.0 copy-done.1
  1.6 0.0 copy-start.5
  1.6 0.7 copy-done.5
  2.3 0.0 copy-start.6
  2.3 0.7 copy-done.6
  3.0 0.0 copy-start.7
  3.0 0.7 copy-done.7
  3.6 0.0 copy-start.3
  3.6 0.0 copy-start.4
  3.7 21.4 %halo.1 = (f32[4,96,8,128]{3,2,1,0:T(8,128)S(1)}, s32[4,8,128]{2,1,0:T(8,128)S(1)}) custom-call(s32[24]{0:T(128)S(1)} %bitcast.20, s32[2]{0:T(128)S(1)} %bitcast.21, s32[2,576]{1,0:T(2,128)S(1)} %bitcast.19, f32[96,8,128]{2,1,0:T(8,128)S(1)} %bitcast.13), custom_call_target="tpu_custom_call" | custom-call | tf_op jit(solution)/shard_map/halo/pallas_call | solution.py:514
  25.0 0.0 copy-start
  25.0 1.1 %copy-done = f32[4,96,8,128]{3,2,1,0:T(8,128)} copy-done((f32[4,96,8,128]{3,2,1,0:T(8,128)}, f32[4,96,8,128]{3,2,1,0:T(8,128)S(1)}, u32[]{:S(2)}) %copy-start) | copy-done | bytes 1572888
  26.2 44.6 %contact.1 = (f32[96,8,128]{2,1,0:T(8,128)}, f32[96,8,128]{2,1,0:T(8,128)S(1)}, f32[144,8,128]{2,1,0:T(8,128)S(1)}) custom-call(s32[4096]{0:T(1024)S(1)} %bitcast.18, f32[384,8,128]{2,1,0:T(8,128)} %bitcast.11), custom_call_target="tpu_custom_call" | custom-call | tf_op jit(solution)/shard_map/contact/pallas_call | solution.py:543
  70.8 0.5 broadcast.3
  71.3 0.0 copy-done.8
  71.3 0.7 reduce.3
  71.9 0.1 reshape.24.table_ref
  72.0 0.0 copy-done.3
  72.0 0.0 copy-done.4
  72.0 0.0 copy-start.2
  72.0 1.0 copy-done.2
  73.0 31.5 %finish.1 = (f32[96,4,128]{2,1,0:T(4,128)S(1)}, f32[2,16,16]{2,1,0:T(8,128)S(1)}) custom-call(f32[96,8,128]{2,1,0:T(8,128)S(1)} %copy-done.2, f32[96,8,128]{2,1,0:T(8,128)S(1)} %get-tuple-element.13.own_ref, f32[3,48,8,128]{3,2,1,0:T(8,128)S(1)} %bitcast.12, s32[96,128]{1,0:T(8,128)S(1)} %bitcast.16, s32[96,128]{1,0:T(8,128)S(1)} %bitcast.17, ...), custom_call_target="tpu_custom_call" | custom-call | tf_op jit(solution)/shard_map/finish/pallas_call | solution.py:566
  104.5 0.7 reshape.25
  105.2 0.7 copy.11
Async XLA Ops:
  0.6 70.6 %copy-start.8 = (f32[1,1,256]{2,1,0:T(1,128)S(1)}, f32[1,1,256]{2,1,0:T(1,128)}, u32[]{:S(2)}) copy-start(f32[1,1,256]{2,1,0:T(1,128)} %param.13) | copy-start | bytes 3076
  0.6 1.0 copy-start.1
  1.6 0.7 copy-start.5
  2.3 0.7 copy-start.6
  3.0 0.7 copy-start.7
  3.6 68.4 %copy-start.3 = (s32[1,1,96,128]{3,2,1,0:T(8,128)S(1)}, s32[1,1,96,128]{3,2,1,0:T(8,128)}, u32[]{:S(2)}) copy-start(s32[1,1,96,128]{3,2,1,0:T(8,128)} %param.11) | copy-start | bytes 147460
  3.6 68.4 %copy-start.4 = (s32[1,1,96,128]{3,2,1,0:T(8,128)S(1)}, s32[1,1,96,128]{3,2,1,0:T(8,128)}, u32[]{:S(2)}) copy-start(s32[1,1,96,128]{3,2,1,0:T(8,128)} %param.12) | copy-start | bytes 147460
  25.0 1.1 %copy-start = (f32[4,96,8,128]{3,2,1,0:T(8,128)}, f32[4,96,8,128]{3,2,1,0:T(8,128)S(1)}, u32[]{:S(2)}) copy-start(f32[4,96,8,128]{3,2,1,0:T(8,128)S(1)} %get-tuple-element.11) | copy-start | bytes 4718596
  72.0 1.0 copy-start.2

commit v2 on v1

--- a/solution.py
+++ b/solution.py
@@ -85,8 +85,12 @@
             hit = hit | (region == name)
         return hit
 
-    kind = jnp.where(among(1, 4, 5), 0, jnp.where(among(0, 3), 1, jnp.where(among(2), 2, 3)))
-    kind = jnp.where(live, kind, 4)
+    kind = jnp.where(
+        among(4),
+        0,
+        jnp.where(among(1, 5), 1, jnp.where(among(0, 3), 2, jnp.where(among(2), 3, 4))),
+    )
+    kind = jnp.where(live, kind, 5)
     u_far = among(0, 1, 2, 3)
     u = jnp.where(u_far, far, own) + jnp.where(among(4, 5, 3), 0, 96)
     v_slot = jnp.where(u_far, own, far)
@@ -110,12 +114,15 @@
 
 
 def halo_kernel(
+    leaving_hbm,
+    counts_hbm,
+    pairs_hbm,
+    state_hbm,
+    cols_ref,
+    lists_ref,
     leaving_ref,
     counts_ref,
     pairs_ref,
-    state_ref,
-    cols_ref,
-    lists_ref,
     cat,
     dep,
     moved,
@@ -129,10 +136,27 @@
     col_send,
     col_recv,
     local_sem,
+    in_sem,
 ):
-    blocks = state_ref.shape[0]
-    count = leaving_ref.shape[0]
+    blocks = state_hbm.shape[0]
+    count = leaving_hbm.shape[0]
     ahead, behind, up, down = neighbours()
+    state_ref = cat.at[count : count + blocks]
+    inputs = [
+        pltpu.make_async_copy(source, target, in_sem.at[at])
+        for at, (source, target) in enumerate(
+            (
+                (leaving_hbm, leaving_ref),
+                (state_hbm, state_ref),
+                (pairs_hbm, pairs_ref),
+                (counts_hbm, counts_ref),
+            )
+        )
+    ]
+    for copy in inputs:
+        copy.start()
+    inputs[0].wait()
+    inputs[1].wait()
     for m in range(count):
         dep[m] = state_ref[leaving_ref[m]]
     greet((ahead, behind, up, down))
@@ -152,7 +176,8 @@
     slot_vec[...] = slot
     to_smem = pltpu.make_async_copy(slot_vec, slot_smem, local_sem)
     to_smem.start()
-    cat[count : count + blocks] = state_ref[...]
+    inputs[2].wait()
+    inputs[3].wait()
     lanes = pad.shape[1]
     pad[...] = jnp.zeros_like(pad)
     pad[0:2, 0 : pairs_ref.shape[1]] = pairs_ref[...]
@@ -199,7 +224,7 @@
         copy.wait()
 
 
-def build_tables(cols_ref, U, V, L, RB, extra):
+def build_tables(cols_ref, U, V, L, RB, extra, start, step):
     rows = iota((8, 128), 0)
     eye = (iota((128, 128), 0) == iota((128, 128), 1)).astype(bf16)
     c6 = jnp.where(rows == 6, 1.0, 0.0)
@@ -207,9 +232,10 @@
     ca = jnp.where(rows < 3, -2.0, 0.0)
     cb = jnp.where(rows < 6, -0.25, 0.0)
     ones = jnp.where(rows >= 6, 1.0, 0.0)
-
-    def dense(g, carry):
-        at = pl.ds(g * 8, 8)
+    zeros = jnp.zeros((8, 128), f32)
+
+    def dense(base):
+        at = pl.ds(base, 8)
         x = [cols_ref[at, c, :] for c in range(3)]
         v = [cols_ref[at, c, :] for c in range(3, 6)]
         root = jnp.sqrt(cols_ref[at, 7, :])
@@ -218,97 +244,140 @@
         extra[at, 5, :] = root
         extra[at, 6, :] = x[0] * x[0] + x[1] * x[1] + x[2] * x[2] + 0.5 * soften
         extra[at, 7, :] = x[0] * v[0] + x[1] * v[1] + x[2] * v[2]
-        return carry
-
-    lax.fori_loop(0, cols_ref.shape[0] // 8, dense, 0, unroll=2)
-
-    def one(i, want_u, v_at):
-        S = cols_ref[i]
-        E = extra[i]
-        hi, mid = split2(jnp.where(rows < 3, S, jnp.where(rows < 6, E, 0.0)))
-        L[i] = jnp.concatenate([hi, mid], axis=0).astype(bf16)
-        full = jnp.where(rows < 6, S, E)
-        hi, mid, lo = split3(full)
-        if want_u:
-            natural = jnp.concatenate(
-                [hi, jnp.where(rows < 6, hi, lo), mid, ones, ones, ones], axis=0
-            ).astype(bf16)
-            U[i] = dot_tt(eye, natural).astype(bf16)
-        if v_at is not None:
-            def swap(value):
-                return jnp.where(
-                    rows < 3, pltpu.roll(value, 5, 0), pltpu.roll(value, 3, 0)
+
+    def swap(value):
+        return jnp.where(rows < 3, pltpu.roll(value, 5, 0), pltpu.roll(value, 3, 0))
+
+    def eight(base, shift, want_u):
+        naturals = []
+        for q in range(8):
+            i = base + q
+            S = cols_ref[i]
+            E = extra[i]
+            hi, mid = split2(jnp.where(rows < 3, S, jnp.where(rows < 6, E, 0.0)))
+            L[i] = jnp.concatenate([hi, mid], axis=0).astype(bf16)
+            hi, mid, lo = split3(jnp.where(rows < 6, S, E))
+            if want_u:
+                naturals.append(
+                    jnp.concatenate(
+                        [hi, jnp.where(rows < 6, hi, lo), mid, ones, ones, ones, zeros, zeros],
+                        axis=0,
+                    ).astype(bf16)
                 )
-
             a0 = hi * ca + c6
             a1 = mid * ca + c6
             b0 = swap(hi) * cb + c7
             b1 = swap(mid) * cb + c7
             A = jnp.concatenate([a0, a1, a0, hi * c6, mid * c6, lo * c6], axis=0)
             B = jnp.concatenate([b0, b1, b0, hi * c7, mid * c7, lo * c7], axis=0)
-            V[v_at, :, 0:128] = A.astype(bf16)
-            V[v_at, :, 128:256] = B.astype(bf16)
-
-    def sweep(low, high, want_u, shift):
-        step = 4
-
-        def body(t, carry):
-            for q in range(step):
-                i = low + t * step + q
-                one(i, want_u, None if shift is None else i + shift)
-            return carry
-
-        lax.fori_loop(0, (high - low) // step, body, 0)
-
-    sweep(0, 96, True, 0)
-    sweep(96, 192, True, None)
-    sweep(192, 384, False, -96)
-
-    for col in range(2):
-        radius = cols_ref[96 * col : 96 * col + 96, 7, :]
-        turned = jnp.concatenate([radius, jnp.zeros((32, 128), f32)], axis=0).T
-
-        def spread(g, carry, turned=turned, col=col):
-            here = pltpu.roll(turned, lax.rem(128 - 8 * g, 128), 1)
-            for c in range(8):
-                RB[96 * col + 8 * g + c] = jnp.broadcast_to(here[:, c : c + 1], (128, 128))
-            return carry
-
-        lax.fori_loop(0, 12, spread, 0)
-
-
-def pair_kernel(lists_ref, cols_ref, moved_ref, own_ref, sides_ref, U, V, L, RB, extra, acc, *rings):
+            V[i + shift, :, 0:128] = A.astype(bf16)
+            V[i + shift, :, 128:256] = B.astype(bf16)
+        if want_u:
+            for half in range(2):
+                four = jnp.concatenate(naturals[4 * half : 4 * half + 4], axis=0)
+                turned = dot_tt(eye, four)
+                for q in range(4):
+                    U[base + 4 * half + q] = turned[:, 64 * q : 64 * q + 48].astype(bf16)
+            radius = cols_ref[pl.ds(base, 8), 7, :].T
+            for q in range(8):
+                RB[base + q] = jnp.broadcast_to(radius[:, q : q + 1], (128, 128))
+
+    def body(t, carry):
+        for col in range(4):
+            dense(96 * col + 8 * t)
+        eight(8 * t, 0, True)
+        eight(96 + 8 * t, 192, True)
+        eight(192 + 8 * t, -96, False)
+        eight(288 + 8 * t, -96, False)
+        return step(step(carry))
+
+    return lax.fori_loop(0, cols_ref.shape[0] // 32, body, start)
+
+
+def shares(counts_ref):
+    total = counts_ref[1:2, :].astype(f32)
+    local = counts_ref[0:1, :].astype(f32)
+    device = iota((128, 128), 0)
+    lanes = iota((128, 128), 1)
+    pick = (lax.shift_right_logical(device, 2) == (lanes & 31)).astype(bf16)
+    mine = (iota((8, 128), 1) & 3) == (iota((8, 128), 0) & 3)
+
+    def laid(value):
+        hi, mid = split2(jnp.where(mine, value, 0.0))
+        return jnp.dot(hi.astype(bf16), pick, preferred_element_type=f32) + jnp.dot(
+            mid.astype(bf16), pick, preferred_element_type=f32
+        )
+
+    local = laid(local)
+    far = (laid(total) - local) * 0.125
+    load = (
+        local
+        + 2.0 * far
+        + 2.0 * pltpu.roll(far, 7, 0)
+        + pltpu.roll(far, 1, 0)
+        + 3.0 * pltpu.roll(far, 1, 1)
+    )
+
+    def step(given):
+        now = load - given + pltpu.roll(given, 1, 1)
+        change = 0.48 * (now - pltpu.roll(now, 127, 1))
+        return jnp.minimum(jnp.maximum(given + change, 0.0), local)
+
+    a = lax.axis_index("gx")
+    b = lax.axis_index("gy")
+    count = lax.axis_size("gx")
+
+    def mask(shift):
+        column = lax.rem(a + shift + count, count)
+        return (iota((8, 128), 1) == column) & (iota((8, 128), 0) == b)
+
+    return jnp.zeros((8, 128), f32), step, mask
+
+
+def pair_kernel(lists_ref, cols_ref, counts_ref, moved_ref, own_ref, sides_ref, U, V, L, RB, extra, acc, *rings):
     AB = rings[0:ring]
     M = rings[ring : 2 * ring]
     moved_ref[...] = cols_ref[0:96]
-    build_tables(cols_ref, U, V, L, RB, extra)
+    given, kept, mask = shares(counts_ref)
+    given = build_tables(cols_ref, U, V, L, RB, extra, given, kept)
+    s_out = jnp.sum(jnp.where(mask(0), given, 0.0)).astype(i32)
+    s_in = jnp.sum(jnp.where(mask(-1), given, 0.0)).astype(i32)
     trash = acc.shape[0] - 1
     acc[...] = jnp.zeros_like(acc)
 
+    def begin(at, name):
+        return lists_ref[at * 1024 + 6 * 128 + name]
+
+    s_out = jnp.minimum(s_out, begin(0, 1))
+    s_in = jnp.minimum(s_in, begin(3, 1))
     ends = []
     shifts = []
     so_far = 0
-    for at in range(4):
-        low = lists_ref[at * 1024 + 6 * 128 + at]
-        high = lists_ref[at * 1024 + 6 * 128 + at + 1]
+    for at, low, high in (
+        (0, s_out, begin(0, 1)),
+        (0, begin(0, 1), begin(0, 2)),
+        (1, begin(1, 2), begin(1, 3)),
+        (2, begin(2, 3), begin(2, 4)),
+        (3, begin(3, 4), begin(3, 5)),
+        (3, 0, s_in),
+    ):
         shifts.append(at * 1024 + low - so_far)
         so_far = so_far + (high - low)
         ends.append(so_far)
-    n = ends[3]
+    n = so_far
     last = jnp.maximum(n - 1, 0)
 
     def entry(k):
         k = jnp.minimum(k, last)
-        shift = jnp.where(
-            k < ends[0],
-            shifts[0],
-            jnp.where(k < ends[1], shifts[1], jnp.where(k < ends[2], shifts[2], shifts[3])),
-        )
+        shift = shifts[5]
+        for at in range(4, -1, -1):
+            shift = jnp.where(k < ends[at], shifts[at], shift)
         code = lists_ref[k + shift]
+        code = code + jnp.where(k < ends[4], 0, 96 + 256 * 288)
         return code & 255, lax.shift_right_logical(code, 8)
 
     def spot(v):
-        return jnp.where(v < 96, v, v + 96)
+        return jnp.where(v < 96, v, jnp.where(v < 288, v + 96, v - 192))
 
     def distances(k, at):
         u, v = entry(k)
@@ -434,7 +503,8 @@
         copy.start()
         copies.append(copy)
 
-    table = jnp.concatenate(split3(table_ref[...]), axis=0).astype(bf16)
+    square = jnp.concatenate([table_ref[:, 16 * a : 16 * a + 16] for a in range(16)], axis=0)
+    table = jnp.concatenate(split3(square), axis=0).astype(bf16)
     sums[...] = jnp.zeros_like(sums)
     sub = iota((16, 128), 0)
 
@@ -470,8 +540,11 @@
 
     lax.fori_loop(0, 12, cells_of, 0)
     total = sums[...]
-    fluid_ref[0] = (total[:, 0:16] + total[:, 16:32] + total[:, 32:48]) / cell_volume
-    fluid_ref[1] = total[:, 48:64] + total[:, 64:80] + total[:, 80:96]
+    solid = (total[:, 0:16] + total[:, 16:32] + total[:, 32:48]) / cell_volume
+    heat = total[:, 48:64] + total[:, 64:80] + total[:, 80:96]
+    for a in range(16):
+        fluid_ref[0:1, 16 * a : 16 * a + 16] = solid[a : a + 1]
+        fluid_ref[1:2, 16 * a : 16 * a + 16] = heat[a : a + 1]
     for copy in copies:
         copy.wait()
 
@@ -511,15 +584,19 @@
     blocks = mine.shape[0]
     count = leaving.shape[2]
     lanes = -(-pairs.shape[3] // 128) * 128
+    every = lax.all_gather(counts.reshape(2, 1), ("gx", "gy"), axis=1, tiled=True)
     cols, lists = pl.pallas_call(
         halo_kernel,
         out_shape=(
             jax.ShapeDtypeStruct((4, blocks, 8, 128), f32),
             jax.ShapeDtypeStruct((4, 8, 128), i32),
         ),
-        in_specs=[smem(), smem(), vmem(), vmem()],
+        in_specs=[pl.BlockSpec(memory_space=pl.ANY)] * 4,
         out_specs=(pl.BlockSpec(memory_space=pl.ANY), vmem()),
         scratch_shapes=[
+            pltpu.SMEM(leaving.shape[2:], i32),
+            pltpu.SMEM(counts.shape[2:], i32),
+            pltpu.VMEM(pairs.shape[2:], i32),
             pltpu.VMEM((count + blocks, 8, 128), f32),
             pltpu.VMEM((count, 8, 128), f32),
             pltpu.VMEM((blocks, 8, 128), f32),
@@ -533,6 +610,7 @@
             pltpu.SemaphoreType.DMA((3,)),
             pltpu.SemaphoreType.DMA((3,)),
             pltpu.SemaphoreType.DMA,
+            pltpu.SemaphoreType.DMA((4,)),
         ],
         compiler_params=pltpu.CompilerParams(
             collective_id=0, has_side_effects=True, vmem_limit_bytes=16 * 2**20
@@ -547,11 +625,11 @@
             jax.ShapeDtypeStruct((blocks, 8, 128), f32),
             jax.ShapeDtypeStruct((3 * blocks // 2, 8, 128), f32),
         ),
-        in_specs=[smem(), vmem()],
+        in_specs=[smem(), vmem(), vmem()],
         out_specs=(vmem(), vmem(), vmem()),
         scratch_shapes=[
             pltpu.VMEM((2 * blocks, 128, 48), bf16),
-            pltpu.VMEM((3 * blocks, 48, 256), bf16),
+            pltpu.VMEM((4 * blocks, 48, 256), bf16),
             pltpu.VMEM((4 * blocks, 16, 128), bf16),
             pltpu.VMEM((2 * blocks, 128, 128), f32),
             pltpu.VMEM((4 * blocks, 8, 128), f32),
@@ -561,13 +639,13 @@
         + [pltpu.VMEM((256, 256), bf16)] * ring,
         compiler_params=pltpu.CompilerParams(vmem_limit_bytes=52 * 2**20),
         name="contact",
-    )(lists.reshape(4096), cols.reshape(4 * blocks, 8, 128))
+    )(lists.reshape(4096), cols.reshape(4 * blocks, 8, 128), every)
 
     rates, fluid = pl.pallas_call(
         finish_kernel,
         out_shape=(
             jax.ShapeDtypeStruct((blocks, 4, 128), f32),
-            jax.ShapeDtypeStruct((2, 16, 16), f32),
+            jax.ShapeDtypeStruct((2, 256), f32),
         ),
         in_specs=[vmem()] * 6,
         out_specs=(vmem(), vmem()),
@@ -589,7 +667,7 @@
         sides.reshape(3, blocks // 2, 8, 128),
         wall_flags[0, 0],
         cell_index[0, 0],
-        fluid_temp.reshape(16, 16),
+        fluid_temp.reshape(1, 256),
     )
     return moved[None, None], rates[None, None], fluid.reshape(1, 1, 2, 256)
 

time: 106 us -> 259 us (2.44)
  the two profiles are of different devices: /device:TPU:3 before, /device:TPU:0 now
where the time goes in v2:
time: 259 us
  blocking collectives  178 us (69%)
  Pallas kernels  73.6 us (28%)
  local copies, waits for them, and re-layouts  6.48 us (3%)
    all_gather x1, blocking collectives, shards(): lax.all_gather(counts.reshape(2, 1), ('gx', 'gy'), axis=1, tiled=True)  178 us
    pallas_call x1, Pallas kernels, shards(): pl.pallas_call(pair_kernel, out_shape=(jax.ShapeDtypeStruct((blocks, 8, 1...  43.5 us
    pallas_call x1, Pallas kernels, shards(): pl.pallas_call(halo_kernel, out_shape=(jax.ShapeDtypeStruct((4, blocks, 8...  19 us
    pallas_call x1, Pallas kernels, shards(): pl.pallas_call(finish_kernel, out_shape=(jax.ShapeDtypeStruct((blocks, 4,...  11.1 us
    unnamed x20, local copies, waits for them, and re-layouts  6.42 us

profile of v2, /device:TPU:0, one launch (start us, length us, event | category | flops | bytes accessed | tf_op | source)
XLA Modules:
  0.0 259.1 jit_solution(1242425391949363304)
XLA Ops:
  0.6 0.0 copy-start.7
  0.6 0.0 copy-start.4
  0.7 0.0 copy-start.3
  0.7 178.3 %all-gather = s32[128,1,2]{2,1,0:T(1,128)S(1)} all-gather(s32[1,1,2]{2,1,0:T(1,128)} %param.10), channel_id=1, replica_groups=mesh['gx'=32,'gy'=4] {'gx','gy'}, dimensions={0}, use_global_device_ids=true | all-gather | bytes 1032 | tf_op jit(solution)/shard_map/all_gather | solution.py:587
  179.0 0.1 copy.11
  179.0 0.0 copy-start.1
  179.0 1.0 copy-done.1
  180.1 0.0 copy-start.5
  180.1 0.7 copy-done.5
  180.8 0.0 copy-start.6
  180.8 0.7 copy-done.6
  181.4 0.0 copy-start.8
  181.4 0.7 copy-done.8
  182.1 19.0 %halo.1 = (f32[4,96,8,128]{3,2,1,0:T(8,128)S(1)}, s32[4,8,128]{2,1,0:T(8,128)S(1)}) custom-call(s32[24]{0:T(128)S(1)} %bitcast.29, s32[2]{0:T(128)S(1)} %bitcast.26, s32[2,576]{1,0:T(2,128)S(1)} %bitcast.24, f32[96,8,128]{2,1,0:T(8,128)S(1)} %bitcast.18), custom_call_target="tpu_custom_call" | custom-call | tf_op jit(solution)/shard_map/halo/pallas_call | solution.py:588
  201.1 0.0 copy-start
  201.1 1.1 copy-done
  202.3 43.5 %contact.1 = (f32[96,8,128]{2,1,0:T(8,128)}, f32[96,8,128]{2,1,0:T(8,128)S(1)}, f32[144,8,128]{2,1,0:T(8,128)S(1)}) custom-call(s32[4096]{0:T(1024)S(1)} %bitcast.23, f32[384,8,128]{2,1,0:T(8,128)} %bitcast.16, s32[2,128]{1,0:T(2,128)S(1)} %bitcast.25), custom_call_target="tpu_custom_call" | custom-call | tf_op jit(solution)/shard_map/contact/pallas_call | solution.py:621
  245.7 0.0 copy-done.7
  245.7 0.0 copy-done.4
  245.7 0.0 copy-done.3
  245.8 0.0 copy-start.2
  245.8 1.0 copy-done.2
  246.8 11.1 %finish.1 = (f32[96,4,128]{2,1,0:T(4,128)S(1)}, f32[2,256]{1,0:T(2,128)S(1)}) custom-call(f32[96,8,128]{2,1,0:T(8,128)S(1)} %copy-done.2, f32[96,8,128]{2,1,0:T(8,128)S(1)} %get-tuple-element.13.own_ref, f32[3,48,8,128]{3,2,1,0:T(8,128)S(1)} %bitcast.17, s32[96,128]{1,0:T(8,128)S(1)} %bitcast.21, s32[96,128]{1,0:T(8,128)S(1)} %bitcast.22, f32[1,256]{1,0:T(1,128)S(1)} %bitcast.28), custom_call_target="tpu_custom_call" | custom-call | tf_op jit(solution)/shard_map/finish/pallas_call | solution.py:644
  257.9 0.7 copy.14
  258.6 0.6 copy.15
Async XLA Ops:
  0.6 245.1 %copy-start.7 = (f32[1,1,256]{2,1,0:T(1,128)S(1)}, f32[1,1,256]{2,1,0:T(1,128)}, u32[]{:S(2)}) copy-start(f32[1,1,256]{2,1,0:T(1,128)} %param.13) | copy-start | bytes 3076
  0.6 245.1 %copy-start.4 = (s32[1,1,96,128]{3,2,1,0:T(8,128)S(1)}, s32[1,1,96,128]{3,2,1,0:T(8,128)}, u32[]{:S(2)}) copy-start(s32[1,1,96,128]{3,2,1,0:T(8,128)} %param.12) | copy-start | bytes 147460
  0.7 245.1 %copy-start.3 = (s32[1,1,96,128]{3,2,1,0:T(8,128)S(1)}, s32[1,1,96,128]{3,2,1,0:T(8,128)}, u32[]{:S(2)}) copy-start(s32[1,1,96,128]{3,2,1,0:T(8,128)} %param.11) | copy-start | bytes 147460
  179.0 1.0 copy-start.1
  180.1 0.7 copy-start.5
  180.8 0.7 copy-start.6
  181.4 0.7 copy-start.8
  201.1 1.2 copy-start
  245.8 1.0 copy-start.2

commit v3 on v2

--- a/solution.py
+++ b/solution.py
@@ -23,10 +23,12 @@
 i32 = jnp.int32
 
 tiny = 1e-30
-group = 12
+group = 16
 lag_a = 2
 lag_b = 2
 ring = lag_a + lag_b
+reach = 4
+vmem_grant = 56 * 2**20
 MESH = pl.DeviceIdType.MESH
 
 
@@ -120,6 +122,7 @@
     state_hbm,
     cols_ref,
     lists_ref,
+    wide_ref,
     leaving_ref,
     counts_ref,
     pairs_ref,
@@ -137,6 +140,11 @@
     col_recv,
     local_sem,
     in_sem,
+    near,
+    near_send,
+    near_recv,
+    wide_send,
+    wide_recv,
 ):
     blocks = state_hbm.shape[0]
     count = leaving_hbm.shape[0]
@@ -155,11 +163,32 @@
     ]
     for copy in inputs:
         copy.start()
-    inputs[0].wait()
-    inputs[1].wait()
+    a = lax.axis_index("gx")
+    na = lax.axis_size("gx")
+    along = {
+        step: {"gx": lax.rem(a + step + na, na)} for step in range(-reach, reach + 1) if step
+    }
+    wide_ref[...] = jnp.zeros_like(wide_ref)
+    for copy in inputs:
+        copy.wait()
+    local = counts_ref[0].astype(f32)
+    far = (counts_ref[1] - counts_ref[0]).astype(f32) * 0.125
+    near[0:1, :] = jnp.full((1, 128), far)
     for m in range(count):
         dep[m] = state_ref[leaving_ref[m]]
-    greet((ahead, behind, up, down))
+    greet((up, down, *along.values()))
+    asks = []
+    for at, device in ((1, down), (2, up), (3, ahead)):
+        copy = pltpu.make_async_remote_copy(
+            src_ref=near.at[0:1],
+            dst_ref=near.at[at : at + 1],
+            send_sem=near_send.at[at - 1],
+            recv_sem=near_recv.at[at - 1],
+            device_id=device,
+            device_id_type=MESH,
+        )
+        copy.start()
+        asks.append(copy)
     depart = pltpu.make_async_remote_copy(
         src_ref=dep,
         dst_ref=cat.at[0:count],
@@ -176,8 +205,6 @@
     slot_vec[...] = slot
     to_smem = pltpu.make_async_copy(slot_vec, slot_smem, local_sem)
     to_smem.start()
-    inputs[2].wait()
-    inputs[3].wait()
     lanes = pad.shape[1]
     pad[...] = jnp.zeros_like(pad)
     pad[0:2, 0 : pairs_ref.shape[1]] = pairs_ref[...]
@@ -198,6 +225,21 @@
         )
         copy.start()
         copies.append(copy)
+    for copy in asks:
+        copy.wait()
+    load = local + 2.0 * far + 2.0 * near[1:2, :] + near[2:3, :] + 3.0 * near[3:4, :]
+    wide_ref[reach : reach + 1, :] = jnp.where(iota((1, 128), 1) < 64, load, local)
+    for at, step in enumerate(along):
+        copy = pltpu.make_async_remote_copy(
+            src_ref=wide_ref.at[reach : reach + 1],
+            dst_ref=wide_ref.at[reach - step : reach - step + 1],
+            send_sem=wide_send.at[at],
+            recv_sem=wide_recv.at[at],
+            device_id=along[step],
+            device_id_type=MESH,
+        )
+        copy.start()
+        copies.append(copy)
     to_smem.wait()
     depart.wait()
 
@@ -224,126 +266,143 @@
         copy.wait()
 
 
-def build_tables(cols_ref, U, V, L, RB, extra, start, step):
+def build_tables(cols_ref, U, V, L, RT, extra, pieces, start, step):
     rows = iota((8, 128), 0)
     eye = (iota((128, 128), 0) == iota((128, 128), 1)).astype(bf16)
     c6 = jnp.where(rows == 6, 1.0, 0.0)
     c7 = jnp.where(rows == 7, 0.25, 0.0)
     ca = jnp.where(rows < 3, -2.0, 0.0)
     cb = jnp.where(rows < 6, -0.25, 0.0)
-    ones = jnp.where(rows >= 6, 1.0, 0.0)
-    zeros = jnp.zeros((8, 128), f32)
+    ones = jnp.where(rows < 6, 1.0, 0.0)
 
     def dense(base):
         at = pl.ds(base, 8)
         x = [cols_ref[at, c, :] for c in range(3)]
         v = [cols_ref[at, c, :] for c in range(3, 6)]
-        root = jnp.sqrt(cols_ref[at, 7, :])
+        radius = cols_ref[at, 7, :]
+        root = jnp.sqrt(radius)
+        square = x[0] * x[0] + x[1] * x[1] + x[2] * x[2] + 0.5 * soften
+        dot = x[0] * v[0] + x[1] * v[1] + x[2] * v[2]
         extra[at, 3, :] = jnp.ones((8, 128), f32)
         extra[at, 4, :] = root * cols_ref[at, 6, :]
         extra[at, 5, :] = root
-        extra[at, 6, :] = x[0] * x[0] + x[1] * x[1] + x[2] * x[2] + 0.5 * soften
-        extra[at, 7, :] = x[0] * v[0] + x[1] * v[1] + x[2] * v[2]
+        extra[at, 6, :] = square
+        extra[at, 7, :] = dot
+        for c, piece in enumerate(split3(square) + split3(0.25 * dot)):
+            pieces[at, c, :] = piece
+        return radius
 
     def swap(value):
         return jnp.where(rows < 3, pltpu.roll(value, 5, 0), pltpu.roll(value, 3, 0))
 
-    def eight(base, shift, want_u):
+    def eight(base, shift, want_u, radius):
         naturals = []
         for q in range(8):
             i = base + q
             S = cols_ref[i]
             E = extra[i]
+            G = pieces[i]
             hi, mid = split2(jnp.where(rows < 3, S, jnp.where(rows < 6, E, 0.0)))
             L[i] = jnp.concatenate([hi, mid], axis=0).astype(bf16)
-            hi, mid, lo = split3(jnp.where(rows < 6, S, E))
+            full = jnp.where(rows < 6, S, E)
+            hi, mid = split2(full)
             if want_u:
-                naturals.append(
-                    jnp.concatenate(
-                        [hi, jnp.where(rows < 6, hi, lo), mid, ones, ones, ones, zeros, zeros],
-                        axis=0,
-                    ).astype(bf16)
-                )
+                low = jnp.where(rows < 6, hi, full - hi - mid)
+                naturals.append(jnp.concatenate([hi, low, mid, ones], axis=0).astype(bf16))
             a0 = hi * ca + c6
             a1 = mid * ca + c6
             b0 = swap(hi) * cb + c7
             b1 = swap(mid) * cb + c7
-            A = jnp.concatenate([a0, a1, a0, hi * c6, mid * c6, lo * c6], axis=0)
-            B = jnp.concatenate([b0, b1, b0, hi * c7, mid * c7, lo * c7], axis=0)
+            A = jnp.concatenate([a0, a1, a0, jnp.where(rows < 3, G, 0.0)], axis=0)
+            B = jnp.concatenate(
+                [b0, b1, b0, jnp.where((rows >= 3) & (rows < 6), G, 0.0)], axis=0
+            )
             V[i + shift, :, 0:128] = A.astype(bf16)
             V[i + shift, :, 128:256] = B.astype(bf16)
         if want_u:
-            for half in range(2):
-                four = jnp.concatenate(naturals[4 * half : 4 * half + 4], axis=0)
-                turned = dot_tt(eye, four)
-                for q in range(4):
-                    U[base + 4 * half + q] = turned[:, 64 * q : 64 * q + 48].astype(bf16)
-            radius = cols_ref[pl.ds(base, 8), 7, :].T
+            turned = dot_tt(eye, jnp.concatenate(naturals, axis=0))
             for q in range(8):
-                RB[base + q] = jnp.broadcast_to(radius[:, q : q + 1], (128, 128))
+                U[base + q] = turned[:, 32 * q : 32 * q + 32].astype(bf16)
+            RT[lax.shift_right_logical(base, 3), :, 0:8] = radius.T
 
     def body(t, carry):
-        for col in range(4):
-            dense(96 * col + 8 * t)
-        eight(8 * t, 0, True)
-        eight(96 + 8 * t, 192, True)
-        eight(192 + 8 * t, -96, False)
-        eight(288 + 8 * t, -96, False)
+        radius = [dense(96 * col + 8 * t) for col in range(4)]
+        eight(8 * t, 0, True, radius[0])
+        eight(96 + 8 * t, 192, True, radius[1])
+        eight(192 + 8 * t, -96, False, None)
+        eight(288 + 8 * t, -96, False, None)
         return step(step(carry))
 
     return lax.fori_loop(0, cols_ref.shape[0] // 32, body, start)
 
 
-def shares(counts_ref):
-    total = counts_ref[1:2, :].astype(f32)
-    local = counts_ref[0:1, :].astype(f32)
-    device = iota((128, 128), 0)
-    lanes = iota((128, 128), 1)
-    pick = (lax.shift_right_logical(device, 2) == (lanes & 31)).astype(bf16)
-    mine = (iota((8, 128), 1) & 3) == (iota((8, 128), 0) & 3)
-
-    def laid(value):
-        hi, mid = split2(jnp.where(mine, value, 0.0))
-        return jnp.dot(hi.astype(bf16), pick, preferred_element_type=f32) + jnp.dot(
-            mid.astype(bf16), pick, preferred_element_type=f32
-        )
-
-    local = laid(local)
-    far = (laid(total) - local) * 0.125
-    load = (
-        local
-        + 2.0 * far
-        + 2.0 * pltpu.roll(far, 7, 0)
-        + pltpu.roll(far, 1, 0)
-        + 3.0 * pltpu.roll(far, 1, 1)
-    )
+def shares(wide):
+    rows = iota((8, 128), 0)
+
+    def chain(load):
+        local = jnp.where(rows < 7, pltpu.roll(load, 64, 1), 0.0)
+
+        def step(given):
+            now = load - given + pltpu.roll(given, 1, 0)
+            change = 0.48 * (now - pltpu.roll(now, 7, 0))
+            return jnp.minimum(jnp.maximum(given + change, 0.0), local)
+
+        return step
+
+    own = chain(wide[1:9, :])
+    behind = chain(wide[0:8, :])
 
     def step(given):
-        now = load - given + pltpu.roll(given, 1, 1)
-        change = 0.48 * (now - pltpu.roll(now, 127, 1))
-        return jnp.minimum(jnp.maximum(given + change, 0.0), local)
-
-    a = lax.axis_index("gx")
-    b = lax.axis_index("gy")
-    count = lax.axis_size("gx")
-
-    def mask(shift):
-        column = lax.rem(a + shift + count, count)
-        return (iota((8, 128), 1) == column) & (iota((8, 128), 0) == b)
-
-    return jnp.zeros((8, 128), f32), step, mask
-
-
-def pair_kernel(lists_ref, cols_ref, counts_ref, moved_ref, own_ref, sides_ref, U, V, L, RB, extra, acc, *rings):
+        return own(given[0]), behind(given[1])
+
+    def value(given):
+        picked = (rows == reach - 1) & (iota((8, 128), 1) == 0)
+        return jnp.sum(jnp.where(picked, given, 0.0)).astype(i32)
+
+    start = jnp.zeros((8, 128), f32)
+    return (start, start), step, value
+
+
+def pair_kernel(
+    lists_hbm,
+    cols_hbm,
+    wide_hbm,
+    moved_ref,
+    own_ref,
+    sides_ref,
+    lists_ref,
+    cols_ref,
+    wide,
+    U,
+    V,
+    L,
+    RT,
+    extra,
+    pieces,
+    acc,
+    sem,
+    *rings,
+):
     AB = rings[0:ring]
     M = rings[ring : 2 * ring]
-    moved_ref[...] = cols_ref[0:96]
-    given, kept, mask = shares(counts_ref)
-    given = build_tables(cols_ref, U, V, L, RB, extra, given, kept)
-    s_out = jnp.sum(jnp.where(mask(0), given, 0.0)).astype(i32)
-    s_in = jnp.sum(jnp.where(mask(-1), given, 0.0)).astype(i32)
+    copies = [
+        pltpu.make_async_copy(source, target, sem.at[at])
+        for at, (source, target) in enumerate(
+            ((cols_hbm, cols_ref), (lists_hbm, lists_ref), (wide_hbm, wide))
+        )
+    ]
+    for copy in copies:
+        copy.start()
     trash = acc.shape[0] - 1
     acc[...] = jnp.zeros_like(acc)
+    for copy in copies:
+        copy.wait()
+    keep = pltpu.make_async_copy(cols_ref.at[0:96], moved_ref, sem.at[3])
+    keep.start()
+    given, step, value = shares(wide)
+    given = build_tables(cols_ref, U, V, L, RT, extra, pieces, given, step)
+    s_out = value(given[0])
+    s_in = value(given[1])
 
     def begin(at, name):
         return lists_ref[at * 1024 + 6 * 128 + name]
@@ -386,10 +445,16 @@
     def weights(k, at):
         u, v = entry(k)
         rt = cols_ref[spot(v), 7:8, :]
+        lane = jnp.full((8, 128), u & 7, i32)
+        eighth = lax.shift_right_logical(u, 3)
+
+        def radius(r):
+            return jnp.take_along_axis(RT[eighth, r : r + 8, :], lane, axis=1)
+
         for r in range(0, 128, 16):
             A = AB[at][r : r + 16, 0:128]
             B = AB[at][r : r + 16, 128:256]
-            R = RB[u, r : r + 16, :] + rt
+            R = jnp.concatenate([radius(r), radius(r + 8)], axis=0) + rt
             inv = lax.rsqrt(A)
             gap = R - A * inv
             inter = jnp.maximum(gap, 0.0)
@@ -445,42 +510,43 @@
 
     lax.fori_loop(0, lax.div(n + group - 1, group), turn, 0)
 
-    def result(i):
-        S = cols_ref[i]
-        got = acc[i]
-        hi, mid = split2(S)
-        force = stiffness * ((hi + mid) * got[3:4] - got)
-        heat = conductance * jnp.sqrt(S[7:8]) * (got[4:5] - S[6:7] * got[5:6])
-        return jnp.where(rows < 3, force, jnp.where(rows == 3, heat, 0.0))
-
-    def close(t, carry):
-        for q in range(4):
-            i = t * 4 + q
-            own_ref[i] = result(i)
+    def close(base, out_ref, out_base):
+        at = pl.ds(base, 8)
+        got = [acc[at, c, :] for c in range(6)]
+        terms = []
+        for c in range(3):
+            hi, mid = split2(cols_ref[at, c, :])
+            terms.append(stiffness * ((hi + mid) * got[3] - got[c]))
+        root = conductance * extra[at, 5, :]
+        terms.append(root * (got[4] - cols_ref[at, 6, :] * got[5]))
+        for c in range(4):
+            out_ref[pl.ds(out_base + c, 8, 4), :] = terms[c]
+
+    def close_all(t, carry):
+        close(8 * t, own_ref, 32 * t)
+        for side in range(3):
+            close(96 * (side + 1) + 8 * t, sides_ref, 384 * side + 32 * t)
         return carry
 
-    lax.fori_loop(0, 24, close, 0)
-
-    def close_far(t, carry):
-        for q in range(4):
-            i = t * 4 + q
-            lower = result(96 + 2 * i)
-            upper = result(97 + 2 * i)
-            sides_ref[i] = jnp.where(rows < 4, lower, pltpu.roll(upper, 4, 0))
-        return carry
-
-    lax.fori_loop(0, 36, close_far, 0)
+    lax.fori_loop(0, 12, close_all, 0)
+    keep.wait()
 
 
 def finish_kernel(
+    moved_hbm,
+    own_hbm,
+    sides_ref,
+    flags_hbm,
+    cells_hbm,
+    table_hbm,
+    rates_ref,
+    fluid_ref,
     moved_ref,
     own_ref,
-    sides_ref,
     flags_ref,
     cells_ref,
     table_ref,
-    rates_ref,
-    fluid_ref,
+    in_sem,
     got,
     heat_in,
     to_fluid,
@@ -489,11 +555,26 @@
     recv,
 ):
     ahead, behind, up, down = neighbours()
+    inputs = [
+        pltpu.make_async_copy(source, target, in_sem.at[at])
+        for at, (source, target) in enumerate(
+            (
+                (moved_hbm, moved_ref),
+                (flags_hbm, flags_ref),
+                (cells_hbm, cells_ref),
+                (table_hbm, table_ref),
+                (own_hbm, own_ref),
+            )
+        )
+    ]
+    for copy in inputs:
+        copy.start()
     greet((ahead, behind, up, down))
     copies = []
+    span = got.shape[1]
     for at, device in ((0, behind), (1, up), (2, down)):
         copy = pltpu.make_async_remote_copy(
-            src_ref=sides_ref.at[at],
+            src_ref=sides_ref.at[span * at : span * at + span],
             dst_ref=got.at[at],
             send_sem=send.at[at],
             recv_sem=recv.at[at],
@@ -503,6 +584,8 @@
         copy.start()
         copies.append(copy)
 
+    for copy in inputs:
+        copy.wait()
     square = jnp.concatenate([table_ref[:, 16 * a : 16 * a + 16] for a in range(16)], axis=0)
     table = jnp.concatenate(split3(square), axis=0).astype(bf16)
     sums[...] = jnp.zeros_like(sums)
@@ -553,13 +636,11 @@
         radius = moved_ref[at, 7, :]
         volume = 4.0 / 3.0 * math.pi * radius * radius * radius
         inverse = 1.0 / volume
-        half = pl.ds(g * 4, 4)
         for c in range(4):
-            near = own_ref[at, c, :]
-            even = got[0, half, c, :] + got[1, half, c, :] + got[2, half, c, :]
-            odd = got[0, half, c + 4, :] + got[1, half, c + 4, :] + got[2, half, c + 4, :]
-            far = jnp.stack([even, odd], axis=1).reshape(8, 128)
-            value = near + far
+            here = pl.ds(g * 32 + c, 8, 4)
+            value = own_ref[here, :]
+            for side in range(3):
+                value = value + got[side, here, :]
             if c == 3:
                 value = value + heat_in[at, :]
             value = value * inverse
@@ -571,12 +652,12 @@
     lax.fori_loop(0, 12, combine, 0)
 
 
+def anywhere():
+    return pl.BlockSpec(memory_space=pl.ANY)
+
+
 def vmem():
     return pl.BlockSpec(memory_space=pltpu.VMEM)
-
-
-def smem():
-    return pl.BlockSpec(memory_space=pltpu.SMEM)
 
 
 def shards(state, leaving, pairs, counts, wall_flags, cell_index, fluid_temp):
@@ -584,15 +665,15 @@
     blocks = mine.shape[0]
     count = leaving.shape[2]
     lanes = -(-pairs.shape[3] // 128) * 128
-    every = lax.all_gather(counts.reshape(2, 1), ("gx", "gy"), axis=1, tiled=True)
-    cols, lists = pl.pallas_call(
+    cols, lists, wide = pl.pallas_call(
         halo_kernel,
         out_shape=(
             jax.ShapeDtypeStruct((4, blocks, 8, 128), f32),
             jax.ShapeDtypeStruct((4, 8, 128), i32),
+            jax.ShapeDtypeStruct((16, 128), f32),
         ),
-        in_specs=[pl.BlockSpec(memory_space=pl.ANY)] * 4,
-        out_specs=(pl.BlockSpec(memory_space=pl.ANY), vmem()),
+        in_specs=[anywhere()] * 4,
+        out_specs=(anywhere(), vmem(), vmem()),
         scratch_shapes=[
             pltpu.SMEM(leaving.shape[2:], i32),
             pltpu.SMEM(counts.shape[2:], i32),
@@ -611,9 +692,14 @@
             pltpu.SemaphoreType.DMA((3,)),
             pltpu.SemaphoreType.DMA,
             pltpu.SemaphoreType.DMA((4,)),
+            pltpu.VMEM((8, 128), f32),
+            pltpu.SemaphoreType.DMA((3,)),
+            pltpu.SemaphoreType.DMA((3,)),
+            pltpu.SemaphoreType.DMA((2 * reach,)),
+            pltpu.SemaphoreType.DMA((2 * reach,)),
         ],
         compiler_params=pltpu.CompilerParams(
-            collective_id=0, has_side_effects=True, vmem_limit_bytes=16 * 2**20
+            collective_id=0, has_side_effects=True, vmem_limit_bytes=vmem_grant
         ),
         name="halo",
     )(leaving[0, 0], counts[0, 0], pairs[0, 0], mine)
@@ -622,24 +708,29 @@
         pair_kernel,
         out_shape=(
             jax.ShapeDtypeStruct((blocks, 8, 128), f32),
-            jax.ShapeDtypeStruct((blocks, 8, 128), f32),
-            jax.ShapeDtypeStruct((3 * blocks // 2, 8, 128), f32),
+            jax.ShapeDtypeStruct((4 * blocks, 128), f32),
+            jax.ShapeDtypeStruct((12 * blocks, 128), f32),
         ),
-        in_specs=[smem(), vmem(), vmem()],
-        out_specs=(vmem(), vmem(), vmem()),
+        in_specs=[anywhere()] * 3,
+        out_specs=(anywhere(), vmem(), vmem()),
         scratch_shapes=[
-            pltpu.VMEM((2 * blocks, 128, 48), bf16),
-            pltpu.VMEM((4 * blocks, 48, 256), bf16),
+            pltpu.SMEM((4096,), i32),
+            pltpu.VMEM((4 * blocks, 8, 128), f32),
+            pltpu.VMEM((16, 128), f32),
+            pltpu.VMEM((2 * blocks, 128, 32), bf16),
+            pltpu.VMEM((4 * blocks, 32, 256), bf16),
             pltpu.VMEM((4 * blocks, 16, 128), bf16),
-            pltpu.VMEM((2 * blocks, 128, 128), f32),
+            pltpu.VMEM((blocks // 4, 128, 128), f32),
+            pltpu.VMEM((4 * blocks, 8, 128), f32),
             pltpu.VMEM((4 * blocks, 8, 128), f32),
             pltpu.VMEM((4 * blocks + 1, 8, 128), f32),
+            pltpu.SemaphoreType.DMA((4,)),
         ]
         + [pltpu.VMEM((128, 256), f32)] * ring
         + [pltpu.VMEM((256, 256), bf16)] * ring,
-        compiler_params=pltpu.CompilerParams(vmem_limit_bytes=52 * 2**20),
+        compiler_params=pltpu.CompilerParams(vmem_limit_bytes=vmem_grant),
         name="contact",
-    )(lists.reshape(4096), cols.reshape(4 * blocks, 8, 128), every)
+    )(lists.reshape(4096), cols.reshape(4 * blocks, 8, 128), wide)
 
     rates, fluid = pl.pallas_call(
         finish_kernel,
@@ -647,10 +738,16 @@
             jax.ShapeDtypeStruct((blocks, 4, 128), f32),
             jax.ShapeDtypeStruct((2, 256), f32),
         ),
-        in_specs=[vmem()] * 6,
+        in_specs=[anywhere()] * 6,
         out_specs=(vmem(), vmem()),
         scratch_shapes=[
-            pltpu.VMEM((3, blocks // 2, 8, 128), f32),
+            pltpu.VMEM((blocks, 8, 128), f32),
+            pltpu.VMEM((4 * blocks, 128), f32),
+            pltpu.VMEM((blocks, 128), i32),
+            pltpu.VMEM((blocks, 128), i32),
+            pltpu.VMEM((1, 256), f32),
+            pltpu.SemaphoreType.DMA((5,)),
+            pltpu.VMEM((3, 4 * blocks, 128), f32),
             pltpu.VMEM((blocks, 128), f32),
             pltpu.VMEM((blocks, 128), f32),
             pltpu.VMEM((16, 96), f32),
@@ -658,13 +755,13 @@
             pltpu.SemaphoreType.DMA((3,)),
         ],
         compiler_params=pltpu.CompilerParams(
-            collective_id=1, has_side_effects=True, vmem_limit_bytes=16 * 2**20
+            collective_id=1, has_side_effects=True, vmem_limit_bytes=vmem_grant
         ),
         name="finish",
     )(
         moved,
         own,
-        sides.reshape(3, blocks // 2, 8, 128),
+        sides,
         wall_flags[0, 0],
         cell_index[0, 0],
         fluid_temp.reshape(1, 256),

time: 259 us -> 91.4 us (0.35)
  the two profiles are of different devices: /device:TPU:0 before, /device:TPU:11 now
where the time goes in v3:
time: 91.4 us; the launch traced here: 91.2 us
  Pallas kernels  87.7 us (96%)
  local copies, waits for them, and re-layouts  2.86 us (3%)
    pallas_call x1, Pallas kernels, shards(): pl.pallas_call(pair_kernel, out_shape=(jax.ShapeDtypeStruct((blocks, 8, 1...  44.3 us
    pallas_call x1, Pallas kernels, shards(): pl.pallas_call(halo_kernel, out_shape=(jax.ShapeDtypeStruct((4, blocks, 8...  22.9 us
    pallas_call x1, Pallas kernels, shards(): pl.pallas_call(finish_kernel, out_shape=(jax.ShapeDtypeStruct((blocks, 4,...  20.4 us
    unnamed x2, local copies, waits for them, and re-layouts  2.86 us

profile of v3, /device:TPU:11, one launch (start us, length us, event | category | flops | bytes accessed | tf_op | source)
XLA Modules:
  0.0 91.2 jit_solution(10855118567601571434)
XLA Ops:
  0.6 22.9 %halo.1 = (f32[4,96,8,128]{3,2,1,0:T(8,128)}, s32[4,8,128]{2,1,0:T(8,128)}, f32[16,128]{1,0:T(8,128)}) custom-call(s32[24]{0:T(128)} %bitcast.22, s32[2]{0:T(128)} %bitcast.23, s32[2,576]{1,0:T(2,128)} %bitcast.19, f32[96,8,128]{2,1,0:T(8,128)} %bitcast.13), custom_call_target="tpu_custom_call" | custom-call | tf_op jit(solution)/shard_map/halo/pallas_call | solution.py:668
  23.6 44.3 %contact.1 = (f32[96,8,128]{2,1,0:T(8,128)}, f32[384,128]{1,0:T(8,128)}, f32[1152,128]{1,0:T(8,128)}) custom-call(s32[4096]{0:T(1024)} %bitcast.18, f32[384,8,128]{2,1,0:T(8,128)} %bitcast.12, f32[16,128]{1,0:T(8,128)} %get-tuple-element.13.wide_hbm), custom_call_target="tpu_custom_call" | custom-call | tf_op jit(solution)/shard_map/contact/pallas_call | solution.py:707
  67.9 20.4 %finish.1 = (f32[96,4,128]{2,1,0:T(4,128)}, f32[2,256]{1,0:T(2,128)}) custom-call(f32[96,8,128]{2,1,0:T(8,128)} %get-tuple-element.14.moved_hbm, f32[384,128]{1,0:T(8,128)} %get-tuple-element.15.own_hbm, f32[1152,128]{1,0:T(8,128)} %get-tuple-element.16.sides_ref, s32[96,128]{1,0:T(8,128)} %bitcast.16, s32[96,128]{1,0:T(8,128)} %bitcast.17, f32[1,256]{1,0:T(1,128)} %bitcast.21), custom_call_target="tpu_custom_call" | custom-call | tf_op jit(solution)/shard_map/finish/pallas_call | solution.py:735
  88.3 1.6 %copy.12 = f32[1,1,96,4,128]{4,3,2,1,0:T(4,128)} copy(f32[1,1,96,4,128]{4,3,2,1,0:T(4,128)} %bitcast.15) | data formatting | bytes 393216
  90.0 1.2 %copy.13 = f32[1,1,2,256]{3,2,1,0:T(2,128)} copy(f32[1,1,2,256]{3,2,1,0:T(2,128)} %bitcast.20) | data formatting | bytes 4096

commit v4 on v3

--- a/solution.py
+++ b/solution.py
@@ -266,6 +266,14 @@
         copy.wait()
 
 
+def rows_of(base, c):
+    return pl.ds(base * 8 + c, 8, 8)
+
+
+def tile(i):
+    return pl.ds(pl.multiple_of(i * 8, 8), 8)
+
+
 def build_tables(cols_ref, U, V, L, RT, extra, pieces, start, step):
     rows = iota((8, 128), 0)
     eye = (iota((128, 128), 0) == iota((128, 128), 1)).astype(bf16)
@@ -276,20 +284,19 @@
     ones = jnp.where(rows < 6, 1.0, 0.0)
 
     def dense(base):
-        at = pl.ds(base, 8)
-        x = [cols_ref[at, c, :] for c in range(3)]
-        v = [cols_ref[at, c, :] for c in range(3, 6)]
-        radius = cols_ref[at, 7, :]
+        x = [cols_ref[rows_of(base, c), :] for c in range(3)]
+        v = [cols_ref[rows_of(base, c), :] for c in range(3, 6)]
+        radius = cols_ref[rows_of(base, 7), :]
         root = jnp.sqrt(radius)
         square = x[0] * x[0] + x[1] * x[1] + x[2] * x[2] + 0.5 * soften
         dot = x[0] * v[0] + x[1] * v[1] + x[2] * v[2]
-        extra[at, 3, :] = jnp.ones((8, 128), f32)
-        extra[at, 4, :] = root * cols_ref[at, 6, :]
-        extra[at, 5, :] = root
-        extra[at, 6, :] = square
-        extra[at, 7, :] = dot
+        extra[rows_of(base, 3), :] = jnp.ones((8, 128), f32)
+        extra[rows_of(base, 4), :] = root * cols_ref[rows_of(base, 6), :]
+        extra[rows_of(base, 5), :] = root
+        extra[rows_of(base, 6), :] = square
+        extra[rows_of(base, 7), :] = dot
         for c, piece in enumerate(split3(square) + split3(0.25 * dot)):
-            pieces[at, c, :] = piece
+            pieces[rows_of(base, c), :] = piece
         return radius
 
     def swap(value):
@@ -299,9 +306,9 @@
         naturals = []
         for q in range(8):
             i = base + q
-            S = cols_ref[i]
-            E = extra[i]
-            G = pieces[i]
+            S = cols_ref[tile(i), :]
+            E = extra[tile(i), :]
+            G = pieces[tile(i), :]
             hi, mid = split2(jnp.where(rows < 3, S, jnp.where(rows < 6, E, 0.0)))
             L[i] = jnp.concatenate([hi, mid], axis=0).astype(bf16)
             full = jnp.where(rows < 6, S, E)
@@ -333,7 +340,7 @@
         eight(288 + 8 * t, -96, False, None)
         return step(step(carry))
 
-    return lax.fori_loop(0, cols_ref.shape[0] // 32, body, start)
+    return lax.fori_loop(0, cols_ref.shape[0] // 256, body, start)
 
 
 def shares(wide):
@@ -393,11 +400,11 @@
     ]
     for copy in copies:
         copy.start()
-    trash = acc.shape[0] - 1
+    trash = acc.shape[0] // 8 - 1
     acc[...] = jnp.zeros_like(acc)
     for copy in copies:
         copy.wait()
-    keep = pltpu.make_async_copy(cols_ref.at[0:96], moved_ref, sem.at[3])
+    keep = pltpu.make_async_copy(cols_ref.at[0:768], moved_ref, sem.at[3])
     keep.start()
     given, step, value = shares(wide)
     given = build_tables(cols_ref, U, V, L, RT, extra, pieces, given, step)
@@ -444,7 +451,7 @@
 
     def weights(k, at):
         u, v = entry(k)
-        rt = cols_ref[spot(v), 7:8, :]
+        rt = cols_ref[pl.ds(spot(v) * 8 + 7, 1), :]
         lane = jnp.full((8, 128), u & 7, i32)
         eighth = lax.shift_right_logical(u, 3)
 
@@ -492,8 +499,8 @@
         live = k < n
         u = jnp.where(live, u, trash)
         w = jnp.where(live, w, trash)
-        acc[u] += to_first
-        acc[w] += to_second
+        acc[tile(u), :] += to_first
+        acc[tile(w), :] += to_second
 
     for q in range(ring):
         distances(q, q)
@@ -511,14 +518,13 @@
     lax.fori_loop(0, lax.div(n + group - 1, group), turn, 0)
 
     def close(base, out_ref, out_base):
-        at = pl.ds(base, 8)
-        got = [acc[at, c, :] for c in range(6)]
+        got = [acc[rows_of(base, c), :] for c in range(6)]
         terms = []
         for c in range(3):
-            hi, mid = split2(cols_ref[at, c, :])
+            hi, mid = split2(cols_ref[rows_of(base, c), :])
             terms.append(stiffness * ((hi + mid) * got[3] - got[c]))
-        root = conductance * extra[at, 5, :]
-        terms.append(root * (got[4] - cols_ref[at, 6, :] * got[5]))
+        root = conductance * extra[rows_of(base, 5), :]
+        terms.append(root * (got[4] - cols_ref[rows_of(base, 6), :] * got[5]))
         for c in range(4):
             out_ref[pl.ds(out_base + c, 8, 4), :] = terms[c]
 
@@ -592,9 +598,9 @@
     sub = iota((16, 128), 0)
 
     def cells_of(g, carry):
-        at = pl.ds(g * 8, 8)
-        temper = moved_ref[at, 6, :]
-        radius = moved_ref[at, 7, :]
+        at = pl.ds(pl.multiple_of(g * 8, 8), 8)
+        temper = moved_ref[rows_of(g * 8, 6), :]
+        radius = moved_ref[rows_of(g * 8, 7), :]
         volume = 4.0 / 3.0 * math.pi * radius * radius * radius
         cell = cells_ref[at, :]
         high = lax.shift_right_logical(cell, 4)
@@ -632,8 +638,8 @@
         copy.wait()
 
     def combine(g, carry):
-        at = pl.ds(g * 8, 8)
-        radius = moved_ref[at, 7, :]
+        at = pl.ds(pl.multiple_of(g * 8, 8), 8)
+        radius = moved_ref[rows_of(g * 8, 7), :]
         volume = 4.0 / 3.0 * math.pi * radius * radius * radius
         inverse = 1.0 / volume
         for c in range(4):
@@ -646,7 +652,7 @@
             value = value * inverse
             if c == 2:
                 value = value - gravity
-            rates_ref[at, c, :] = value
+            rates_ref[here, :] = value
         return carry
 
     lax.fori_loop(0, 12, combine, 0)
@@ -707,7 +713,7 @@
     moved, own, sides = pl.pallas_call(
         pair_kernel,
         out_shape=(
-            jax.ShapeDtypeStruct((blocks, 8, 128), f32),
+            jax.ShapeDtypeStruct((8 * blocks, 128), f32),
             jax.ShapeDtypeStruct((4 * blocks, 128), f32),
             jax.ShapeDtypeStruct((12 * blocks, 128), f32),
         ),
@@ -715,33 +721,33 @@
         out_specs=(anywhere(), vmem(), vmem()),
         scratch_shapes=[
             pltpu.SMEM((4096,), i32),
-            pltpu.VMEM((4 * blocks, 8, 128), f32),
+            pltpu.VMEM((32 * blocks, 128), f32),
             pltpu.VMEM((16, 128), f32),
             pltpu.VMEM((2 * blocks, 128, 32), bf16),
             pltpu.VMEM((4 * blocks, 32, 256), bf16),
             pltpu.VMEM((4 * blocks, 16, 128), bf16),
             pltpu.VMEM((blocks // 4, 128, 128), f32),
-            pltpu.VMEM((4 * blocks, 8, 128), f32),
-            pltpu.VMEM((4 * blocks, 8, 128), f32),
-            pltpu.VMEM((4 * blocks + 1, 8, 128), f32),
+            pltpu.VMEM((32 * blocks, 128), f32),
+            pltpu.VMEM((32 * blocks, 128), f32),
+            pltpu.VMEM((32 * blocks + 8, 128), f32),
             pltpu.SemaphoreType.DMA((4,)),
         ]
         + [pltpu.VMEM((128, 256), f32)] * ring
         + [pltpu.VMEM((256, 256), bf16)] * ring,
         compiler_params=pltpu.CompilerParams(vmem_limit_bytes=vmem_grant),
         name="contact",
-    )(lists.reshape(4096), cols.reshape(4 * blocks, 8, 128), wide)
+    )(lists.reshape(4096), cols.reshape(32 * blocks, 128), wide)
 
     rates, fluid = pl.pallas_call(
         finish_kernel,
         out_shape=(
-            jax.ShapeDtypeStruct((blocks, 4, 128), f32),
+            jax.ShapeDtypeStruct((4 * blocks, 128), f32),
             jax.ShapeDtypeStruct((2, 256), f32),
         ),
         in_specs=[anywhere()] * 6,
         out_specs=(vmem(), vmem()),
         scratch_shapes=[
-            pltpu.VMEM((blocks, 8, 128), f32),
+            pltpu.VMEM((8 * blocks, 128), f32),
             pltpu.VMEM((4 * blocks, 128), f32),
             pltpu.VMEM((blocks, 128), i32),
             pltpu.VMEM((blocks, 128), i32),
@@ -766,7 +772,11 @@
         cell_index[0, 0],
         fluid_temp.reshape(1, 256),
     )
-    return moved[None, None], rates[None, None], fluid.reshape(1, 1, 2, 256)
+    return (
+        moved.reshape(1, 1, blocks, 8, 128),
+        rates.reshape(1, 1, blocks, 4, 128),
+        fluid[None, None],
+    )
 
 
 def solution(mesh):

time: 91.4 us -> 87 us (0.952)
  the two profiles are of different devices: /device:TPU:11 before, /device:TPU:3 now
where the time goes in v4:
time: 87 us; the launch traced here: 86.8 us
  Pallas kernels  83.3 us (96%)
  local copies, waits for them, and re-layouts  2.86 us (3%)
    pallas_call x1, Pallas kernels, shards(): pl.pallas_call(pair_kernel, out_shape=(jax.ShapeDtypeStruct((8 * blocks,...  37.7 us
    pallas_call x1, Pallas kernels, shards(): pl.pallas_call(halo_kernel, out_shape=(jax.ShapeDtypeStruct((4, blocks, 8...  24.4 us
    pallas_call x1, Pallas kernels, shards(): pl.pallas_call(finish_kernel, out_shape=(jax.ShapeDtypeStruct((4 * blocks...  21.2 us
    unnamed x2, local copies, waits for them, and re-layouts  2.86 us

profile of v4, /device:TPU:3, one launch (start us, length us, event | category | flops | bytes accessed | tf_op | source)
XLA Modules:
  0.0 86.8 jit_solution(14788646711977538879)
XLA Ops:
  0.6 24.4 %halo.1 = (f32[4,96,8,128]{3,2,1,0:T(8,128)}, s32[4,8,128]{2,1,0:T(8,128)}, f32[16,128]{1,0:T(8,128)}) custom-call(s32[24]{0:T(128)} %bitcast.22, s32[2]{0:T(128)} %bitcast.23, s32[2,576]{1,0:T(2,128)} %bitcast.19, f32[96,8,128]{2,1,0:T(8,128)} %bitcast.13), custom_call_target="tpu_custom_call" | custom-call | tf_op jit(solution)/shard_map/halo/pallas_call | solution.py:674
  25.0 37.7 %contact.1 = (f32[768,128]{1,0:T(8,128)}, f32[384,128]{1,0:T(8,128)}, f32[1152,128]{1,0:T(8,128)}) custom-call(s32[4096]{0:T(1024)} %bitcast.18, f32[3072,128]{1,0:T(8,128)} %bitcast.12, f32[16,128]{1,0:T(8,128)} %get-tuple-element.13.wide_hbm), custom_call_target="tpu_custom_call" | custom-call | tf_op jit(solution)/shard_map/contact/pallas_call | solution.py:713
  62.8 21.2 %finish.1 = (f32[384,128]{1,0:T(8,128)}, f32[2,256]{1,0:T(2,128)}) custom-call(f32[768,128]{1,0:T(8,128)} %get-tuple-element.14.moved_hbm, f32[384,128]{1,0:T(8,128)} %get-tuple-element.15.own_hbm, f32[1152,128]{1,0:T(8,128)} %get-tuple-element.16.sides_ref, s32[96,128]{1,0:T(8,128)} %bitcast.16, s32[96,128]{1,0:T(8,128)} %bitcast.17, f32[1,256]{1,0:T(1,128)} %bitcast.21), custom_call_target="tpu_custom_call" | custom-call | tf_op jit(solution)/shard_map/finish/pallas_call | solution.py:741
  84.0 1.6 %copy.12 = f32[1,1,96,4,128]{4,3,2,1,0:T(4,128)} copy(f32[1,1,96,4,128]{4,3,2,1,0:T(4,128)} %bitcast.15) | data formatting | bytes 393216
  85.6 1.2 %copy.13 = f32[1,1,2,256]{3,2,1,0:T(2,128)} copy(f32[1,1,2,256]{3,2,1,0:T(2,128)} %bitcast.20) | data formatting | bytes 4096

commit v5 on v4

--- a/solution.py
+++ b/solution.py
@@ -109,7 +109,7 @@
         rows == 0, u, jnp.where(rows == 1, v_slot, jnp.where(rows == 2, v_side, 0))
     )
     moved = dot_tt(values.astype(bf16), target)
-    packed = moved[0:1] + 256.0 * (moved[1:2] + 96.0 * moved[2:3])
+    packed = moved[0:1] + 512.0 * (moved[1:2] + 96.0 * moved[2:3])
     diag = iota((8, 128), 0) == iota((8, 128), 1)
     begin = jnp.sum(jnp.where(diag, starts, 0.0), axis=0, keepdims=True)
     return packed.astype(i32), begin.astype(i32)
@@ -176,7 +176,19 @@
     near[0:1, :] = jnp.full((1, 128), far)
     for m in range(count):
         dep[m] = state_ref[leaving_ref[m]]
-    greet((up, down, *along.values()))
+    b = lax.axis_index("gy")
+    nb = lax.axis_size("gy")
+    across = {"gy": lax.rem(b + 2, nb)}
+    greet((up, down, across, *along.values()))
+    depart = pltpu.make_async_remote_copy(
+        src_ref=dep,
+        dst_ref=cat.at[0:count],
+        send_sem=dep_send,
+        recv_sem=dep_recv,
+        device_id=ahead,
+        device_id_type=MESH,
+    )
+    depart.start()
     asks = []
     for at, device in ((1, down), (2, up), (3, ahead)):
         copy = pltpu.make_async_remote_copy(
@@ -189,15 +201,23 @@
         )
         copy.start()
         asks.append(copy)
-    depart = pltpu.make_async_remote_copy(
-        src_ref=dep,
-        dst_ref=cat.at[0:count],
-        send_sem=dep_send,
-        recv_sem=dep_recv,
-        device_id=ahead,
-        device_id_type=MESH,
-    )
-    depart.start()
+    for copy in asks:
+        copy.wait()
+    lane = iota((1, 128), 1)
+    load = local + 2.0 * far + 2.0 * near[1:2, :] + near[2:3, :] + 3.0 * near[3:4, :]
+    near[4:5, :] = jnp.where(lane < 64, load, local)
+    tells = []
+    for at, device in ((5, down), (6, up), (7, across)):
+        copy = pltpu.make_async_remote_copy(
+            src_ref=near.at[4:5],
+            dst_ref=near.at[at : at + 1],
+            send_sem=near_send.at[at - 2],
+            recv_sem=near_recv.at[at - 2],
+            device_id=device,
+            device_id_type=MESH,
+        )
+        copy.start()
+        tells.append(copy)
     place = iota((8, 128), 1)
     slot = place + count
     for m in range(count):
@@ -225,10 +245,13 @@
         )
         copy.start()
         copies.append(copy)
-    for copy in asks:
+    for copy in tells:
         copy.wait()
-    load = local + 2.0 * far + 2.0 * near[1:2, :] + near[2:3, :] + 3.0 * near[3:4, :]
-    wide_ref[reach : reach + 1, :] = jnp.where(iota((1, 128), 1) < 64, load, local)
+    turn = lane & 3
+    row = near[4:5, :]
+    for at, step in ((5, 1), (6, nb - 1), (7, 2)):
+        row = jnp.where(turn == lax.rem(b + step, nb), near[at : at + 1, :], row)
+    wide_ref[reach : reach + 1, :] = row
     for at, step in enumerate(along):
         copy = pltpu.make_async_remote_copy(
             src_ref=wide_ref.at[reach : reach + 1],
@@ -302,7 +325,7 @@
     def swap(value):
         return jnp.where(rows < 3, pltpu.roll(value, 5, 0), pltpu.roll(value, 3, 0))
 
-    def eight(base, shift, want_u, radius):
+    def eight(base, shift, u_base, radius):
         naturals = []
         for q in range(8):
             i = base + q
@@ -313,7 +336,7 @@
             L[i] = jnp.concatenate([hi, mid], axis=0).astype(bf16)
             full = jnp.where(rows < 6, S, E)
             hi, mid = split2(full)
-            if want_u:
+            if u_base is not None:
                 low = jnp.where(rows < 6, hi, full - hi - mid)
                 naturals.append(jnp.concatenate([hi, low, mid, ones], axis=0).astype(bf16))
             a0 = hi * ca + c6
@@ -326,18 +349,18 @@
             )
             V[i + shift, :, 0:128] = A.astype(bf16)
             V[i + shift, :, 128:256] = B.astype(bf16)
-        if want_u:
+        if u_base is not None:
             turned = dot_tt(eye, jnp.concatenate(naturals, axis=0))
             for q in range(8):
-                U[base + q] = turned[:, 32 * q : 32 * q + 32].astype(bf16)
-            RT[lax.shift_right_logical(base, 3), :, 0:8] = radius.T
+                U[u_base + q] = turned[:, 32 * q : 32 * q + 32].astype(bf16)
+            RT[lax.shift_right_logical(u_base, 3), :, 0:8] = radius.T
 
     def body(t, carry):
         radius = [dense(96 * col + 8 * t) for col in range(4)]
-        eight(8 * t, 0, True, radius[0])
-        eight(96 + 8 * t, 192, True, radius[1])
-        eight(192 + 8 * t, -96, False, None)
-        eight(288 + 8 * t, -96, False, None)
+        eight(8 * t, 0, 8 * t, radius[0])
+        eight(96 + 8 * t, 192, 96 + 8 * t, radius[1])
+        eight(192 + 8 * t, -96, None, None)
+        eight(288 + 8 * t, -96, 192 + 8 * t, radius[3])
         return step(step(carry))
 
     return lax.fori_loop(0, cols_ref.shape[0] // 256, body, start)
@@ -345,14 +368,22 @@
 
 def shares(wide):
     rows = iota((8, 128), 0)
+    lanes = iota((8, 128), 1)
+    b = lax.axis_index("gy")
+    nb = lax.axis_size("gy")
 
     def chain(load):
-        local = jnp.where(rows < 7, pltpu.roll(load, 64, 1), 0.0)
+        local = pltpu.roll(load, 64, 1)
+        passing = jnp.where(rows < 7, local, 0.0)
 
         def step(given):
-            now = load - given + pltpu.roll(given, 1, 0)
-            change = 0.48 * (now - pltpu.roll(now, 7, 0))
-            return jnp.minimum(jnp.maximum(given + change, 0.0), local)
+            ahead, up = given
+            now = load - ahead - up + pltpu.roll(ahead, 1, 0) + pltpu.roll(up, 1, 1)
+            ahead = ahead + 0.24 * (now - pltpu.roll(now, 7, 0))
+            ahead = jnp.minimum(jnp.maximum(ahead, 0.0), jnp.maximum(passing - up, 0.0))
+            up = up + 0.24 * (now - pltpu.roll(now, 127, 1))
+            up = jnp.minimum(jnp.maximum(up, 0.0), jnp.maximum(local - ahead, 0.0))
+            return ahead, up
 
         return step
 
@@ -362,12 +393,13 @@
     def step(given):
         return own(given[0]), behind(given[1])
 
-    def value(given):
-        picked = (rows == reach - 1) & (iota((8, 128), 1) == 0)
+    def value(given, shift):
+        column = lax.rem(b + shift + nb, nb)
+        picked = (rows == reach - 1) & (lanes == column + 32)
         return jnp.sum(jnp.where(picked, given, 0.0)).astype(i32)
 
     start = jnp.zeros((8, 128), f32)
-    return (start, start), step, value
+    return ((start, start), (start, start)), step, value
 
 
 def pair_kernel(
@@ -408,24 +440,33 @@
     keep.start()
     given, step, value = shares(wide)
     given = build_tables(cols_ref, U, V, L, RT, extra, pieces, given, step)
-    s_out = value(given[0])
-    s_in = value(given[1])
+    ahead_out = value(given[0][0], 0)
+    up_out = value(given[0][1], 0)
+    ahead_in = value(given[1][0], 0)
+    ahead_down = value(given[0][0], -1)
+    up_in = value(given[0][1], -1)
 
     def begin(at, name):
         return lists_ref[at * 1024 + 6 * 128 + name]
 
-    s_out = jnp.minimum(s_out, begin(0, 1))
-    s_in = jnp.minimum(s_in, begin(3, 1))
+    def cut(at, first, second):
+        first = jnp.minimum(first, begin(at, 1))
+        return first, jnp.minimum(first + second, begin(at, 1))
+
+    _, kept = cut(0, ahead_out, up_out)
+    ahead_in = jnp.minimum(ahead_in, begin(3, 1))
+    up_low, up_high = cut(2, ahead_down, up_in)
     ends = []
     shifts = []
     so_far = 0
     for at, low, high in (
-        (0, s_out, begin(0, 1)),
+        (0, kept, begin(0, 1)),
         (0, begin(0, 1), begin(0, 2)),
         (1, begin(1, 2), begin(1, 3)),
         (2, begin(2, 3), begin(2, 4)),
         (3, begin(3, 4), begin(3, 5)),
-        (3, 0, s_in),
+        (3, 0, ahead_in),
+        (2, up_low, up_high),
     ):
         shifts.append(at * 1024 + low - so_far)
         so_far = so_far + (high - low)
@@ -435,12 +476,17 @@
 
     def entry(k):
         k = jnp.minimum(k, last)
-        shift = shifts[5]
-        for at in range(4, -1, -1):
+        shift = shifts[6]
+        for at in range(5, -1, -1):
             shift = jnp.where(k < ends[at], shifts[at], shift)
         code = lists_ref[k + shift]
-        code = code + jnp.where(k < ends[4], 0, 96 + 256 * 288)
-        return code & 255, lax.shift_right_logical(code, 8)
+        code = code + jnp.where(
+            k < ends[4], 0, jnp.where(k < ends[5], 96 + 512 * 288, 192 + 512 * 192)
+        )
+        return code & 511, lax.shift_right_logical(code, 9)
+
+    def spot_u(u):
+        return jnp.where(u < 192, u, u + 96)
 
     def spot(v):
         return jnp.where(v < 96, v, jnp.where(v < 288, v + 96, v - 192))
@@ -484,7 +530,8 @@
     def sums(k, at):
         u, v = entry(k)
         w = spot(v)
-        first = jnp.concatenate([L[u], L[u]], axis=1)
+        o = spot_u(u)
+        first = jnp.concatenate([L[o], L[o]], axis=1)
         second = jnp.concatenate([L[w], L[w]], axis=1)
         m = M[at]
         crossed = jnp.concatenate(
@@ -497,9 +544,9 @@
         to_second = folded(jnp.dot(first, m[...], preferred_element_type=f32))
         to_first = folded(dot_tt(second, crossed))
         live = k < n
-        u = jnp.where(live, u, trash)
+        o = jnp.where(live, o, trash)
         w = jnp.where(live, w, trash)
-        acc[tile(u), :] += to_first
+        acc[tile(o), :] += to_first
         acc[tile(w), :] += to_second
 
     for q in range(ring):
@@ -540,22 +587,17 @@
 
 def finish_kernel(
     moved_hbm,
-    own_hbm,
     sides_ref,
     flags_hbm,
     cells_hbm,
     table_hbm,
-    rates_ref,
+    mix_ref,
     fluid_ref,
     moved_ref,
-    own_ref,
     flags_ref,
     cells_ref,
     table_ref,
     in_sem,
-    got,
-    heat_in,
-    to_fluid,
     sums,
     send,
     recv,
@@ -569,7 +611,6 @@
                 (flags_hbm, flags_ref),
                 (cells_hbm, cells_ref),
                 (table_hbm, table_ref),
-                (own_hbm, own_ref),
             )
         )
     ]
@@ -577,11 +618,12 @@
         copy.start()
     greet((ahead, behind, up, down))
     copies = []
-    span = got.shape[1]
+    span = sides_ref.shape[0] // 3
+    blocks = span // 4
     for at, device in ((0, behind), (1, up), (2, down)):
         copy = pltpu.make_async_remote_copy(
             src_ref=sides_ref.at[span * at : span * at + span],
-            dst_ref=got.at[at],
+            dst_ref=mix_ref.at[span * at : span * at + span],
             send_sem=send.at[at],
             recv_sem=recv.at[at],
             device_id=device,
@@ -615,7 +657,6 @@
             fluid.append(jnp.sum(value * hot_high, axis=0, keepdims=True))
             hots.append((hot_high, hot_low))
         flow = film_gain * radius * radius * (temper - jnp.concatenate(fluid, axis=0))
-        to_fluid[at, :] = flow
         pieces = split3(volume) + split3(flow)
         total = sums[...]
         for c in range(8):
@@ -624,7 +665,8 @@
             total = total + dot_tt(hot_high.astype(bf16), spread.astype(bf16))
         sums[...] = total
         wall = wall_gain * flags_ref[at, :].astype(f32) * (wall_temp - temper) * radius
-        heat_in[at, :] = wall - flow
+        mix_ref[pl.ds(pl.multiple_of(3 * span + g * 8, 8), 8), :] = wall - flow
+        mix_ref[pl.ds(pl.multiple_of(3 * span + blocks + g * 8, 8), 8), :] = 1.0 / volume
         return carry
 
     lax.fori_loop(0, 12, cells_of, 0)
@@ -637,25 +679,41 @@
     for copy in copies:
         copy.wait()
 
+
+def rates_kernel(
+    own_hbm, mix_hbm, fluid_hbm, rates_ref, fluid_ref, own, mix, fluid, sem
+):
+    copies = [
+        pltpu.make_async_copy(source, target, sem.at[at])
+        for at, (source, target) in enumerate(
+            ((mix_hbm, mix), (own_hbm, own), (fluid_hbm, fluid))
+        )
+    ]
+    for copy in copies:
+        copy.start()
+    for copy in copies:
+        copy.wait()
+    fluid_ref[...] = fluid[...]
+    span = own.shape[0]
+    blocks = span // 4
+
     def combine(g, carry):
-        at = pl.ds(pl.multiple_of(g * 8, 8), 8)
-        radius = moved_ref[rows_of(g * 8, 7), :]
-        volume = 4.0 / 3.0 * math.pi * radius * radius * radius
-        inverse = 1.0 / volume
+        at = pl.multiple_of(g * 8, 8)
+        inverse = mix[pl.ds(3 * span + blocks + at, 8), :]
         for c in range(4):
             here = pl.ds(g * 32 + c, 8, 4)
-            value = own_ref[here, :]
+            value = own[here, :]
             for side in range(3):
-                value = value + got[side, here, :]
+                value = value + mix[pl.ds(span * side + g * 32 + c, 8, 4), :]
             if c == 3:
-                value = value + heat_in[at, :]
+                value = value + mix[pl.ds(3 * span + at, 8), :]
             value = value * inverse
             if c == 2:
                 value = value - gravity
             rates_ref[here, :] = value
         return carry
 
-    lax.fori_loop(0, 12, combine, 0)
+    lax.fori_loop(0, blocks // 8, combine, 0, unroll=4)
 
 
 def anywhere():
@@ -699,8 +757,8 @@
             pltpu.SemaphoreType.DMA,
             pltpu.SemaphoreType.DMA((4,)),
             pltpu.VMEM((8, 128), f32),
-            pltpu.SemaphoreType.DMA((3,)),
-            pltpu.SemaphoreType.DMA((3,)),
+            pltpu.SemaphoreType.DMA((6,)),
+            pltpu.SemaphoreType.DMA((6,)),
             pltpu.SemaphoreType.DMA((2 * reach,)),
             pltpu.SemaphoreType.DMA((2 * reach,)),
         ],
@@ -723,10 +781,10 @@
             pltpu.SMEM((4096,), i32),
             pltpu.VMEM((32 * blocks, 128), f32),
             pltpu.VMEM((16, 128), f32),
-            pltpu.VMEM((2 * blocks, 128, 32), bf16),
+            pltpu.VMEM((3 * blocks, 128, 32), bf16),
             pltpu.VMEM((4 * blocks, 32, 256), bf16),
             pltpu.VMEM((4 * blocks, 16, 128), bf16),
-            pltpu.VMEM((blocks // 4, 128, 128), f32),
+            pltpu.VMEM((3 * blocks // 8, 128, 128), f32),
             pltpu.VMEM((32 * blocks, 128), f32),
             pltpu.VMEM((32 * blocks, 128), f32),
             pltpu.VMEM((32 * blocks + 8, 128), f32),
@@ -738,24 +796,20 @@
         name="contact",
     )(lists.reshape(4096), cols.reshape(32 * blocks, 128), wide)
 
-    rates, fluid = pl.pallas_call(
+    mix, fluid = pl.pallas_call(
         finish_kernel,
         out_shape=(
-            jax.ShapeDtypeStruct((4 * blocks, 128), f32),
+            jax.ShapeDtypeStruct((14 * blocks, 128), f32),
             jax.ShapeDtypeStruct((2, 256), f32),
         ),
-        in_specs=[anywhere()] * 6,
+        in_specs=[anywhere()] * 5,
         out_specs=(vmem(), vmem()),
         scratch_shapes=[
             pltpu.VMEM((8 * blocks, 128), f32),
-            pltpu.VMEM((4 * blocks, 128), f32),
             pltpu.VMEM((blocks, 128), i32),
             pltpu.VMEM((blocks, 128), i32),
             pltpu.VMEM((1, 256), f32),
-            pltpu.SemaphoreType.DMA((5,)),
-            pltpu.VMEM((3, 4 * blocks, 128), f32),
-            pltpu.VMEM((blocks, 128), f32),
-            pltpu.VMEM((blocks, 128), f32),
+            pltpu.SemaphoreType.DMA((4,)),
             pltpu.VMEM((16, 96), f32),
             pltpu.SemaphoreType.DMA((3,)),
             pltpu.SemaphoreType.DMA((3,)),
@@ -764,14 +818,25 @@
             collective_id=1, has_side_effects=True, vmem_limit_bytes=vmem_grant
         ),
         name="finish",
-    )(
-        moved,
-        own,
-        sides,
-        wall_flags[0, 0],
-        cell_index[0, 0],
-        fluid_temp.reshape(1, 256),
-    )
+    )(moved, sides, wall_flags[0, 0], cell_index[0, 0], fluid_temp.reshape(1, 256))
+
+    rates, fluid = pl.pallas_call(
+        rates_kernel,
+        out_shape=(
+            jax.ShapeDtypeStruct((4 * blocks, 128), f32),
+            jax.ShapeDtypeStruct((2, 256), f32),
+        ),
+        in_specs=[anywhere()] * 3,
+        out_specs=(vmem(), vmem()),
+        scratch_shapes=[
+            pltpu.VMEM((4 * blocks, 128), f32),
+            pltpu.VMEM((14 * blocks, 128), f32),
+            pltpu.VMEM((2, 256), f32),
+            pltpu.SemaphoreType.DMA((3,)),
+        ],
+        compiler_params=pltpu.CompilerParams(vmem_limit_bytes=vmem_grant),
+        name="rates",
+    )(own, mix, fluid)
     return (
         moved.reshape(1, 1, blocks, 8, 128),
         rates.reshape(1, 1, blocks, 4, 128),

time: 87 us -> 92.8 us (1.067)
  Pallas kernels: 83.3 us -> 92 us
  local copies, waits for them, and re-layouts: 2.86 us -> 0 us
    pallas_call x1, Pallas kernels: 37.7 us -> 45.2 us  [shards(): pl.pallas_call(pair_kernel, out_shape=(jax.ShapeDtypeStruct((8 * blocks,...]
    pallas_call x1, Pallas kernels: 24.4 us -> 27.9 us  [shards(): pl.pallas_call(halo_kernel, out_shape=(jax.ShapeDtypeStruct((4, blocks, 8...]
    unnamed x2 -> x0, local copies, waits for them, and re-layouts: 2.86 us -> none
    pallas_call x1 -> x2, Pallas kernels: 21.2 us -> 18.9 us  [the longest x1 17 us: shards(): pl.pallas_call(finish_kernel, out_shape=(jax.ShapeDtypeStruct((14 * block...]
where the time goes in v5:
time: 92.8 us; the launch traced here: 92.6 us
  Pallas kernels  92 us (99%)
    pallas_call x1, Pallas kernels, shards(): pl.pallas_call(pair_kernel, out_shape=(jax.ShapeDtypeStruct((8 * blocks,...  45.2 us
    pallas_call x1, Pallas kernels, shards(): pl.pallas_call(halo_kernel, out_shape=(jax.ShapeDtypeStruct((4, blocks, 8...  27.9 us
    pallas_call x1, Pallas kernels, shards(): pl.pallas_call(finish_kernel, out_shape=(jax.ShapeDtypeStruct((14 * block...  17 us
    pallas_call x1, Pallas kernels, shards(): pl.pallas_call(rates_kernel, out_shape=(jax.ShapeDtypeStruct((4 * blocks,...  1.9 us

profile of v5, /device:TPU:3, one launch (start us, length us, event | category | flops | bytes accessed | tf_op | source)
XLA Modules:
  0.0 92.6 jit_solution(368874104399946330)
XLA Ops:
  0.6 27.9 %halo.1 = (f32[4,96,8,128]{3,2,1,0:T(8,128)}, s32[4,8,128]{2,1,0:T(8,128)}, f32[16,128]{1,0:T(8,128)}) custom-call(s32[24]{0:T(128)} %bitcast.20, s32[2]{0:T(128)} %bitcast.21, s32[2,576]{1,0:T(2,128)} %bitcast.18, f32[96,8,128]{2,1,0:T(8,128)} %bitcast.14), custom_call_target="tpu_custom_call" | custom-call | tf_op jit(solution)/shard_map/halo/pallas_call | solution.py:732
  28.5 45.2 %contact.1 = (f32[768,128]{1,0:T(8,128)}, f32[384,128]{1,0:T(8,128)}, f32[1152,128]{1,0:T(8,128)}) custom-call(s32[4096]{0:T(1024)} %bitcast.17, f32[3072,128]{1,0:T(8,128)} %bitcast.12, f32[16,128]{1,0:T(8,128)} %get-tuple-element.15.wide_hbm), custom_call_target="tpu_custom_call" | custom-call | tf_op jit(solution)/shard_map/contact/pallas_call | solution.py:771
  73.7 17.0 %finish.1 = (f32[1344,128]{1,0:T(8,128)}, f32[2,256]{1,0:T(2,128)}) custom-call(f32[768,128]{1,0:T(8,128)} %get-tuple-element.16.moved_hbm, f32[1152,128]{1,0:T(8,128)} %get-tuple-element.18.sides_ref, s32[96,128]{1,0:T(8,128)} %bitcast.15, s32[96,128]{1,0:T(8,128)} %bitcast.16, f32[1,256]{1,0:T(1,128)} %bitcast.19), custom_call_target="tpu_custom_call" | custom-call | tf_op jit(solution)/shard_map/finish/pallas_call | solution.py:799
  90.7 1.9 %rates.1 = (f32[384,128]{1,0:T(8,128)}, f32[2,256]{1,0:T(2,128)}) custom-call(f32[384,128]{1,0:T(8,128)} %get-tuple-element.17.own_hbm, f32[1344,128]{1,0:T(8,128)} %get-tuple-element.19.mix_hbm, f32[2,256]{1,0:T(2,128)} %get-tuple-element.20.fluid_hbm), custom_call_target="tpu_custom_call" | custom-call | tf_op jit(solution)/shard_map/rates/pallas_call | solution.py:823

commit v6 on v5

--- a/solution.py
+++ b/solution.py
@@ -173,13 +173,26 @@
         copy.wait()
     local = counts_ref[0].astype(f32)
     far = (counts_ref[1] - counts_ref[0]).astype(f32) * 0.125
-    near[0:1, :] = jnp.full((1, 128), far)
+    lane = iota((1, 128), 1)
+    near[0:1, :] = jnp.where(lane < 64, far, local)
     for m in range(count):
         dep[m] = state_ref[leaving_ref[m]]
     b = lax.axis_index("gy")
     nb = lax.axis_size("gy")
     across = {"gy": lax.rem(b + 2, nb)}
     greet((up, down, across, *along.values()))
+    asks = []
+    for at, device in ((1, down), (2, up), (3, across)):
+        copy = pltpu.make_async_remote_copy(
+            src_ref=near.at[0:1],
+            dst_ref=near.at[at : at + 1],
+            send_sem=near_send.at[at - 1],
+            recv_sem=near_recv.at[at - 1],
+            device_id=device,
+            device_id_type=MESH,
+        )
+        copy.start()
+        asks.append(copy)
     depart = pltpu.make_async_remote_copy(
         src_ref=dep,
         dst_ref=cat.at[0:count],
@@ -189,35 +202,6 @@
         device_id_type=MESH,
     )
     depart.start()
-    asks = []
-    for at, device in ((1, down), (2, up), (3, ahead)):
-        copy = pltpu.make_async_remote_copy(
-            src_ref=near.at[0:1],
-            dst_ref=near.at[at : at + 1],
-            send_sem=near_send.at[at - 1],
-            recv_sem=near_recv.at[at - 1],
-            device_id=device,
-            device_id_type=MESH,
-        )
-        copy.start()
-        asks.append(copy)
-    for copy in asks:
-        copy.wait()
-    lane = iota((1, 128), 1)
-    load = local + 2.0 * far + 2.0 * near[1:2, :] + near[2:3, :] + 3.0 * near[3:4, :]
-    near[4:5, :] = jnp.where(lane < 64, load, local)
-    tells = []
-    for at, device in ((5, down), (6, up), (7, across)):
-        copy = pltpu.make_async_remote_copy(
-            src_ref=near.at[4:5],
-            dst_ref=near.at[at : at + 1],
-            send_sem=near_send.at[at - 2],
-            recv_sem=near_recv.at[at - 2],
-            device_id=device,
-            device_id_type=MESH,
-        )
-        copy.start()
-        tells.append(copy)
     place = iota((8, 128), 1)
     slot = place + count
     for m in range(count):
@@ -234,22 +218,11 @@
         lists_ref[0, row : row + 1, :] = packed[:, 128 * row : 128 * row + 128]
     lists_ref[0, 6:7, :] = begin
     copies = []
-    for at, device in ((1, down), (2, up), (3, ahead)):
-        copy = pltpu.make_async_remote_copy(
-            src_ref=lists_ref.at[0],
-            dst_ref=lists_ref.at[at],
-            send_sem=list_send.at[at - 1],
-            recv_sem=list_recv.at[at - 1],
-            device_id=device,
-            device_id_type=MESH,
-        )
-        copy.start()
-        copies.append(copy)
-    for copy in tells:
+    for copy in asks:
         copy.wait()
     turn = lane & 3
-    row = near[4:5, :]
-    for at, step in ((5, 1), (6, nb - 1), (7, 2)):
+    row = near[0:1, :]
+    for at, step in ((1, 1), (2, nb - 1), (3, 2)):
         row = jnp.where(turn == lax.rem(b + step, nb), near[at : at + 1, :], row)
     wide_ref[reach : reach + 1, :] = row
     for at, step in enumerate(along):
@@ -259,6 +232,17 @@
             send_sem=wide_send.at[at],
             recv_sem=wide_recv.at[at],
             device_id=along[step],
+            device_id_type=MESH,
+        )
+        copy.start()
+        copies.append(copy)
+    for at, device in ((1, down), (2, up), (3, ahead)):
+        copy = pltpu.make_async_remote_copy(
+            src_ref=lists_ref.at[0],
+            dst_ref=lists_ref.at[at],
+            send_sem=list_send.at[at - 1],
+            recv_sem=list_recv.at[at - 1],
+            device_id=device,
             device_id_type=MESH,
         )
         copy.start()
@@ -297,9 +281,10 @@
     return pl.ds(pl.multiple_of(i * 8, 8), 8)
 
 
-def build_tables(cols_ref, U, V, L, RT, extra, pieces, start, step):
+def build_tables(cols_ref, U, V, L, RT, extra, pieces, natural, start, step, never, spare):
     rows = iota((8, 128), 0)
     eye = (iota((128, 128), 0) == iota((128, 128), 1)).astype(bf16)
+    eyes = jnp.concatenate([eye, eye, eye], axis=1)
     c6 = jnp.where(rows == 6, 1.0, 0.0)
     c7 = jnp.where(rows == 7, 0.25, 0.0)
     ca = jnp.where(rows < 3, -2.0, 0.0)
@@ -320,25 +305,27 @@
         extra[rows_of(base, 7), :] = dot
         for c, piece in enumerate(split3(square) + split3(0.25 * dot)):
             pieces[rows_of(base, c), :] = piece
-        return radius
 
     def swap(value):
         return jnp.where(rows < 3, pltpu.roll(value, 5, 0), pltpu.roll(value, 3, 0))
 
-    def eight(base, shift, u_base, radius):
-        naturals = []
+    def eight(base, shift, at, held=None):
         for q in range(8):
             i = base + q
             S = cols_ref[tile(i), :]
+            if held is not None:
+                S = jnp.where(never, held, S)
             E = extra[tile(i), :]
             G = pieces[tile(i), :]
             hi, mid = split2(jnp.where(rows < 3, S, jnp.where(rows < 6, E, 0.0)))
             L[i] = jnp.concatenate([hi, mid], axis=0).astype(bf16)
             full = jnp.where(rows < 6, S, E)
             hi, mid = split2(full)
-            if u_base is not None:
+            if at is not None:
                 low = jnp.where(rows < 6, hi, full - hi - mid)
-                naturals.append(jnp.concatenate([hi, low, mid, ones], axis=0).astype(bf16))
+                natural[at, 32 * q : 32 * q + 32, :] = jnp.concatenate(
+                    [hi, low, mid, ones], axis=0
+                ).astype(bf16)
             a0 = hi * ca + c6
             a1 = mid * ca + c6
             b0 = swap(hi) * cb + c7
@@ -349,21 +336,40 @@
             )
             V[i + shift, :, 0:128] = A.astype(bf16)
             V[i + shift, :, 128:256] = B.astype(bf16)
-        if u_base is not None:
-            turned = dot_tt(eye, jnp.concatenate(naturals, axis=0))
-            for q in range(8):
-                U[u_base + q] = turned[:, 32 * q : 32 * q + 32].astype(bf16)
-            RT[lax.shift_right_logical(u_base, 3), :, 0:8] = radius.T
+
+    def turn(at, u_base):
+        turned = dot_tt(eye, natural[at]).astype(bf16)
+        for q in range(8):
+            U[u_base + q, :, 0:32] = turned[:, 32 * q : 32 * q + 32]
+
+    def column(base, u_base):
+        radius = cols_ref[rows_of(base, 7), :]
+        three = jnp.concatenate(split3(radius), axis=1).astype(bf16)
+        RT[lax.shift_right_logical(u_base, 3), :, 0:8] = dot_tt(eyes, three)
+
+    def turns(t):
+        turn(0, 8 * t)
+        turn(1, 96 + 8 * t)
+        turn(2, 192 + 8 * t)
+        column(8 * t, 8 * t)
+        column(96 + 8 * t, 96 + 8 * t)
+        column(288 + 8 * t, 192 + 8 * t)
 
     def body(t, carry):
-        radius = [dense(96 * col + 8 * t) for col in range(4)]
-        eight(8 * t, 0, 8 * t, radius[0])
-        eight(96 + 8 * t, 192, 96 + 8 * t, radius[1])
-        eight(192 + 8 * t, -96, None, None)
-        eight(288 + 8 * t, -96, 192 + 8 * t, radius[3])
-        return step(step(carry))
-
-    return lax.fori_loop(0, cols_ref.shape[0] // 256, body, start)
+        turns(jnp.maximum(t - 1, 0))
+        for col in range(4):
+            dense(96 * col + 8 * t)
+        eight(8 * t, 0, 0)
+        eight(96 + 8 * t, 192, 1)
+        eight(288 + 8 * t, -96, 2)
+        held = U[spare, 0:16, :].astype(f32)[0:8]
+        eight(192 + 8 * t, -96, None, held)
+        return step(carry)
+
+    count = cols_ref.shape[0] // 256
+    carry = lax.fori_loop(0, count, body, start)
+    turns(count - 1)
+    return carry
 
 
 def shares(wide):
@@ -371,35 +377,35 @@
     lanes = iota((8, 128), 1)
     b = lax.axis_index("gy")
     nb = lax.axis_size("gy")
-
-    def chain(load):
-        local = pltpu.roll(load, 64, 1)
-        passing = jnp.where(rows < 7, local, 0.0)
-
-        def step(given):
-            ahead, up = given
-            now = load - ahead - up + pltpu.roll(ahead, 1, 0) + pltpu.roll(up, 1, 1)
-            ahead = ahead + 0.24 * (now - pltpu.roll(now, 7, 0))
-            ahead = jnp.minimum(jnp.maximum(ahead, 0.0), jnp.maximum(passing - up, 0.0))
-            up = up + 0.24 * (now - pltpu.roll(now, 127, 1))
-            up = jnp.minimum(jnp.maximum(up, 0.0), jnp.maximum(local - ahead, 0.0))
-            return ahead, up
-
-        return step
-
-    own = chain(wide[1:9, :])
-    behind = chain(wide[0:8, :])
+    own = wide[1:9, :]
+    behind = wide[0:8, :]
+    far = jnp.where(lanes < 64, own, pltpu.roll(behind, 64, 1))
+    local = jnp.where(lanes < 64, pltpu.roll(own, 64, 1), behind)
+    load = (
+        local
+        + 2.0 * far
+        + 2.0 * pltpu.roll(far, 127, 1)
+        + pltpu.roll(far, 1, 1)
+        + 3.0 * jnp.where(rows == 0, far, pltpu.roll(far, 1, 0))
+    )
+    passing = jnp.where(rows < 7, local, 0.0)
 
     def step(given):
-        return own(given[0]), behind(given[1])
-
-    def value(given, shift):
+        ahead, up = given
+        now = load - ahead - up + pltpu.roll(ahead, 1, 0) + pltpu.roll(up, 1, 1)
+        ahead = ahead + 0.26 * (now - pltpu.roll(now, 7, 0))
+        ahead = jnp.minimum(jnp.maximum(ahead, 0.0), jnp.maximum(passing - up, 0.0))
+        up = up + 0.26 * (now - pltpu.roll(now, 127, 1))
+        up = jnp.minimum(jnp.maximum(up, 0.0), jnp.maximum(local - ahead, 0.0))
+        return ahead, up
+
+    def value(given, shift, base):
         column = lax.rem(b + shift + nb, nb)
-        picked = (rows == reach - 1) & (lanes == column + 32)
+        picked = (rows == reach - 1) & (lanes == column + base)
         return jnp.sum(jnp.where(picked, given, 0.0)).astype(i32)
 
     start = jnp.zeros((8, 128), f32)
-    return ((start, start), (start, start)), step, value
+    return (start, start), step, value
 
 
 def pair_kernel(
@@ -418,6 +424,7 @@
     RT,
     extra,
     pieces,
+    natural,
     acc,
     sem,
     *rings,
@@ -439,12 +446,13 @@
     keep = pltpu.make_async_copy(cols_ref.at[0:768], moved_ref, sem.at[3])
     keep.start()
     given, step, value = shares(wide)
-    given = build_tables(cols_ref, U, V, L, RT, extra, pieces, given, step)
-    ahead_out = value(given[0][0], 0)
-    up_out = value(given[0][1], 0)
-    ahead_in = value(given[1][0], 0)
-    ahead_down = value(given[0][0], -1)
-    up_in = value(given[0][1], -1)
+    first = lists_ref[0]
+    given = build_tables(cols_ref, U, V, L, RT, extra, pieces, natural, given, step, first < 0, first & 63)
+    ahead_out = value(given[0], 0, 32)
+    up_out = value(given[1], 0, 32)
+    ahead_in = value(given[0], 0, 96)
+    ahead_down = value(given[0], -1, 32)
+    up_in = value(given[1], -1, 32)
 
     def begin(at, name):
         return lists_ref[at * 1024 + 6 * 128 + name]
@@ -493,7 +501,7 @@
 
     def distances(k, at):
         u, v = entry(k)
-        AB[at][...] = jnp.dot(U[u], V[v], preferred_element_type=f32)
+        AB[at][...] = jnp.dot(U[u, :, 0:32], V[v], preferred_element_type=f32)
 
     def weights(k, at):
         u, v = entry(k)
@@ -757,8 +765,8 @@
             pltpu.SemaphoreType.DMA,
             pltpu.SemaphoreType.DMA((4,)),
             pltpu.VMEM((8, 128), f32),
-            pltpu.SemaphoreType.DMA((6,)),
-            pltpu.SemaphoreType.DMA((6,)),
+            pltpu.SemaphoreType.DMA((3,)),
+            pltpu.SemaphoreType.DMA((3,)),
             pltpu.SemaphoreType.DMA((2 * reach,)),
             pltpu.SemaphoreType.DMA((2 * reach,)),
         ],
@@ -781,12 +789,13 @@
             pltpu.SMEM((4096,), i32),
             pltpu.VMEM((32 * blocks, 128), f32),
             pltpu.VMEM((16, 128), f32),
-            pltpu.VMEM((3 * blocks, 128, 32), bf16),
+            pltpu.VMEM((3 * blocks, 128, 128), bf16),
             pltpu.VMEM((4 * blocks, 32, 256), bf16),
             pltpu.VMEM((4 * blocks, 16, 128), bf16),
             pltpu.VMEM((3 * blocks // 8, 128, 128), f32),
             pltpu.VMEM((32 * blocks, 128), f32),
             pltpu.VMEM((32 * blocks, 128), f32),
+            pltpu.VMEM((3, 256, 128), bf16),
             pltpu.VMEM((32 * blocks + 8, 128), f32),
             pltpu.SemaphoreType.DMA((4,)),
         ]

time: 92.8 us -> 83.6 us (0.901)
  Pallas kernels: 92 us -> 82.4 us
    pallas_call x1, Pallas kernels: 45.2 us -> 40.7 us  [shards(): pl.pallas_call(pair_kernel, out_shape=(jax.ShapeDtypeStruct((8 * blocks,...]
    pallas_call x1, Pallas kernels: 27.9 us -> 24.4 us  [shards(): pl.pallas_call(halo_kernel, out_shape=(jax.ShapeDtypeStruct((4, blocks, 8...]
    pallas_call x1, Pallas kernels: 17 us -> 15.4 us  [shards(): pl.pallas_call(finish_kernel, out_shape=(jax.ShapeDtypeStruct((14 * block...]
where the time goes in v6:
time: 83.6 us; the launch traced here: 83.1 us
  Pallas kernels  82.4 us (99%)
    pallas_call x1, Pallas kernels, shards(): pl.pallas_call(pair_kernel, out_shape=(jax.ShapeDtypeStruct((8 * blocks,...  40.7 us
    pallas_call x1, Pallas kernels, shards(): pl.pallas_call(halo_kernel, out_shape=(jax.ShapeDtypeStruct((4, blocks, 8...  24.4 us
    pallas_call x1, Pallas kernels, shards(): pl.pallas_call(finish_kernel, out_shape=(jax.ShapeDtypeStruct((14 * block...  15.4 us
    pallas_call x1, Pallas kernels, shards(): pl.pallas_call(rates_kernel, out_shape=(jax.ShapeDtypeStruct((4 * blocks,...  1.9 us

profile of v6, /device:TPU:3, one launch (start us, length us, event | category | flops | bytes accessed | tf_op | source)
XLA Modules:
  0.0 83.1 jit_solution(17624458875280712615)
XLA Ops:
  0.6 24.4 %halo.1 = (f32[4,96,8,128]{3,2,1,0:T(8,128)}, s32[4,8,128]{2,1,0:T(8,128)}, f32[16,128]{1,0:T(8,128)}) custom-call(s32[24]{0:T(128)} %bitcast.20, s32[2]{0:T(128)} %bitcast.21, s32[2,576]{1,0:T(2,128)} %bitcast.18, f32[96,8,128]{2,1,0:T(8,128)} %bitcast.14), custom_call_target="tpu_custom_call" | custom-call | tf_op jit(solution)/shard_map/halo/pallas_call | solution.py:740
  25.0 40.7 %contact.1 = (f32[768,128]{1,0:T(8,128)}, f32[384,128]{1,0:T(8,128)}, f32[1152,128]{1,0:T(8,128)}) custom-call(s32[4096]{0:T(1024)} %bitcast.17, f32[3072,128]{1,0:T(8,128)} %bitcast.12, f32[16,128]{1,0:T(8,128)} %get-tuple-element.15.wide_hbm), custom_call_target="tpu_custom_call" | custom-call | tf_op jit(solution)/shard_map/contact/pallas_call | solution.py:779
  65.8 15.4 %finish.1 = (f32[1344,128]{1,0:T(8,128)}, f32[2,256]{1,0:T(2,128)}) custom-call(f32[768,128]{1,0:T(8,128)} %get-tuple-element.16.moved_hbm, f32[1152,128]{1,0:T(8,128)} %get-tuple-element.18.sides_ref, s32[96,128]{1,0:T(8,128)} %bitcast.15, s32[96,128]{1,0:T(8,128)} %bitcast.16, f32[1,256]{1,0:T(1,128)} %bitcast.19), custom_call_target="tpu_custom_call" | custom-call | tf_op jit(solution)/shard_map/finish/pallas_call | solution.py:808
  81.2 1.9 %rates.1 = (f32[384,128]{1,0:T(8,128)}, f32[2,256]{1,0:T(2,128)}) custom-call(f32[384,128]{1,0:T(8,128)} %get-tuple-element.17.own_hbm, f32[1344,128]{1,0:T(8,128)} %get-tuple-element.19.mix_hbm, f32[2,256]{1,0:T(2,128)} %get-tuple-element.20.fluid_hbm), custom_call_target="tpu_custom_call" | custom-call | tf_op jit(solution)/shard_map/rates/pallas_call | solution.py:832

commit v7 on v6

--- a/solution.py
+++ b/solution.py
@@ -28,6 +28,7 @@
 lag_b = 2
 ring = lag_a + lag_b
 reach = 4
+lateness = (37.0, 28.0, 22.0, 125.0, 20.0)
 vmem_grant = 56 * 2**20
 MESH = pl.DeviceIdType.MESH
 
@@ -388,6 +389,10 @@
         + pltpu.roll(far, 1, 1)
         + 3.0 * jnp.where(rows == 0, far, pltpu.roll(far, 1, 0))
     )
+    column = lax.axis_index("gx") + rows - (reach - 1) - jnp.where(lanes < 64, 0, 1)
+    phase = (column + 32) & 15
+    for at, late in enumerate(lateness):
+        load = load + jnp.where(phase == at, late, 0.0)
     passing = jnp.where(rows < 7, local, 0.0)
 
     def step(given):

time: 83.6 us -> 81 us (0.969)
  the two profiles are of different devices: /device:TPU:3 before, /device:TPU:15 now
where the time goes in v7:
time: 81 us; the launch traced here: 80.9 us
  Pallas kernels  80.2 us (99%)
    pallas_call x1, Pallas kernels, shards(): pl.pallas_call(pair_kernel, out_shape=(jax.ShapeDtypeStruct((8 * blocks,...  43 us
    pallas_call x1, Pallas kernels, shards(): pl.pallas_call(halo_kernel, out_shape=(jax.ShapeDtypeStruct((4, blocks, 8...  22.5 us
    pallas_call x1, Pallas kernels, shards(): pl.pallas_call(finish_kernel, out_shape=(jax.ShapeDtypeStruct((14 * block...  12.7 us
    pallas_call x1, Pallas kernels, shards(): pl.pallas_call(rates_kernel, out_shape=(jax.ShapeDtypeStruct((4 * blocks,...  1.9 us

profile of v7, /device:TPU:15, one launch (start us, length us, event | category | flops | bytes accessed | tf_op | source)
XLA Modules:
  0.0 80.9 jit_solution(16474853480130877968)
XLA Ops:
  0.6 22.5 %halo.1 = (f32[4,96,8,128]{3,2,1,0:T(8,128)}, s32[4,8,128]{2,1,0:T(8,128)}, f32[16,128]{1,0:T(8,128)}) custom-call(s32[24]{0:T(128)} %bitcast.20, s32[2]{0:T(128)} %bitcast.21, s32[2,576]{1,0:T(2,128)} %bitcast.18, f32[96,8,128]{2,1,0:T(8,128)} %bitcast.14), custom_call_target="tpu_custom_call" | custom-call | tf_op jit(solution)/shard_map/halo/pallas_call | solution.py:745
  23.2 43.0 %contact.1 = (f32[768,128]{1,0:T(8,128)}, f32[384,128]{1,0:T(8,128)}, f32[1152,128]{1,0:T(8,128)}) custom-call(s32[4096]{0:T(1024)} %bitcast.17, f32[3072,128]{1,0:T(8,128)} %bitcast.12, f32[16,128]{1,0:T(8,128)} %get-tuple-element.15.wide_hbm), custom_call_target="tpu_custom_call" | custom-call | tf_op jit(solution)/shard_map/contact/pallas_call | solution.py:784
  66.2 12.7 %finish.1 = (f32[1344,128]{1,0:T(8,128)}, f32[2,256]{1,0:T(2,128)}) custom-call(f32[768,128]{1,0:T(8,128)} %get-tuple-element.16.moved_hbm, f32[1152,128]{1,0:T(8,128)} %get-tuple-element.18.sides_ref, s32[96,128]{1,0:T(8,128)} %bitcast.15, s32[96,128]{1,0:T(8,128)} %bitcast.16, f32[1,256]{1,0:T(1,128)} %bitcast.19), custom_call_target="tpu_custom_call" | custom-call | tf_op jit(solution)/shard_map/finish/pallas_call | solution.py:813
  79.0 1.9 %rates.1 = (f32[384,128]{1,0:T(8,128)}, f32[2,256]{1,0:T(2,128)}) custom-call(f32[384,128]{1,0:T(8,128)} %get-tuple-element.17.own_hbm, f32[1344,128]{1,0:T(8,128)} %get-tuple-element.19.mix_hbm, f32[2,256]{1,0:T(2,128)} %get-tuple-element.20.fluid_hbm), custom_call_target="tpu_custom_call" | custom-call | tf_op jit(solution)/shard_map/rates/pallas_call | solution.py:837

commit v8 on v7

--- a/solution.py
+++ b/solution.py
@@ -28,7 +28,9 @@
 lag_b = 2
 ring = lag_a + lag_b
 reach = 4
-lateness = (37.0, 28.0, 22.0, 125.0, 20.0)
+lateness = (50.0, 28.0, 22.0, 125.0, 20.0, 0.0, 0.0, 0.0, 0.0, 0.0, 0.0, 0.0, 30.0, 0.0, 0.0, 25.0)
+early = 80
+early_turn = 7
 vmem_grant = 56 * 2**20
 MESH = pl.DeviceIdType.MESH
 
@@ -116,6 +118,41 @@
     return packed.astype(i32), begin.astype(i32)
 
 
+def own_pairs(list_smem, refs, rings, early_ref):
+    cols_ref, U, V, L, RT = refs[0:5]
+    AB = rings[0:ring]
+    M = rings[ring : 2 * ring]
+    build_own_tables(refs)
+
+    def entry(k):
+        k = jnp.minimum(k, early - 1)
+        code = list_smem[lax.shift_right_logical(k, 7), k & 127]
+        u = jnp.minimum(code & 511, 95)
+        v = jnp.minimum(lax.shift_right_logical(code, 9), 95)
+        return u, v
+
+    def same(block):
+        return block
+
+    distances, weights, both = pair_machine(entry, same, same, cols_ref, U, V, L, RT, AB, M)
+    for q in range(ring):
+        distances(q, q)
+    for q in range(lag_b):
+        weights(q, q)
+
+    def turn(t, carry):
+        for q in range(group):
+            k = t * group + q
+            _, _, to_first, to_second = both(k, q % ring)
+            early_ref[tile(2 * k), :] = to_first
+            early_ref[tile(2 * k + 1), :] = to_second
+            weights(k + lag_b, (q + lag_b) % ring)
+            distances(k + ring, q % ring)
+        return carry
+
+    lax.fori_loop(0, early // group, turn, 0)
+
+
 def halo_kernel(
     leaving_hbm,
     counts_hbm,
@@ -124,6 +161,7 @@
     cols_ref,
     lists_ref,
     wide_ref,
+    early_ref,
     leaving_ref,
     counts_ref,
     pairs_ref,
@@ -146,6 +184,15 @@
     near_recv,
     wide_send,
     wide_recv,
+    list_smem,
+    U,
+    V,
+    L,
+    RT,
+    extra,
+    pieces,
+    natural,
+    *rings,
 ):
     blocks = state_hbm.shape[0]
     count = leaving_hbm.shape[0]
@@ -172,7 +219,7 @@
     wide_ref[...] = jnp.zeros_like(wide_ref)
     for copy in inputs:
         copy.wait()
-    local = counts_ref[0].astype(f32)
+    local = jnp.maximum(counts_ref[0] - early, 0).astype(f32)
     far = (counts_ref[1] - counts_ref[0]).astype(f32) * 0.125
     lane = iota((1, 128), 1)
     near[0:1, :] = jnp.where(lane < 64, far, local)
@@ -249,10 +296,13 @@
         copy.start()
         copies.append(copy)
     to_smem.wait()
+    own_list = pltpu.make_async_copy(lists_ref.at[0], list_smem, local_sem)
+    own_list.start()
+    own_list.wait()
     depart.wait()
 
     def place_block(j, carry):
-        moved[j] = cat[slot_smem[0, j]]
+        moved[tile(j), :] = cat[slot_smem[0, j]]
         return carry
 
     lax.fori_loop(0, blocks, place_block, 0)
@@ -270,6 +320,9 @@
         copy.start()
         copies.append(copy)
     keep.wait()
+    own_pairs(
+        list_smem, (moved, U, V, L, RT, extra, pieces, natural), rings, early_ref
+    )
     for copy in copies:
         copy.wait()
 
@@ -282,7 +335,7 @@
     return pl.ds(pl.multiple_of(i * 8, 8), 8)
 
 
-def build_tables(cols_ref, U, V, L, RT, extra, pieces, natural, start, step, never, spare):
+def table_steps(cols_ref, U, V, L, RT, extra, pieces, natural, never):
     rows = iota((8, 128), 0)
     eye = (iota((128, 128), 0) == iota((128, 128), 1)).astype(bf16)
     eyes = jnp.concatenate([eye, eye, eye], axis=1)
@@ -348,6 +401,13 @@
         three = jnp.concatenate(split3(radius), axis=1).astype(bf16)
         RT[lax.shift_right_logical(u_base, 3), :, 0:8] = dot_tt(eyes, three)
 
+    return dense, eight, turn, column
+
+
+def build_tables(refs, first, start, step):
+    dense, eight, turn, column = table_steps(*refs, first < 0)
+    cols_ref, U = refs[0:2]
+
     def turns(t):
         turn(0, 8 * t)
         turn(1, 96 + 8 * t)
@@ -363,14 +423,27 @@
         eight(8 * t, 0, 0)
         eight(96 + 8 * t, 192, 1)
         eight(288 + 8 * t, -96, 2)
-        held = U[spare, 0:16, :].astype(f32)[0:8]
+        held = U[first & 63, 0:16, :].astype(f32)[0:8]
         eight(192 + 8 * t, -96, None, held)
-        return step(carry)
+        return step(t, carry)
 
     count = cols_ref.shape[0] // 256
     carry = lax.fori_loop(0, count, body, start)
     turns(count - 1)
     return carry
+
+
+def build_own_tables(refs):
+    dense, eight, turn, column = table_steps(*refs, None)
+
+    def body(t, carry):
+        dense(8 * t)
+        eight(8 * t, 0, 0)
+        turn(0, 8 * t)
+        column(8 * t, 8 * t)
+        return carry
+
+    lax.fori_loop(0, refs[0].shape[0] // 64, body, 0)
 
 
 def shares(wide):
@@ -413,97 +486,7 @@
     return (start, start), step, value
 
 
-def pair_kernel(
-    lists_hbm,
-    cols_hbm,
-    wide_hbm,
-    moved_ref,
-    own_ref,
-    sides_ref,
-    lists_ref,
-    cols_ref,
-    wide,
-    U,
-    V,
-    L,
-    RT,
-    extra,
-    pieces,
-    natural,
-    acc,
-    sem,
-    *rings,
-):
-    AB = rings[0:ring]
-    M = rings[ring : 2 * ring]
-    copies = [
-        pltpu.make_async_copy(source, target, sem.at[at])
-        for at, (source, target) in enumerate(
-            ((cols_hbm, cols_ref), (lists_hbm, lists_ref), (wide_hbm, wide))
-        )
-    ]
-    for copy in copies:
-        copy.start()
-    trash = acc.shape[0] // 8 - 1
-    acc[...] = jnp.zeros_like(acc)
-    for copy in copies:
-        copy.wait()
-    keep = pltpu.make_async_copy(cols_ref.at[0:768], moved_ref, sem.at[3])
-    keep.start()
-    given, step, value = shares(wide)
-    first = lists_ref[0]
-    given = build_tables(cols_ref, U, V, L, RT, extra, pieces, natural, given, step, first < 0, first & 63)
-    ahead_out = value(given[0], 0, 32)
-    up_out = value(given[1], 0, 32)
-    ahead_in = value(given[0], 0, 96)
-    ahead_down = value(given[0], -1, 32)
-    up_in = value(given[1], -1, 32)
-
-    def begin(at, name):
-        return lists_ref[at * 1024 + 6 * 128 + name]
-
-    def cut(at, first, second):
-        first = jnp.minimum(first, begin(at, 1))
-        return first, jnp.minimum(first + second, begin(at, 1))
-
-    _, kept = cut(0, ahead_out, up_out)
-    ahead_in = jnp.minimum(ahead_in, begin(3, 1))
-    up_low, up_high = cut(2, ahead_down, up_in)
-    ends = []
-    shifts = []
-    so_far = 0
-    for at, low, high in (
-        (0, kept, begin(0, 1)),
-        (0, begin(0, 1), begin(0, 2)),
-        (1, begin(1, 2), begin(1, 3)),
-        (2, begin(2, 3), begin(2, 4)),
-        (3, begin(3, 4), begin(3, 5)),
-        (3, 0, ahead_in),
-        (2, up_low, up_high),
-    ):
-        shifts.append(at * 1024 + low - so_far)
-        so_far = so_far + (high - low)
-        ends.append(so_far)
-    n = so_far
-    last = jnp.maximum(n - 1, 0)
-
-    def entry(k):
-        k = jnp.minimum(k, last)
-        shift = shifts[6]
-        for at in range(5, -1, -1):
-            shift = jnp.where(k < ends[at], shifts[at], shift)
-        code = lists_ref[k + shift]
-        code = code + jnp.where(
-            k < ends[4], 0, jnp.where(k < ends[5], 96 + 512 * 288, 192 + 512 * 192)
-        )
-        return code & 511, lax.shift_right_logical(code, 9)
-
-    def spot_u(u):
-        return jnp.where(u < 192, u, u + 96)
-
-    def spot(v):
-        return jnp.where(v < 96, v, jnp.where(v < 288, v + 96, v - 192))
-
+def pair_machine(entry, spot, spot_u, cols_ref, U, V, L, RT, AB, M):
     def distances(k, at):
         u, v = entry(k)
         AB[at][...] = jnp.dot(U[u, :, 0:32], V[v], preferred_element_type=f32)
@@ -540,7 +523,7 @@
         both = out[0:8] + out[8:16]
         return jnp.where(rows < 4, both[:, 0:128], both[:, 128:256])
 
-    def sums(k, at):
+    def both(k, at):
         u, v = entry(k)
         w = spot(v)
         o = spot_u(u)
@@ -556,6 +539,129 @@
         )
         to_second = folded(jnp.dot(first, m[...], preferred_element_type=f32))
         to_first = folded(dot_tt(second, crossed))
+        return o, w, to_first, to_second
+
+    return distances, weights, both
+
+
+def pair_kernel(
+    lists_hbm,
+    cols_hbm,
+    wide_hbm,
+    early_hbm,
+    moved_ref,
+    own_ref,
+    sides_ref,
+    lists_ref,
+    cols_ref,
+    wide,
+    U,
+    V,
+    L,
+    RT,
+    extra,
+    pieces,
+    natural,
+    acc,
+    before,
+    sem,
+    *rings,
+):
+    AB = rings[0:ring]
+    M = rings[ring : 2 * ring]
+    copies = [
+        pltpu.make_async_copy(source, target, sem.at[at])
+        for at, (source, target) in enumerate(
+            (
+                (cols_hbm, cols_ref),
+                (lists_hbm, lists_ref),
+                (wide_hbm, wide),
+                (early_hbm, before.at[0 : 16 * early]),
+            )
+        )
+    ]
+    for copy in copies:
+        copy.start()
+    trash = acc.shape[0] // 8 - 1
+    acc[...] = jnp.zeros_like(acc)
+    for copy in copies:
+        copy.wait()
+    keep = pltpu.make_async_copy(cols_ref.at[0:768], moved_ref, sem.at[4])
+    keep.start()
+    given, step, value = shares(wide)
+    first = lists_ref[0]
+    done = jnp.minimum(lists_ref[6 * 128 + 1], early)
+
+    def turn_in(t, carry):
+        for q in range(early_turn):
+            k = t * early_turn + q
+            live = k < done
+            code = lists_ref[k]
+            o = jnp.where(live, code & 511, trash)
+            w = jnp.where(live, lax.shift_right_logical(code, 9), trash)
+            acc[tile(o), :] += before[tile(2 * k), :]
+            acc[tile(w), :] += before[tile(2 * k + 1), :]
+        return step(carry)
+
+    refs = (cols_ref, U, V, L, RT, extra, pieces, natural)
+    given = build_tables(refs, first, given, turn_in)
+    ahead_out = value(given[0], 0, 32)
+    up_out = value(given[1], 0, 32)
+    ahead_in = value(given[0], 0, 96)
+    ahead_down = value(given[0], -1, 32)
+    up_in = value(given[1], -1, 32)
+
+    def begin(at, name):
+        return lists_ref[at * 1024 + 6 * 128 + name]
+
+    def cut(at, first, second):
+        end = begin(at, 1)
+        low = jnp.minimum(end, early)
+        first = jnp.minimum(low + first, end)
+        return low, first, jnp.minimum(first + second, end)
+
+    _, _, kept = cut(0, ahead_out, up_out)
+    ahead_low, ahead_high, _ = cut(3, ahead_in, 0)
+    _, up_low, up_high = cut(2, ahead_down, up_in)
+    ends = []
+    shifts = []
+    so_far = 0
+    for at, low, high in (
+        (0, kept, begin(0, 1)),
+        (0, begin(0, 1), begin(0, 2)),
+        (1, begin(1, 2), begin(1, 3)),
+        (2, begin(2, 3), begin(2, 4)),
+        (3, begin(3, 4), begin(3, 5)),
+        (3, ahead_low, ahead_high),
+        (2, up_low, up_high),
+    ):
+        shifts.append(at * 1024 + low - so_far)
+        so_far = so_far + (high - low)
+        ends.append(so_far)
+    n = so_far
+    last = jnp.maximum(n - 1, 0)
+
+    def entry(k):
+        k = jnp.minimum(k, last)
+        shift = shifts[6]
+        for at in range(5, -1, -1):
+            shift = jnp.where(k < ends[at], shifts[at], shift)
+        code = lists_ref[k + shift]
+        code = code + jnp.where(
+            k < ends[4], 0, jnp.where(k < ends[5], 96 + 512 * 288, 192 + 512 * 192)
+        )
+        return code & 511, lax.shift_right_logical(code, 9)
+
+    def spot_u(u):
+        return jnp.where(u < 192, u, u + 96)
+
+    def spot(v):
+        return jnp.where(v < 96, v, jnp.where(v < 288, v + 96, v - 192))
+
+    distances, weights, both = pair_machine(entry, spot, spot_u, cols_ref, U, V, L, RT, AB, M)
+
+    def sums(k, at):
+        o, w, to_first, to_second = both(k, at)
         live = k < n
         o = jnp.where(live, o, trash)
         w = jnp.where(live, w, trash)
@@ -742,22 +848,23 @@
     blocks = mine.shape[0]
     count = leaving.shape[2]
     lanes = -(-pairs.shape[3] // 128) * 128
-    cols, lists, wide = pl.pallas_call(
+    cols, lists, wide, ahead_of = pl.pallas_call(
         halo_kernel,
         out_shape=(
-            jax.ShapeDtypeStruct((4, blocks, 8, 128), f32),
+            jax.ShapeDtypeStruct((4, 8 * blocks, 128), f32),
             jax.ShapeDtypeStruct((4, 8, 128), i32),
             jax.ShapeDtypeStruct((16, 128), f32),
+            jax.ShapeDtypeStruct((16 * early, 128), f32),
         ),
         in_specs=[anywhere()] * 4,
-        out_specs=(anywhere(), vmem(), vmem()),
+        out_specs=(anywhere(), vmem(), vmem(), vmem()),
         scratch_shapes=[
             pltpu.SMEM(leaving.shape[2:], i32),
             pltpu.SMEM(counts.shape[2:], i32),
             pltpu.VMEM(pairs.shape[2:], i32),
             pltpu.VMEM((count + blocks, 8, 128), f32),
             pltpu.VMEM((count, 8, 128), f32),
-            pltpu.VMEM((blocks, 8, 128), f32),
+            pltpu.VMEM((8 * blocks, 128), f32),
             pltpu.VMEM((8, lanes), i32),
             pltpu.VMEM((8, 128), i32),
             pltpu.SMEM((8, 128), i32),
@@ -774,7 +881,17 @@
             pltpu.SemaphoreType.DMA((3,)),
             pltpu.SemaphoreType.DMA((2 * reach,)),
             pltpu.SemaphoreType.DMA((2 * reach,)),
-        ],
+            pltpu.SMEM((8, 128), i32),
+            pltpu.VMEM((blocks, 128, 128), bf16),
+            pltpu.VMEM((blocks, 32, 256), bf16),
+            pltpu.VMEM((blocks, 16, 128), bf16),
+            pltpu.VMEM((blocks // 8, 128, 128), f32),
+            pltpu.VMEM((8 * blocks, 128), f32),
+            pltpu.VMEM((8 * blocks, 128), f32),
+            pltpu.VMEM((1, 256, 128), bf16),
+        ]
+        + [pltpu.VMEM((128, 256), f32)] * ring
+        + [pltpu.VMEM((256, 256), bf16)] * ring,
         compiler_params=pltpu.CompilerParams(
             collective_id=0, has_side_effects=True, vmem_limit_bytes=vmem_grant
         ),
@@ -788,7 +905,7 @@
             jax.ShapeDtypeStruct((4 * blocks, 128), f32),
             jax.ShapeDtypeStruct((12 * blocks, 128), f32),
         ),
-        in_specs=[anywhere()] * 3,
+        in_specs=[anywhere()] * 4,
         out_specs=(anywhere(), vmem(), vmem()),
         scratch_shapes=[
             pltpu.SMEM((4096,), i32),
@@ -802,13 +919,14 @@
             pltpu.VMEM((32 * blocks, 128), f32),
             pltpu.VMEM((3, 256, 128), bf16),
             pltpu.VMEM((32 * blocks + 8, 128), f32),
-            pltpu.SemaphoreType.DMA((4,)),
+            pltpu.VMEM((16 * early_turn * blocks // 8, 128), f32),
+            pltpu.SemaphoreType.DMA((5,)),
         ]
         + [pltpu.VMEM((128, 256), f32)] * ring
         + [pltpu.VMEM((256, 256), bf16)] * ring,
         compiler_params=pltpu.CompilerParams(vmem_limit_bytes=vmem_grant),
         name="contact",
-    )(lists.reshape(4096), cols.reshape(32 * blocks, 128), wide)
+    )(lists.reshape(4096), cols.reshape(32 * blocks, 128), wide, ahead_of)
 
     mix, fluid = pl.pallas_call(
         finish_kernel,

time: 81 us -> 78 us (0.963)
  the two profiles are of different devices: /device:TPU:15 before, /device:TPU:11 now
where the time goes in v8:
time: 78 us; the launch traced here: 77.8 us
  Pallas kernels  77.2 us (99%)
    pallas_call x1, Pallas kernels, shards(): pl.pallas_call(pair_kernel, out_shape=(jax.ShapeDtypeStruct((8 * blocks,...  27.9 us
    pallas_call x1, Pallas kernels, shards(): pl.pallas_call(finish_kernel, out_shape=(jax.ShapeDtypeStruct((14 * block...  24.2 us
    pallas_call x1, Pallas kernels, shards(): pl.pallas_call(halo_kernel, out_shape=(jax.ShapeDtypeStruct((4, 8 * block...  23.2 us
    pallas_call x1, Pallas kernels, shards(): pl.pallas_call(rates_kernel, out_shape=(jax.ShapeDtypeStruct((4 * blocks,...  1.9 us

profile of v8, /device:TPU:11, one launch (start us, length us, event | category | flops | bytes accessed | tf_op | source)
XLA Modules:
  0.0 77.8 jit_solution(10189111554470864743)
XLA Ops:
  0.6 23.2 %halo.1 = (f32[4,768,128]{2,1,0:T(8,128)}, s32[4,8,128]{2,1,0:T(8,128)}, f32[16,128]{1,0:T(8,128)}, f32[1280,128]{1,0:T(8,128)}) custom-call(s32[24]{0:T(128)} %bitcast.20, s32[2]{0:T(128)} %bitcast.21, s32[2,576]{1,0:T(2,128)} %bitcast.18, f32[96,8,128]{2,1,0:T(8,128)} %bitcast.14), custom_call_target="tpu_custom_call" | custom-call | tf_op jit(solution)/shard_map/halo/pallas_call | solution.py:851
  23.8 27.9 %contact.1 = (f32[768,128]{1,0:T(8,128)}, f32[384,128]{1,0:T(8,128)}, f32[1152,128]{1,0:T(8,128)}) custom-call(s32[4096]{0:T(1024)} %bitcast.17, f32[3072,128]{1,0:T(8,128)} %bitcast.12, f32[16,128]{1,0:T(8,128)} %get-tuple-element.16.wide_hbm, f32[1280,128]{1,0:T(8,128)} %get-tuple-element.17.early_hbm), custom_call_target="tpu_custom_call" | custom-call | tf_op jit(solution)/shard_map/contact/pallas_call | solution.py:901
  51.7 24.2 %finish.1 = (f32[1344,128]{1,0:T(8,128)}, f32[2,256]{1,0:T(2,128)}) custom-call(f32[768,128]{1,0:T(8,128)} %get-tuple-element.18.moved_hbm, f32[1152,128]{1,0:T(8,128)} %get-tuple-element.20.sides_ref, s32[96,128]{1,0:T(8,128)} %bitcast.15, s32[96,128]{1,0:T(8,128)} %bitcast.16, f32[1,256]{1,0:T(1,128)} %bitcast.19), custom_call_target="tpu_custom_call" | custom-call | tf_op jit(solution)/shard_map/finish/pallas_call | solution.py:931
  75.9 1.9 %rates.1 = (f32[384,128]{1,0:T(8,128)}, f32[2,256]{1,0:T(2,128)}) custom-call(f32[384,128]{1,0:T(8,128)} %get-tuple-element.19.own_hbm, f32[1344,128]{1,0:T(8,128)} %get-tuple-element.21.mix_hbm, f32[2,256]{1,0:T(2,128)} %get-tuple-element.22.fluid_hbm), custom_call_target="tpu_custom_call" | custom-call | tf_op jit(solution)/shard_map/rates/pallas_call | solution.py:955

commit v9 on v8

--- a/solution.py
+++ b/solution.py
@@ -31,6 +31,7 @@
 lateness = (50.0, 28.0, 22.0, 125.0, 20.0, 0.0, 0.0, 0.0, 0.0, 0.0, 0.0, 0.0, 30.0, 0.0, 0.0, 25.0)
 early = 80
 early_turn = 7
+raw_first = 8
 vmem_grant = 56 * 2**20
 MESH = pl.DeviceIdType.MESH
 
@@ -72,7 +73,10 @@
     barrier = pltpu.get_barrier_semaphore()
     for device in everyone:
         pl.semaphore_signal(barrier, inc=1, device_id=device, device_id_type=MESH)
-    pl.semaphore_wait(barrier, len(everyone))
+
+
+def await_all(everyone):
+    pl.semaphore_wait(pltpu.get_barrier_semaphore(), len(everyone))
 
 
 def sort_pairs(lanes, pad, total):
@@ -122,14 +126,13 @@
     cols_ref, U, V, L, RT = refs[0:5]
     AB = rings[0:ring]
     M = rings[ring : 2 * ring]
-    build_own_tables(refs)
+    last = U.shape[0] - 1
 
     def entry(k):
         k = jnp.minimum(k, early - 1)
         code = list_smem[lax.shift_right_logical(k, 7), k & 127]
-        u = jnp.minimum(code & 511, 95)
-        v = jnp.minimum(lax.shift_right_logical(code, 9), 95)
-        return u, v
+        u = jnp.minimum(code & 511, last)
+        return u, jnp.minimum(lax.shift_right_logical(code, 9), last)
 
     def same(block):
         return block
@@ -184,6 +187,7 @@
     near_recv,
     wide_send,
     wide_recv,
+    list_vec,
     list_smem,
     U,
     V,
@@ -194,10 +198,19 @@
     natural,
     *rings,
 ):
-    blocks = state_hbm.shape[0]
+    blocks = state_hbm.shape[0] // 8
     count = leaving_hbm.shape[0]
     ahead, behind, up, down = neighbours()
-    state_ref = cat.at[count : count + blocks]
+    a = lax.axis_index("gx")
+    na = lax.axis_size("gx")
+    along = {
+        step: {"gx": lax.rem(a + step + na, na)} for step in range(-reach, reach + 1) if step
+    }
+    b = lax.axis_index("gy")
+    nb = lax.axis_size("gy")
+    across = {"gy": lax.rem(b + 2, nb)}
+    everyone = (up, down, across, *along.values())
+    state_ref = cat.at[8 * count : 8 * count + 8 * blocks]
     inputs = [
         pltpu.make_async_copy(source, target, in_sem.at[at])
         for at, (source, target) in enumerate(
@@ -206,17 +219,14 @@
                 (state_hbm, state_ref),
                 (pairs_hbm, pairs_ref),
                 (counts_hbm, counts_ref),
+                (state_hbm, moved),
             )
         )
     ]
     for copy in inputs:
         copy.start()
-    a = lax.axis_index("gx")
-    na = lax.axis_size("gx")
-    along = {
-        step: {"gx": lax.rem(a + step + na, na)} for step in range(-reach, reach + 1) if step
-    }
     wide_ref[...] = jnp.zeros_like(wide_ref)
+    greet(everyone)
     for copy in inputs:
         copy.wait()
     local = jnp.maximum(counts_ref[0] - early, 0).astype(f32)
@@ -224,11 +234,8 @@
     lane = iota((1, 128), 1)
     near[0:1, :] = jnp.where(lane < 64, far, local)
     for m in range(count):
-        dep[m] = state_ref[leaving_ref[m]]
-    b = lax.axis_index("gy")
-    nb = lax.axis_size("gy")
-    across = {"gy": lax.rem(b + 2, nb)}
-    greet((up, down, across, *along.values()))
+        dep[8 * m : 8 * m + 8, :] = moved[pl.ds(leaving_ref[m] * 8, 8), :]
+    await_all(everyone)
     asks = []
     for at, device in ((1, down), (2, up), (3, across)):
         copy = pltpu.make_async_remote_copy(
@@ -243,7 +250,7 @@
         asks.append(copy)
     depart = pltpu.make_async_remote_copy(
         src_ref=dep,
-        dst_ref=cat.at[0:count],
+        dst_ref=cat.at[0 : 8 * count],
         send_sem=dep_send,
         recv_sem=dep_recv,
         device_id=ahead,
@@ -296,13 +303,22 @@
         copy.start()
         copies.append(copy)
     to_smem.wait()
-    own_list = pltpu.make_async_copy(lists_ref.at[0], list_smem, local_sem)
+    codes = lists_ref[0]
+    u = jnp.take_along_axis(slot, jnp.minimum(codes & 511, 95), axis=1)
+    v = jnp.take_along_axis(
+        slot, jnp.minimum(lax.shift_right_logical(codes, 9), 95), axis=1
+    )
+    list_vec[...] = u + 512 * v
+    own_list = pltpu.make_async_copy(list_vec, list_smem, local_sem)
     own_list.start()
     own_list.wait()
+    refs = (cat, U, V, L, RT, extra, pieces, natural)
+    raw = count // 8
+    build_groups(refs, raw, raw + raw_first, 2)
     depart.wait()
 
     def place_block(j, carry):
-        moved[tile(j), :] = cat[slot_smem[0, j]]
+        moved[tile(j), :] = cat[pl.ds(slot_smem[0, j] * 8, 8), :]
         return carry
 
     lax.fori_loop(0, blocks, place_block, 0)
@@ -320,9 +336,9 @@
         copy.start()
         copies.append(copy)
     keep.wait()
-    own_pairs(
-        list_smem, (moved, U, V, L, RT, extra, pieces, natural), rings, early_ref
-    )
+    build_groups(refs, raw + raw_first, raw + blocks // 8, 2)
+    build_groups(refs, 0, raw, 3)
+    own_pairs(list_smem, refs, rings, early_ref)
     for copy in copies:
         copy.wait()
 
@@ -433,17 +449,22 @@
     return carry
 
 
-def build_own_tables(refs):
+def build_groups(refs, low, high, step):
     dense, eight, turn, column = table_steps(*refs, None)
 
     def body(t, carry):
-        dense(8 * t)
-        eight(8 * t, 0, 0)
-        turn(0, 8 * t)
-        column(8 * t, 8 * t)
+        bases = [8 * (t * step + low + q) for q in range(step)]
+        for base in bases:
+            dense(base)
+        for at, base in enumerate(bases):
+            eight(base, 0, at)
+        for at, base in enumerate(bases):
+            turn(at, base)
+        for base in bases:
+            column(base, base)
         return carry
 
-    lax.fori_loop(0, refs[0].shape[0] // 64, body, 0)
+    lax.fori_loop(0, (high - low) // step, body, 0)
 
 
 def shares(wide):
@@ -736,6 +757,7 @@
     for copy in inputs:
         copy.start()
     greet((ahead, behind, up, down))
+    await_all((ahead, behind, up, down))
     copies = []
     span = sides_ref.shape[0] // 3
     blocks = span // 4
@@ -862,8 +884,8 @@
             pltpu.SMEM(leaving.shape[2:], i32),
             pltpu.SMEM(counts.shape[2:], i32),
             pltpu.VMEM(pairs.shape[2:], i32),
-            pltpu.VMEM((count + blocks, 8, 128), f32),
-            pltpu.VMEM((count, 8, 128), f32),
+            pltpu.VMEM((8 * (count + blocks), 128), f32),
+            pltpu.VMEM((8 * count, 128), f32),
             pltpu.VMEM((8 * blocks, 128), f32),
             pltpu.VMEM((8, lanes), i32),
             pltpu.VMEM((8, 128), i32),
@@ -875,20 +897,21 @@
             pltpu.SemaphoreType.DMA((3,)),
             pltpu.SemaphoreType.DMA((3,)),
             pltpu.SemaphoreType.DMA,
-            pltpu.SemaphoreType.DMA((4,)),
+            pltpu.SemaphoreType.DMA((5,)),
             pltpu.VMEM((8, 128), f32),
             pltpu.SemaphoreType.DMA((3,)),
             pltpu.SemaphoreType.DMA((3,)),
             pltpu.SemaphoreType.DMA((2 * reach,)),
             pltpu.SemaphoreType.DMA((2 * reach,)),
+            pltpu.VMEM((8, 128), i32),
             pltpu.SMEM((8, 128), i32),
-            pltpu.VMEM((blocks, 128, 128), bf16),
-            pltpu.VMEM((blocks, 32, 256), bf16),
-            pltpu.VMEM((blocks, 16, 128), bf16),
-            pltpu.VMEM((blocks // 8, 128, 128), f32),
-            pltpu.VMEM((8 * blocks, 128), f32),
-            pltpu.VMEM((8 * blocks, 128), f32),
-            pltpu.VMEM((1, 256, 128), bf16),
+            pltpu.VMEM((count + blocks, 128, 128), bf16),
+            pltpu.VMEM((count + blocks, 32, 256), bf16),
+            pltpu.VMEM((count + blocks, 16, 128), bf16),
+            pltpu.VMEM(((count + blocks) // 8, 128, 128), f32),
+            pltpu.VMEM((8 * (count + blocks), 128), f32),
+            pltpu.VMEM((8 * (count + blocks), 128), f32),
+            pltpu.VMEM((3, 256, 128), bf16),
         ]
         + [pltpu.VMEM((128, 256), f32)] * ring
         + [pltpu.VMEM((256, 256), bf16)] * ring,
@@ -896,7 +919,7 @@
             collective_id=0, has_side_effects=True, vmem_limit_bytes=vmem_grant
         ),
         name="halo",
-    )(leaving[0, 0], counts[0, 0], pairs[0, 0], mine)
+    )(leaving[0, 0], counts[0, 0], pairs[0, 0], mine.reshape(8 * blocks, 128))
 
     moved, own, sides = pl.pallas_call(
         pair_kernel,

time: 78 us -> 77.3 us (level)
  the two profiles are of different devices: /device:TPU:11 before, /device:TPU:3 now
where the time goes in v9:
time: 77.3 us; the launch traced here: 77.1 us
  Pallas kernels  76.4 us (99%)
    pallas_call x1, Pallas kernels, shards(): pl.pallas_call(pair_kernel, out_shape=(jax.ShapeDtypeStruct((8 * blocks,...  30.3 us
    pallas_call x1, Pallas kernels, shards(): pl.pallas_call(halo_kernel, out_shape=(jax.ShapeDtypeStruct((4, 8 * block...  25.9 us
    pallas_call x1, Pallas kernels, shards(): pl.pallas_call(finish_kernel, out_shape=(jax.ShapeDtypeStruct((14 * block...  18.4 us
    pallas_call x1, Pallas kernels, shards(): pl.pallas_call(rates_kernel, out_shape=(jax.ShapeDtypeStruct((4 * blocks,...  1.9 us

profile of v9, /device:TPU:3, one launch (start us, length us, event | category | flops | bytes accessed | tf_op | source)
XLA Modules:
  0.0 77.1 jit_solution(13563163735194475538)
XLA Ops:
  0.6 25.9 %halo.1 = (f32[4,768,128]{2,1,0:T(8,128)}, s32[4,8,128]{2,1,0:T(8,128)}, f32[16,128]{1,0:T(8,128)}, f32[1280,128]{1,0:T(8,128)}) custom-call(s32[24]{0:T(128)} %bitcast.20, s32[2]{0:T(128)} %bitcast.21, s32[2,576]{1,0:T(2,128)} %bitcast.18, f32[768,128]{1,0:T(8,128)} %bitcast.14), custom_call_target="tpu_custom_call" | custom-call | tf_op jit(solution)/shard_map/halo/pallas_call | solution.py:873
  26.5 30.3 %contact.1 = (f32[768,128]{1,0:T(8,128)}, f32[384,128]{1,0:T(8,128)}, f32[1152,128]{1,0:T(8,128)}) custom-call(s32[4096]{0:T(1024)} %bitcast.17, f32[3072,128]{1,0:T(8,128)} %bitcast.12, f32[16,128]{1,0:T(8,128)} %get-tuple-element.16.wide_hbm, f32[1280,128]{1,0:T(8,128)} %get-tuple-element.17.early_hbm), custom_call_target="tpu_custom_call" | custom-call | tf_op jit(solution)/shard_map/contact/pallas_call | solution.py:924
  56.8 18.4 %finish.1 = (f32[1344,128]{1,0:T(8,128)}, f32[2,256]{1,0:T(2,128)}) custom-call(f32[768,128]{1,0:T(8,128)} %get-tuple-element.18.moved_hbm, f32[1152,128]{1,0:T(8,128)} %get-tuple-element.20.sides_ref, s32[96,128]{1,0:T(8,128)} %bitcast.15, s32[96,128]{1,0:T(8,128)} %bitcast.16, f32[1,256]{1,0:T(1,128)} %bitcast.19), custom_call_target="tpu_custom_call" | custom-call | tf_op jit(solution)/shard_map/finish/pallas_call | solution.py:954
  75.2 1.9 %rates.1 = (f32[384,128]{1,0:T(8,128)}, f32[2,256]{1,0:T(2,128)}) custom-call(f32[384,128]{1,0:T(8,128)} %get-tuple-element.19.own_hbm, f32[1344,128]{1,0:T(8,128)} %get-tuple-element.21.mix_hbm, f32[2,256]{1,0:T(2,128)} %get-tuple-element.22.fluid_hbm), custom_call_target="tpu_custom_call" | custom-call | tf_op jit(solution)/shard_map/rates/pallas_call | solution.py:978

commit v10 on v9

--- a/solution.py
+++ b/solution.py
@@ -28,10 +28,9 @@
 lag_b = 2
 ring = lag_a + lag_b
 reach = 4
-lateness = (50.0, 28.0, 22.0, 125.0, 20.0, 0.0, 0.0, 0.0, 0.0, 0.0, 0.0, 0.0, 30.0, 0.0, 0.0, 25.0)
-early = 80
-early_turn = 7
-raw_first = 8
+lateness = (50.0, 28.0, 22.0, 125.0, 20.0, 0.0, 0.0, 0.0, 0.0, 0.0, 0.0, 0.0, 70.0, 0.0, 0.0, 35.0)
+early = 64
+early_turn = 6
 vmem_grant = 56 * 2**20
 MESH = pl.DeviceIdType.MESH
 
@@ -314,7 +313,6 @@
     own_list.wait()
     refs = (cat, U, V, L, RT, extra, pieces, natural)
     raw = count // 8
-    build_groups(refs, raw, raw + raw_first, 2)
     depart.wait()
 
     def place_block(j, carry):
@@ -336,7 +334,7 @@
         copy.start()
         copies.append(copy)
     keep.wait()
-    build_groups(refs, raw + raw_first, raw + blocks // 8, 2)
+    build_groups(refs, raw, raw + blocks // 8, 2)
     build_groups(refs, 0, raw, 3)
     own_pairs(list_smem, refs, rings, early_ref)
     for copy in copies:

time: 77.3 us -> 75.8 us (0.981); the launches traced: 77.1 us -> 74.5 us
  Pallas kernels: 76.4 us -> 73.9 us
    pallas_call x1, Pallas kernels: 18.4 us -> 12.1 us  [shards(): pl.pallas_call(finish_kernel, out_shape=(jax.ShapeDtypeStruct((14 * block...]
    pallas_call x1, Pallas kernels: 30.3 us -> 36.2 us  [shards(): pl.pallas_call(pair_kernel, out_shape=(jax.ShapeDtypeStruct((8 * blocks,...]
    pallas_call x1, Pallas kernels: 25.9 us -> 23.6 us  [shards(): pl.pallas_call(halo_kernel, out_shape=(jax.ShapeDtypeStruct((4, 8 * block...]
where the time goes in v10:
time: 75.8 us; the launch traced here: 74.5 us
  Pallas kernels  73.9 us (97%)
    pallas_call x1, Pallas kernels, shards(): pl.pallas_call(pair_kernel, out_shape=(jax.ShapeDtypeStruct((8 * blocks,...  36.2 us
    pallas_call x1, Pallas kernels, shards(): pl.pallas_call(halo_kernel, out_shape=(jax.ShapeDtypeStruct((4, 8 * block...  23.6 us
    pallas_call x1, Pallas kernels, shards(): pl.pallas_call(finish_kernel, out_shape=(jax.ShapeDtypeStruct((14 * block...  12.1 us
    pallas_call x1, Pallas kernels, shards(): pl.pallas_call(rates_kernel, out_shape=(jax.ShapeDtypeStruct((4 * blocks,...  1.9 us

profile of v10, /device:TPU:3, one launch (start us, length us, event | category | flops | bytes accessed | tf_op | source)
XLA Modules:
  0.0 74.5 jit_solution(4283944686638510261)
XLA Ops:
  0.6 23.6 %halo.1 = (f32[4,768,128]{2,1,0:T(8,128)}, s32[4,8,128]{2,1,0:T(8,128)}, f32[16,128]{1,0:T(8,128)}, f32[1024,128]{1,0:T(8,128)}) custom-call(s32[24]{0:T(128)} %bitcast.20, s32[2]{0:T(128)} %bitcast.21, s32[2,576]{1,0:T(2,128)} %bitcast.18, f32[768,128]{1,0:T(8,128)} %bitcast.14), custom_call_target="tpu_custom_call" | custom-call | tf_op jit(solution)/shard_map/halo/pallas_call | solution.py:871
  24.2 36.2 %contact.1 = (f32[768,128]{1,0:T(8,128)}, f32[384,128]{1,0:T(8,128)}, f32[1152,128]{1,0:T(8,128)}) custom-call(s32[4096]{0:T(1024)} %bitcast.17, f32[3072,128]{1,0:T(8,128)} %bitcast.12, f32[16,128]{1,0:T(8,128)} %get-tuple-element.16.wide_hbm, f32[1024,128]{1,0:T(8,128)} %get-tuple-element.17.early_hbm), custom_call_target="tpu_custom_call" | custom-call | tf_op jit(solution)/shard_map/contact/pallas_call | solution.py:922
  60.5 12.1 %finish.1 = (f32[1344,128]{1,0:T(8,128)}, f32[2,256]{1,0:T(2,128)}) custom-call(f32[768,128]{1,0:T(8,128)} %get-tuple-element.18.moved_hbm, f32[1152,128]{1,0:T(8,128)} %get-tuple-element.20.sides_ref, s32[96,128]{1,0:T(8,128)} %bitcast.15, s32[96,128]{1,0:T(8,128)} %bitcast.16, f32[1,256]{1,0:T(1,128)} %bitcast.19), custom_call_target="tpu_custom_call" | custom-call | tf_op jit(solution)/shard_map/finish/pallas_call | solution.py:952
  72.6 1.9 %rates.1 = (f32[384,128]{1,0:T(8,128)}, f32[2,256]{1,0:T(2,128)}) custom-call(f32[384,128]{1,0:T(8,128)} %get-tuple-element.19.own_hbm, f32[1344,128]{1,0:T(8,128)} %get-tuple-element.21.mix_hbm, f32[2,256]{1,0:T(2,128)} %get-tuple-element.22.fluid_hbm), custom_call_target="tpu_custom_call" | custom-call | tf_op jit(solution)/shard_map/rates/pallas_call | solution.py:976
